TPU v7x, 768 devices: a whole 4x8x12 slice. The times are simulated.
768 devices in a mesh: wide: 48 (over z, y_lo, core), narrow: 16 (over x, y_hi).
Axes of the slice: x: 4, y: 8 (y_hi: 4, y_lo: 2; y = y_hi * 2 + y_lo), z: 12, core: 2. Of those that a mesh axis runs over, the one named last changes fastest.
Arguments:
- queries: bfloat16 [147456, 768], P(('wide', 'narrow')), may hold values from -18 to 18
- passages: bfloat16 [49152, 768], P(('wide', 'narrow')), may hold values from -6 to 6
- positive: int32 [147456], P(('wide', 'narrow')), may hold values from 0 to 1023
- negative_owners: int32 [768, 8], P(('wide', 'narrow')), may hold values from 0 to 47, as said below
Outputs:
- query_grad: float32 [147456, 768], P(('wide', 'narrow'))
- passage_grad: float32 [49152, 768], P(('wide', 'narrow'))
Inputs may be any that keep to these rules, and one draw needn't show every extreme that they name: `negative_owners`: each row names 8 different groups, never the group of its own block; some groups are named far more often than others.
All inputs are finite; a program needn't handle non-finite values.
Results may differ from a plain program's by a relative error of at most 0.038.
Values may be sent and summed in bfloat16 or wider, within the bound.
No kernel may reach another device: no remote copies, remote signals or barrier semaphores. Data moves between devices by JAX's collectives and lax.ppermute only.
A program may use at most 64 MiB of HBM per device.

v0:
```python
import math

import jax
import jax.numpy as jnp
from jax import lax
from jax.sharding import PartitionSpec as P


def local(queries, passages, positive, negative_owners):
    query_count, width = queries.shape
    block_rows = passages.shape[0]
    neg_count = negative_owners.shape[1]
    scaling = 4.0 / math.sqrt(width)
    owners = negative_owners[0]
    pool = lax.all_gather(passages, "narrow", axis=0, tiled=True)
    group_rows = pool.shape[0]
    piece_rows = lax.all_gather(passages, "wide", axis=0, tiled=True)
    block_count = piece_rows.shape[0] // block_rows
    block_ids = jnp.arange(block_count, dtype=jnp.int32)
    matched = (owners[:, None] == block_ids[None, :]).astype(jnp.bfloat16)
    shaped = piece_rows.reshape(block_count, block_rows, width)
    chosen = jnp.einsum("ki,ird->krd", matched, shaped, preferred_element_type=jnp.float32).astype(
        jnp.bfloat16
    )
    key_rows = jnp.concatenate([pool, chosen.reshape(neg_count * block_rows, width)], axis=0)
    logits = jnp.dot(queries, key_rows.T, preferred_element_type=jnp.float32) * scaling
    row_max = jnp.max(logits, axis=-1, keepdims=True)
    row_total = row_max + jnp.log(jnp.sum(jnp.exp(logits - row_max), axis=-1, keepdims=True))
    chances = jnp.exp(logits - row_total)
    columns = jnp.arange(key_rows.shape[0], dtype=jnp.int32)
    target = (positive[:, None] == columns[None, :]).astype(jnp.float32)
    dlogits = chances - target
    query_wide = queries.astype(jnp.float32)
    query_grad = (
        jnp.dot(dlogits, key_rows.astype(jnp.float32), precision=lax.Precision.HIGHEST) * scaling
    )
    dlogits_pool = dlogits[:, :group_rows]
    dlogits_named = dlogits[:, group_rows:]
    named_terms = jnp.dot(dlogits_named.T, query_wide, precision=lax.Precision.HIGHEST) * scaling
    named_terms = named_terms.reshape(neg_count, block_rows, width)
    block_count = block_rows * lax.axis_size("wide") // block_rows
    block_ids = jnp.arange(block_count, dtype=jnp.int32)
    matched = (block_ids[:, None] == owners[None, :]).astype(jnp.float32)
    summed = jnp.einsum("jk,krd->jrd", matched, named_terms, precision=lax.Precision.HIGHEST)
    returned = lax.psum_scatter(
        summed.reshape(block_rows * lax.axis_size("wide"), width),
        "wide",
        scatter_dimension=0,
        tiled=True,
    )
    pool_grad = jnp.dot(dlogits_pool.T, query_wide, precision=lax.Precision.HIGHEST) * scaling
    owned_grad = lax.psum_scatter(pool_grad, "narrow", scatter_dimension=0, tiled=True)
    return (query_grad, owned_grad + returned)


def solution(mesh):
    in_specs = (
        P(("wide", "narrow"), None),
        P(("wide", "narrow"), None),
        P(("wide", "narrow")),
        P(("wide", "narrow"), None),
    )
    out_specs = (P(("wide", "narrow"), None), P(("wide", "narrow"), None))
    return jax.shard_map(local, mesh=mesh, in_specs=in_specs, out_specs=out_specs, check_vma=False)
```

profile of v0, /device:TPU:1, one launch (start us, length us, event | category | flops | bytes accessed | tf_op | source)
XLA Modules:
  0.0 491.2 jit_solution(5524978069341168333)
XLA Ops:
  7.2 0.0 copy-start
  7.2 0.0 all-gather.5.cloned.1.call-start
  7.2 0.7 all-gather.5.cloned.1.call-update
  7.9 0.0 all-gather.3.cloned.1.call-start
  8.0 0.7 all-gather.3.cloned.1.call-update
  8.7 0.0 reduce-scatter.3.cloned.1.call-start
  8.7 110.4 %all-gather.5.cloned.1.call-done = bf16[3072,768]{1,0:T(8,128)(2,1)} async-done(((bf16[64,768]{1,0:T(8,128)(2,1)}), bf16[3072,768]{1,0:T(8,128)(2,1)}) %all-gather.5.cloned.1.call-update) | async-done | bytes 4718608 | tf_op jit(solution)/shard_map/all_gather | solution.py:17
  119.1 5.8 %fusion.5 = bf16[8,64,768]{2,0,1:T(8,128)(2,1)S(1)} fusion(bf16[48,64,768]{2,1,0:T(8,128)(2,1)} %bitcast.19, s32[8]{0:T(128)} %bitcast.22), kind=kOutput, calls=%fused_computation.9 | convolution fusion | flops 38142336 | bytes 5505056 | tf_op jit(solution)/shard_map/ki,ird->krd/dot_general | solution.py:22
  124.8 0.1 copy.9
  125.0 60.3 %all-gather.3.cloned.1.call-done = bf16[1024,768]{1,0:T(8,128)(2,1)} async-done(((bf16[64,768]{1,0:T(8,128)(2,1)}), bf16[1024,768]{1,0:T(8,128)(2,1)}) %all-gather.3.cloned.1.call-update) | async-done | bytes 1572880 | tf_op jit(solution)/shard_map/all_gather | solution.py:15
  185.3 0.0 copy-done
  185.3 0.0 copy-start.2
  185.3 2.4 fusion.19
  187.7 0.3 exponential_reduce_fusion
  188.1 0.0 copy-done.2
  188.1 0.4 bitcast_subtract_fusion
  188.5 3.3 convolution_multiply_fusion.1
  191.8 0.0 reduce-scatter.3.cloned.1.call-update
  191.8 0.0 copy-start.1
  191.8 0.2 reduce-scatter.5.cloned.1.call-start
  192.0 0.9 convolution_multiply_fusion.2
  193.0 0.0 copy-done.1
  193.0 4.0 fusion.2
  197.0 9.1 %copy.11 = f32[48,64,768]{2,1,0:T(8,128)} copy(f32[48,64,768]{2,0,1:T(8,128)S(1)} %fusion.2) | data formatting | bytes 18874368 | tf_op jit(solution)/shard_map/jk,krd->jrd/dot_general | solution.py:44
  206.1 0.0 reduce-scatter.5.cloned.1.call-update
  206.1 3.8 fusion.8
  210.0 81.9 %reduce-scatter.3.cloned.1.call-done = f32[64,768]{1,0:T(8,128)} async-done(((f32[1024,768]{1,0:T(8,128)}), f32[64,768]{1,0:T(8,128)}) %reduce-scatter.3.cloned.1.call-update) | async-done | bytes 196624 | tf_op jit(solution)/shard_map/reduce_scatter | solution.py:52
  291.9 191.1 %reduce-scatter.5.cloned.1.call-done = f32[64,768]{1,0:T(8,128)} async-done(((f32[3072,768]{1,0:T(8,128)}), f32[64,768]{1,0:T(8,128)}) %reduce-scatter.5.cloned.1.call-update) | async-done | bytes 196624 | tf_op jit(solution)/shard_map/reduce_scatter | solution.py:45
  483.0 1.7 add.16
  (1 shorter events, 0.0 us)
Async XLA Ops:
  7.2 178.1 %copy-start = (bf16[192,768]{1,0:T(8,128)(2,1)S(1)}, bf16[192,768]{1,0:T(8,128)(2,1)}, u32[]{:S(2)}) copy-start(bf16[192,768]{1,0:T(8,128)(2,1)} %param.4) | copy-start | bytes 884740
  7.2 111.9 %all-gather.5.cloned.1.call-start = ((), (), s32[]{:S(2)}) async-start(), calls=%async_computation.3 | async-start | bytes 4816896 | tf_op jit(solution)/shard_map/all_gather | solution.py:17
  7.9 177.4 %all-gather.3.cloned.1.call-start = ((), (), s32[]{:S(2)}) async-start(), calls=%async_computation.2 | async-start | bytes 1671168 | tf_op jit(solution)/shard_map/all_gather | solution.py:15
  8.7 283.2 %reduce-scatter.3.cloned.1.call-start = ((), (), s32[]{:S(2)}) async-start(), calls=%async_computation.4 | async-start | bytes 3342336 | tf_op jit(solution)/shard_map/reduce_scatter | solution.py:52
  185.3 2.8 copy-start.2
  191.8 1.2 copy-start.1
  191.8 291.2 %reduce-scatter.5.cloned.1.call-start = ((), (), s32[]{:S(2)}) async-start(), calls=%async_computation.5 | async-start | bytes 9633792 | tf_op jit(solution)/shard_map/reduce_scatter | solution.py:45
Sparse Core Ops, SparseCore 0:
  10.5 108.5 all-gather.4
  122.7 62.5 all-gather.2
  191.9 99.8 reduce-scatter.2
  294.9 188.0 reduce-scatter.4
where the time goes:
time: 494 us; the launch traced here: 491 us
  waiting for transfers between devices  445 us (90%)
  matrix products  20.3 us (4%)
  between operations  13.8 us (3%)
  local copies, waits for them, and re-layouts  9.24 us (2%)
    reduce_scatter x1, waiting for transfers between devices, local(): lax.psum_scatter(summed.reshape(block_rows * lax.axis_size('wide'), width...  191 us
    all_gather x1, waiting for transfers between devices, local(): piece_rows = lax.all_gather(passages, 'wide', axis=0, tiled=True)  110 us
    reduce_scatter x1, waiting for transfers between devices, local(): lax.psum_scatter(pool_grad, 'narrow', scatter_dimension=0, tiled=True)  81.9 us
    all_gather x1, waiting for transfers between devices, local(): pool = lax.all_gather(passages, 'narrow', axis=0, tiled=True)  60.3 us
  transfers between devices with their start and end apart: 4, of which 4 were waited for; matrix products, arithmetic and copies ran while one was open for 5% of the time, Pallas kernels for 0%

commit v1 on v0

v1 whole, which is shorter than its diff:
```python
import functools
import math

import jax
import jax.numpy as jnp
from jax import lax
from jax.experimental import pallas as pl
from jax.experimental.pallas import tpu as pltpu
from jax.sharding import Mesh
from jax.sharding import PartitionSpec as P

AXES = ("zs", "zl", "yl", "c", "x", "yh")
WIDE = ("zs", "zl", "yl", "c")
RUN = ("zl", "yl", "c")
LANES = 128
SUBS = 8
LIFT = 128.0
DROP = 1.0 / 16.0
VMEM = 12 * 1024 * 1024
STEP = 256


def dot_nt(a, b):
    return lax.dot_general(a, b, (((1,), (1,)), ((), ())), preferred_element_type=jnp.float32)


def dot_tn(a, b):
    return lax.dot_general(a, b, (((0,), (0,)), ((), ())), preferred_element_type=jnp.float32)


def dot_nn(a, b):
    return lax.dot_general(a, b, (((1,), (0,)), ((), ())), preferred_element_type=jnp.float32)


def join_pieces(named_ref, keys_ref, row_tiles, col_tiles):
    rows = named_ref.shape[1]
    for r in range(row_tiles):
        for c in range(col_tiles):
            keys_ref[r * rows : (r + 1) * rows, c * LANES : (c + 1) * LANES] = named_ref[r * col_tiles + c]


def pick_kernel(run_ref, owners_ref, held_ref, out_ref):
    members, tiles, count = out_ref.shape[:3]
    stride = held_ref.shape[0] // (owners_ref.shape[0] // count)

    def body(i, carry):
        for k in range(count):
            owner = owners_ref[(run_ref[0] * members + i) * count + k]
            for u in range(tiles):
                out_ref[i, u, k] = held_ref[owner * stride + u]
        return carry

    lax.fori_loop(0, members, body, 0)


def gather_sum_kernel(run_ref, owners_ref, terms_ref, out_ref, *acc_refs):
    members, tiles, count = terms_ref.shape[:3]
    for u in range(tiles):
        acc_refs[u][...] = jnp.zeros_like(acc_refs[u])

    def body(i, carry):
        for k in range(count):
            owner = owners_ref[(run_ref[0] * members + i) * count + k]
            for u in range(tiles):
                acc_refs[u][owner] += terms_ref[i, u, k]
        return carry

    lax.fori_loop(0, members, body, 0)
    for u in range(tiles):
        out_ref[:, u] = acc_refs[u][...] * DROP


def pool_kernel(q_ref, *refs):
    slab_refs, (exp_ref, top_ref, sum_ref) = refs[:-3], refs[-3:]
    width = q_ref.shape[1]
    step = slab_refs[0].shape[0]
    scaling = 4.0 / math.sqrt(width)
    q = q_ref[...]
    top = None
    for slot, slab_ref in enumerate(slab_refs):
        part = dot_nt(q, slab_ref[...]) * scaling
        exp_ref[:, slot * step : (slot + 1) * step] = part
        high = jnp.max(part, axis=-1, keepdims=True)
        top = high if top is None else jnp.maximum(top, high)
    total = jnp.zeros_like(top)
    for slot in range(len(slab_refs)):
        part = jnp.exp(exp_ref[:, slot * step : (slot + 1) * step] - top)
        exp_ref[:, slot * step : (slot + 1) * step] = part
        total += jnp.sum(part, axis=-1, keepdims=True)
    top_ref[...] = top
    sum_ref[...] = total


def split(grad):
    hi = grad.astype(jnp.bfloat16)
    return hi, (grad - hi.astype(jnp.float32)).astype(jnp.bfloat16)


def named_kernel(q_ref, named_ref, top_ref, sum_ref, hi_ref, lo_ref, grad_ref, share_ref, keys_ref, l_ref):
    width = q_ref.shape[1]
    col_tiles = width // LANES
    row_tiles = named_ref.shape[0] // col_tiles
    piece_rows = named_ref.shape[1]
    named_rows = row_tiles * piece_rows
    scaling = 4.0 / math.sqrt(width)
    join_pieces(named_ref, keys_ref, row_tiles, col_tiles)
    q = q_ref[...]
    pool_top = top_ref[...]
    top = pool_top
    for c in range(0, named_rows, STEP):
        part = dot_nt(q, keys_ref[c : c + STEP, :]) * scaling
        l_ref[:, c : c + STEP] = part
        top = jnp.maximum(top, jnp.max(part, axis=-1, keepdims=True))
    pool_scale = jnp.exp(pool_top - top)
    total = sum_ref[...] * pool_scale
    for c in range(0, named_rows, STEP):
        part = jnp.exp(l_ref[:, c : c + STEP] - top)
        l_ref[:, c : c + STEP] = part
        total += jnp.sum(part, axis=-1, keepdims=True)
    share = 1.0 / total
    share_ref[...] = share * pool_scale
    for c in range(0, named_rows, STEP):
        hi, lo = split(l_ref[:, c : c + STEP] * share)
        hi_ref[:, c : c + STEP] = hi
        lo_ref[:, c : c + STEP] = lo
        terms = (dot_tn(hi, q) + dot_tn(lo, q)) * (scaling * LIFT)
        first = c // piece_rows
        for r in range(STEP // piece_rows):
            for k in range(col_tiles):
                grad_ref[(first + r) * col_tiles + k] = terms[
                    r * piece_rows : (r + 1) * piece_rows, k * LANES : (k + 1) * LANES
                ]


def pool_grad_kernel(q_ref, exp_ref, share_ref, pos_ref, hi_ref, lo_ref, *grad_refs):
    queries, width = q_ref.shape
    scaling = 4.0 / math.sqrt(width)
    q = q_ref[...]
    share = share_ref[...]
    across = lax.broadcasted_iota(jnp.int32, (queries, queries), 1)
    down = lax.broadcasted_iota(jnp.int32, (queries, queries), 0)
    pos = jnp.sum(jnp.where(across == down, pos_ref[...].astype(jnp.float32), 0.0), axis=1, keepdims=True)
    pos = pos.astype(jnp.int32)
    step = grad_refs[0].shape[0]
    for slot, grad_ref in enumerate(grad_refs):
        first, last = slot * step, (slot + 1) * step
        columns = lax.broadcasted_iota(jnp.int32, (queries, step), 1) + first
        hi, lo = split(exp_ref[:, first:last] * share - (columns == pos).astype(jnp.float32))
        hi_ref[:, first:last] = hi
        lo_ref[:, first:last] = lo
        grad_ref[...] = (dot_tn(hi, q) + dot_tn(lo, q)) * (scaling * LIFT)


def query_kernel(pool_hi_ref, pool_lo_ref, hi_ref, lo_ref, named_ref, *refs):
    slab_refs, out_ref, keys_ref = refs[:-2], refs[-2], refs[-1]
    step, width = slab_refs[0].shape
    col_tiles = width // LANES
    row_tiles = named_ref.shape[0] // col_tiles
    scaling = 4.0 / math.sqrt(width)
    join_pieces(named_ref, keys_ref, row_tiles, col_tiles)
    total = dot_nn(hi_ref[...], keys_ref[...]) + dot_nn(lo_ref[...], keys_ref[...])
    for slot, slab_ref in enumerate(slab_refs):
        first, last = slot * step, (slot + 1) * step
        total += dot_nn(pool_hi_ref[:, first:last], slab_ref[...])
        total += dot_nn(pool_lo_ref[:, first:last], slab_ref[...])
    out_ref[...] = total * scaling


def call(kernel, outs, scratch, flops, *args, smem=0, after=()):
    vmem = pl.BlockSpec(memory_space=pltpu.VMEM)
    specs = [pl.BlockSpec(memory_space=pltpu.SMEM)] * smem + [vmem] * (len(args) - smem)
    specs += [pl.BlockSpec(memory_space=pltpu.HBM)] * len(after)
    count = len(args)

    def body(*refs):
        kernel(*refs[:count], *refs[count + len(after) :])

    return pl.pallas_call(
        body,
        out_shape=tuple(jax.ShapeDtypeStruct(shape, dtype) for shape, dtype in outs),
        in_specs=specs,
        out_specs=(vmem,) * len(outs),
        scratch_shapes=scratch,
        compiler_params=pltpu.CompilerParams(vmem_limit_bytes=VMEM),
        cost_estimate=pl.CostEstimate(flops=flops, bytes_accessed=4 * 1024 * 1024, transcendentals=0),
    )(*args, *after)


def local(queries, passages, positive, negative_owners):
    query_count, width = queries.shape
    block_rows = passages.shape[0]
    neg_count = negative_owners.shape[1]
    f32, bf16, half = jnp.float32, jnp.bfloat16, jnp.float16
    wide, members, runs = lax.axis_size(WIDE), lax.axis_size(RUN), lax.axis_size("zs")
    near, far = lax.axis_size("yh"), lax.axis_size("x")
    row_tiles, col_tiles = block_rows // SUBS, width // LANES
    tiles = row_tiles * col_tiles // members
    pool_rows = far * near * block_rows
    named_rows = neg_count * block_rows
    swaps = [[(i, i ^ k) for i in range(near)] for k in range(near)]
    here_x, here_y = lax.axis_index("x"), lax.axis_index("yh")
    run = lax.axis_index("zs").astype(jnp.int32)[None]

    pieces = passages.reshape(row_tiles, SUBS, col_tiles, LANES).transpose(0, 2, 1, 3)
    pieces = pieces.reshape(members, tiles * SUBS, LANES)
    names = jnp.zeros((SUBS, LANES), bf16).at[0, :neg_count].set(negative_owners[0].astype(bf16))
    sent = jnp.concatenate([pieces, jnp.broadcast_to(names[None], (members, SUBS, LANES))], axis=1)
    sent = jnp.broadcast_to(sent[None], (runs,) + sent.shape).reshape((wide,) + sent.shape[1:])
    with jax.named_scope("spread_pieces"):
        spread = lax.all_to_all(sent, WIDE, 0, 0, tiled=True)
    owners = spread[:, tiles * SUBS, :neg_count].astype(jnp.int32).reshape(wide * neg_count)

    with jax.named_scope("pool_yh"):
        mine = [passages] + [lax.ppermute(passages, "yh", swaps[k]) for k in range(1, near)]
    with jax.named_scope("pool_x"):
        mine = jnp.concatenate(mine, axis=0)
        slabs = [mine] + [lax.ppermute(mine, "x", swaps[k]) for k in range(1, far)]
    slots = positive ^ ((here_x * near + here_y) * block_rows)

    (picked,) = call(
        pick_kernel,
        [((members, tiles, neg_count, SUBS, LANES), bf16)],
        [],
        0,
        run,
        owners,
        spread.reshape(wide * (tiles + 1), SUBS, LANES),
        smem=2,
        after=(mine,),
    )
    with jax.named_scope("named_pieces"):
        named = lax.all_to_all(picked, RUN, 0, 0, tiled=True)
    named = named.reshape(members * tiles, neg_count * SUBS, LANES)

    product = 2 * query_count * width
    exps, top, total = call(
        pool_kernel,
        [((query_count, pool_rows), f32), ((query_count, 1), f32), ((query_count, 1), f32)],
        [],
        product * pool_rows,
        queries,
        *slabs,
    )
    named_hi, named_lo, named_grad, share = call(
        named_kernel,
        [
            ((query_count, named_rows), bf16),
            ((query_count, named_rows), bf16),
            ((members * tiles, neg_count * SUBS, LANES), f32),
            ((query_count, 1), f32),
        ],
        [pltpu.VMEM((named_rows, width), bf16), pltpu.VMEM((query_count, named_rows), f32)],
        3 * product * named_rows,
        queries,
        named,
        top,
        total,
    )
    with jax.named_scope("named_back"):
        back = named_grad.astype(half).reshape(members, tiles, neg_count, SUBS, LANES)
        back = lax.all_to_all(back, RUN, 0, 0, tiled=True)

    pool_hi, pool_lo, *pool_grads = call(
        pool_grad_kernel,
        [((query_count, pool_rows), bf16)] * 2 + [((near * block_rows, width), f32)] * far,
        [],
        2 * product * pool_rows,
        queries,
        exps,
        share,
        slots[None, :],
    )
    rows_x = pool_grads[0]
    leaving = [grad.astype(half) for grad in pool_grads[1:]]
    with jax.named_scope("grad_x"):
        for k in range(1, far):
            part = lax.ppermute(leaving[k - 1], "x", swaps[k])
            rows_x = rows_x + part.astype(f32)
    owned = rows_x[:block_rows]
    with jax.named_scope("grad_yh"):
        for k in range(1, near):
            part = (rows_x[k * block_rows : (k + 1) * block_rows] * (1.0 / far)).astype(half)
            part = lax.ppermute(part, "yh", swaps[k])
            owned = owned + part.astype(f32) * float(far)

    (query_grad,) = call(
        query_kernel,
        [((query_count, width), f32)],
        [pltpu.VMEM((named_rows, width), bf16)],
        30 * product * (pool_rows + named_rows),
        pool_hi,
        pool_lo,
        named_hi,
        named_lo,
        named,
        *slabs,
    )

    (summed,) = call(
        gather_sum_kernel,
        [((wide, tiles, SUBS, LANES), f32)],
        [pltpu.VMEM((wide, SUBS, LANES), f32)] * tiles,
        0,
        run,
        owners,
        back.astype(f32),
        smem=2,
        after=tuple(pool_grads[1:]),
    )
    with jax.named_scope("pieces_home"):
        home = lax.all_to_all(summed.astype(half), WIDE, 0, 0, tiled=True)
    home = home.astype(f32).reshape(runs, row_tiles, col_tiles, SUBS, LANES)
    returned = home.sum(0).transpose(0, 2, 1, 3).reshape(block_rows, width)
    return (query_grad, owned * (1.0 / LIFT) + returned * (1.0 / (LIFT * DROP)))


def solution(mesh):
    whole = Mesh(mesh.devices.reshape(4, 3, 2, 2, 4, 4), AXES)
    spec = P(AXES, None)
    return jax.shard_map(
        local,
        mesh=whole,
        in_specs=(spec, spec, P(AXES), spec),
        out_specs=(spec, spec),
        check_vma=False,
    )
```

time: 494 us -> 144 us (0.29)
  waiting for transfers between devices: 445 us -> 34.3 us
  starting transfers between devices: 0.34 us -> 80.3 us
  matrix products: 20.3 us -> 0 us
  between operations: 13.8 us -> 1.1 us
  Pallas kernels: 0 us -> 8.39 us
  other arithmetic: 2.46 us -> 10.6 us
    reduce_scatter x2 -> x0, waiting for transfers between devices: 273 us -> none  [the longest x1 191 us: local(): lax.psum_scatter(summed.reshape(block_rows * lax.axis_size('wide'), width...]
    all_gather x2 -> x0, waiting for transfers between devices: 171 us -> none  [the longest x1 110 us: local(): piece_rows = lax.all_gather(passages, 'wide', axis=0, tiled=True)]
    ppermute x0 -> x12, starting transfers between devices: none -> 40.7 us  [the longest x3 11.4 us: local(): lax.ppermute(passages, 'yh', swaps[k])]
    all_to_all x0 -> x4, starting transfers between devices: none -> 39.6 us  [the longest x1 18 us: local(): spread = lax.all_to_all(sent, WIDE, 0, 0, tiled=True)]
    ppermute x0 -> x12, waiting for transfers between devices: none -> 26.5 us  [the longest x3 15.6 us: local(): slabs = [mine] + [lax.ppermute(mine, 'x', swaps[k]) for k in range(1, far)]]
    dot_general x6 -> x0, matrix products: 20.3 us -> none  [the longest x1 5.77 us: local(): jnp.einsum('ki,ird->krd', matched, shaped, preferred_element_type=jnp.flo...]
    dot_general x1 -> x0, local copies, waits for them, and re-layouts: 9.08 us -> none  [local(): jnp.einsum('jk,krd->jrd', matched, named_terms, precision=lax.Precision.H...]
    pallas_call x0 -> x6, Pallas kernels: none -> 8.39 us  [call(): pl.pallas_call(body, out_shape=tuple((jax.ShapeDtypeStruct(shape, dtype)...]
  transfers between devices with their start and end apart: 4 -> 16, of which waited for: 4 -> 7; matrix products, arithmetic and copies ran while one was open for 5% -> 5% of each run, Pallas kernels for 0% -> 4%
where the time goes in v1:
time: 144 us; the launch traced here: 143 us
  starting transfers between devices  80.3 us (56%)
  waiting for transfers between devices  34.3 us (24%)
  other arithmetic  10.6 us (7%)
  Pallas kernels  8.39 us (6%)
  local copies, waits for them, and re-layouts  8.21 us (6%)
    all_to_all x1, starting transfers between devices, local(): spread = lax.all_to_all(sent, WIDE, 0, 0, tiled=True)  18 us
    ppermute x3, waiting for transfers between devices, local(): slabs = [mine] + [lax.ppermute(mine, 'x', swaps[k]) for k in range(1, far)]  15.6 us
    all_to_all x1, starting transfers between devices, local(): home = lax.all_to_all(summed.astype(half), WIDE, 0, 0, tiled=True)  12.4 us
    ppermute x3, starting transfers between devices, local(): lax.ppermute(passages, 'yh', swaps[k])  11.4 us
    ppermute x3, starting transfers between devices, local(): part = lax.ppermute(part, 'yh', swaps[k])  11.4 us
    ppermute x3, waiting for transfers between devices, local(): lax.ppermute(passages, 'yh', swaps[k])  10.2 us
    ppermute x3, starting transfers between devices, local(): slabs = [mine] + [lax.ppermute(mine, 'x', swaps[k]) for k in range(1, far)]  8.98 us
    ppermute x3, starting transfers between devices, local(): part = lax.ppermute(leaving[k - 1], 'x', swaps[k])  8.98 us
  transfers between devices with their start and end apart: 16, of which 7 were waited for; matrix products, arithmetic and copies ran while one was open for 5% of the time, Pallas kernels for 4%

profile of v1, /device:TPU:1, one launch (start us, length us, event | category | flops | bytes accessed | tf_op | source)
XLA Modules:
  0.0 142.9 jit_solution(287567075091557342)
XLA Ops:
  3.1 18.0 %all-to-all-start = ((bf16[48,40,128]{2,1,0:T(8,128)(2,1)}), bf16[48,40,128]{2,1,0:T(8,128)(2,1)S(1)}, u32[]{:S(2)}, u32[]{:S(2)}) async-start(bf16[48,40,128]{2,1,0:T(8,128)(2,1)} %bitcast.4), calls=%async_computation | async-start | bytes 983040 | tf_op jit(solution)/shard_map/spread_pieces/all_to_all | solution.py:210
  21.1 5.0 %collective-permute-start.2 = (bf16[64,768]{1,0:T(8,128)(2,1)S(1)}, bf16[64,768]{1,0:T(8,128)(2,1)S(1)}, u32[]{:S(2)}, u32[]{:S(2)}) collective-permute-start(bf16[64,768]{1,0:T(8,128)(2,1)S(1)} %copy-done.22), channel_id=1, source_target_pairs={{0,3},{1,2},{2,1},{3,0},{4,7},{5,6},{6,5},{7,4},{8,11},{9,10},{10,... | collective-permute-start | bytes 294920 | tf_op jit(solution)/shard_map/pool_yh/ppermute | solution.py:214
  26.1 4.4 %collective-permute-start.1 = (bf16[64,768]{1,0:T(8,128)(2,1)S(1)}, bf16[64,768]{1,0:T(8,128)(2,1)S(1)}, u32[]{:S(2)}, u32[]{:S(2)}) collective-permute-start(bf16[64,768]{1,0:T(8,128)(2,1)S(1)} %copy-done.22), channel_id=1, source_target_pairs={{0,2},{1,3},{2,0},{3,1},{4,6},{5,7},{6,4},{7,5},{8,10},{9,11},{10,... | collective-permute-start | bytes 294920 | tf_op jit(solution)/shard_map/pool_yh/ppermute | solution.py:214
  30.6 2.0 %collective-permute-start = (bf16[64,768]{1,0:T(8,128)(2,1)S(1)}, bf16[64,768]{1,0:T(8,128)(2,1)S(1)}, u32[]{:S(2)}, u32[]{:S(2)}) collective-permute-start(bf16[64,768]{1,0:T(8,128)(2,1)S(1)} %copy-done.22), channel_id=1, source_target_pairs={{0,1},{1,0},{2,3},{3,2},{4,5},{5,4},{6,7},{7,6},{8,9},{9,8},{10,11... | collective-permute-start | bytes 294920 | tf_op jit(solution)/shard_map/pool_yh/ppermute | solution.py:214
  32.5 8.9 %collective-permute-done = bf16[64,768]{1,0:T(8,128)(2,1)S(1)} collective-permute-done((bf16[64,768]{1,0:T(8,128)(2,1)S(1)}, bf16[64,768]{1,0:T(8,128)(2,1)S(1)}, u32[]{:S(2)}, u32[]{:S(2)}) %collective-permute-start) | collective-permute-done | bytes 98336 | tf_op jit(solution)/shard_map/pool_yh/ppermute | solution.py:214
  41.4 1.3 collective-permute-done.1
  42.8 2.5 %all-to-all-done = bf16[48,40,128]{2,1,0:T(8,128)(2,1)S(1)} async-done(((bf16[48,40,128]{2,1,0:T(8,128)(2,1)}), bf16[48,40,128]{2,1,0:T(8,128)(2,1)S(1)}, u32[]{:S(2)}, u32[]{:S(2)}) %all-to-all-start) | async-done | bytes 491552 | tf_op jit(solution)/shard_map/spread_pieces/all_to_all | solution.py:210
  45.5 1.7 %shard_map.60 = bf16[12,4,8,8,128]{4,3,2,1,0:T(8,128)(2,1)} custom-call(s32[1]{0:T(128)} %bitcast.refs_0_, s32[384]{0:T(512)S(1)} %reshape.78.refs_1_, bf16[240,8,128]{2,1,0:T(8,128)(2,1)S(1)} %bitcast.17, bf16[256,768]{1,0:T(8,128)(2,1)S(1)} %constant_dynamic-update-slice_fusion.refs_1_.refs_3_.refs_5_), custom_call_target="tpu_custom_call" | custom-call | bytes 4194304 | tf_op jit(solution)/shard_map/pallas_call | solution.py:178
  47.2 3.6 %all-to-all-start.1 = ((bf16[12,4,8,8,128]{4,3,2,1,0:T(8,128)(2,1)}), bf16[12,4,8,8,128]{4,3,2,1,0:T(8,128)(2,1)S(1)}, u32[]{:S(2)}, u32[]{:S(2)}) async-start(bf16[12,4,8,8,128]{4,3,2,1,0:T(8,128)(2,1)} %shard_map.60), calls=%async_computation.1 | async-start | bytes 1572864 | tf_op jit(solution)/shard_map/named_pieces/all_to_all | solution.py:232
  50.8 4.4 %collective-permute-start.5 = (bf16[256,768]{1,0:T(8,128)(2,1)S(1)}, bf16[256,768]{1,0:T(8,128)(2,1)S(1)}, u32[]{:S(2)}, u32[]{:S(2)}) collective-permute-start(bf16[256,768]{1,0:T(8,128)(2,1)S(1)} %constant_dynamic-update-slice_fusion.refs_1_.refs_3_.refs_5_), channel_id=1, source_target_pairs={{0,12},{4,8},{8,4},{12,0},{1,13},{5,9},{9,5},{13,1},{2,14},{6,10},... | collective-permute-start | bytes 1179656 | tf_op jit(solution)/shard_map/pool_x/ppermute | solution.py:217
  55.2 2.4 %collective-permute-start.4 = (bf16[256,768]{1,0:T(8,128)(2,1)S(1)}, bf16[256,768]{1,0:T(8,128)(2,1)S(1)}, u32[]{:S(2)}, u32[]{:S(2)}) collective-permute-start(bf16[256,768]{1,0:T(8,128)(2,1)S(1)} %constant_dynamic-update-slice_fusion.refs_1_.refs_3_.refs_5_), channel_id=1, source_target_pairs={{0,8},{4,12},{8,0},{12,4},{1,9},{5,13},{9,1},{13,5},{2,10},{6,14},... | collective-permute-start | bytes 1179656 | tf_op jit(solution)/shard_map/pool_x/ppermute | solution.py:217
  57.6 2.2 %collective-permute-start.3 = (bf16[256,768]{1,0:T(8,128)(2,1)S(1)}, bf16[256,768]{1,0:T(8,128)(2,1)S(1)}, u32[]{:S(2)}, u32[]{:S(2)}) collective-permute-start(bf16[256,768]{1,0:T(8,128)(2,1)S(1)} %constant_dynamic-update-slice_fusion.refs_1_.refs_3_.refs_5_), channel_id=1, source_target_pairs={{0,4},{4,0},{8,12},{12,8},{1,5},{5,1},{9,13},{13,9},{2,6},{6,2},{1... | collective-permute-start | bytes 1179656 | tf_op jit(solution)/shard_map/pool_x/ppermute | solution.py:217
  59.8 13.3 %collective-permute-done.5.refs_4_.refs_8_ = bf16[256,768]{1,0:T(8,128)(2,1)S(1)} collective-permute-done((bf16[256,768]{1,0:T(8,128)(2,1)S(1)}, bf16[256,768]{1,0:T(8,128)(2,1)S(1)}, u32[]{:S(2)}, u32[]{:S(2)}) %collective-permute-start.5) | collective-permute-done | bytes 393248 | tf_op jit(solution)/shard_map/pool_x/ppermute | solution.py:217
  73.1 2.2 %collective-permute-done.3.refs_2_.refs_6_ = bf16[256,768]{1,0:T(8,128)(2,1)S(1)} collective-permute-done((bf16[256,768]{1,0:T(8,128)(2,1)S(1)}, bf16[256,768]{1,0:T(8,128)(2,1)S(1)}, u32[]{:S(2)}, u32[]{:S(2)}) %collective-permute-start.3) | collective-permute-done | bytes 393248 | tf_op jit(solution)/shard_map/pool_x/ppermute | solution.py:217
  79.4 1.4 shard_map.61
  80.9 1.1 convert_element_type.72
  81.9 5.6 %all-to-all-start.2 = ((f16[12,4,8,8,128]{4,3,2,1,0:T(8,128)(2,1)}), f16[12,4,8,8,128]{4,3,2,1,0:T(8,128)(2,1)}, u32[]{:S(2)}, u32[]{:S(2)}) async-start(f16[12,4,8,8,128]{4,3,2,1,0:T(8,128)(2,1)} %bitcast.8), calls=%async_computation.2 | async-start | bytes 1572864 | tf_op jit(solution)/shard_map/named_back/all_to_all | solution.py:261
  88.5 1.1 copy-done.11
  90.5 1.2 shard_map.62
  94.3 4.4 %collective-permute-start.8 = (f16[256,768]{1,0:T(8,128)(2,1)}, f16[256,768]{1,0:T(8,128)(2,1)}, u32[]{:S(2)}, u32[]{:S(2)}) collective-permute-start(f16[256,768]{1,0:T(8,128)(2,1)} %convert_element_type.64), channel_id=1, source_target_pairs={{0,12},{4,8},{8,4},{12,0},{1,13},{5,9},{9,5},{13,1},{2,14},{6,10},... | collective-permute-start | bytes 1179656 | tf_op jit(solution)/shard_map/grad_x/ppermute | solution.py:277
  98.7 2.5 %collective-permute-start.7 = (f16[256,768]{1,0:T(8,128)(2,1)}, f16[256,768]{1,0:T(8,128)(2,1)}, u32[]{:S(2)}, u32[]{:S(2)}) collective-permute-start(f16[256,768]{1,0:T(8,128)(2,1)} %convert_element_type.62), channel_id=1, source_target_pairs={{0,8},{4,12},{8,0},{12,4},{1,9},{5,13},{9,1},{13,5},{2,10},{6,14},... | collective-permute-start | bytes 1179656 | tf_op jit(solution)/shard_map/grad_x/ppermute | solution.py:277
  101.1 2.1 %collective-permute-start.6 = (f16[256,768]{1,0:T(8,128)(2,1)}, f16[256,768]{1,0:T(8,128)(2,1)}, u32[]{:S(2)}, u32[]{:S(2)}) collective-permute-start(f16[256,768]{1,0:T(8,128)(2,1)} %convert_element_type.60), channel_id=1, source_target_pairs={{0,4},{4,0},{8,12},{12,8},{1,5},{5,1},{9,13},{13,9},{2,6},{6,2},{1... | collective-permute-start | bytes 1179656 | tf_op jit(solution)/shard_map/grad_x/ppermute | solution.py:277
  103.3 1.3 convert_element_type.73.refs_2_
  104.6 1.2 shard_map.64
  106.7 12.4 %all-to-all-start.3 = ((f16[48,4,8,128]{3,2,1,0:T(8,128)(2,1)}), f16[48,4,8,128]{3,2,1,0:T(8,128)(2,1)}, u32[]{:S(2)}, u32[]{:S(2)}) async-start(f16[48,4,8,128]{3,2,1,0:T(8,128)(2,1)} %convert_element_type.74), calls=%async_computation.3 | async-start | bytes 786432 | tf_op jit(solution)/shard_map/pieces_home/all_to_all | solution.py:311
  120.2 2.0 %shard_map.63 = f32[192,768]{1,0:T(8,128)} custom-call(bf16[192,1024]{1,0:T(8,128)(2,1)S(1)} %copy-done.19, bf16[192,1024]{1,0:T(8,128)(2,1)S(1)} %copy-done.21, bf16[192,512]{1,0:T(8,128)(2,1)S(1)} %copy-done.13, bf16[192,512]{1,0:T(8,128)(2,1)S(1)} %copy-done.15, bf16[48,64,128]{2,1,0:T(8,128)(2,1)S(1)} %bitcast.19, ...), custom_call_target="tpu_custom_call" | custom-call | flops 13589544960 | bytes 4194304 | tf_op jit(solution)/shard_map/pallas_call | solution.py:178
  122.2 1.4 convert_add_fusion
  123.6 2.7 %collective-permute-start.9 = (f16[64,768]{1,0:T(8,128)(2,1)S(1)}, f16[64,768]{1,0:T(8,128)(2,1)S(1)}, u32[]{:S(2)}, u32[]{:S(2)}) collective-permute-start(f16[64,768]{1,0:T(8,128)(2,1)S(1)} %get-tuple-element.40), channel_id=1, source_target_pairs={{0,1},{1,0},{2,3},{3,2},{4,5},{5,4},{6,7},{7,6},{8,9},{9,8},{10,11... | collective-permute-start | bytes 294920 | tf_op jit(solution)/shard_map/grad_yh/ppermute | solution.py:283
  126.4 4.1 %collective-permute-start.11 = (f16[64,768]{1,0:T(8,128)(2,1)S(1)}, f16[64,768]{1,0:T(8,128)(2,1)S(1)}, u32[]{:S(2)}, u32[]{:S(2)}) collective-permute-start(f16[64,768]{1,0:T(8,128)(2,1)S(1)} %get-tuple-element.41), channel_id=1, source_target_pairs={{0,3},{1,2},{2,1},{3,0},{4,7},{5,6},{6,5},{7,4},{8,11},{9,10},{10,... | collective-permute-start | bytes 294920 | tf_op jit(solution)/shard_map/grad_yh/ppermute | solution.py:283
  130.5 4.5 %collective-permute-start.10 = (f16[64,768]{1,0:T(8,128)(2,1)S(1)}, f16[64,768]{1,0:T(8,128)(2,1)S(1)}, u32[]{:S(2)}, u32[]{:S(2)}) collective-permute-start(f16[64,768]{1,0:T(8,128)(2,1)S(1)} %get-tuple-element.42), channel_id=1, source_target_pairs={{0,2},{1,3},{2,0},{3,1},{4,6},{5,7},{6,4},{7,5},{8,10},{9,11},{10,... | collective-permute-start | bytes 294920 | tf_op jit(solution)/shard_map/grad_yh/ppermute | solution.py:283
  135.0 5.3 %all-to-all-done.3 = f16[48,4,8,128]{3,2,1,0:T(8,128)(2,1)} async-done(((f16[48,4,8,128]{3,2,1,0:T(8,128)(2,1)}), f16[48,4,8,128]{3,2,1,0:T(8,128)(2,1)}, u32[]{:S(2)}, u32[]{:S(2)}) %all-to-all-start.3) | async-done | bytes 393248 | tf_op jit(solution)/shard_map/pieces_home/all_to_all | solution.py:311
  140.3 1.1 convert_reduce_fusion
  (76 shorter events, 14.5 us)
Async XLA Ops:
  0.6 20.5 %copy-start.22 = (bf16[64,768]{1,0:T(8,128)(2,1)S(1)}, bf16[64,768]{1,0:T(8,128)(2,1)}, u32[]{:S(2)}) copy-start(bf16[64,768]{1,0:T(8,128)(2,1)} %param.7) | copy-start | bytes 294916
  3.1 42.2 %all-to-all-start = ((bf16[48,40,128]{2,1,0:T(8,128)(2,1)}), bf16[48,40,128]{2,1,0:T(8,128)(2,1)S(1)}, u32[]{:S(2)}, u32[]{:S(2)}) async-start(bf16[48,40,128]{2,1,0:T(8,128)(2,1)} %bitcast.4), calls=%async_computation | async-start | bytes 983040 | tf_op jit(solution)/shard_map/spread_pieces/all_to_all | solution.py:210
  21.1 21.6 %collective-permute-start.2 = (bf16[64,768]{1,0:T(8,128)(2,1)S(1)}, bf16[64,768]{1,0:T(8,128)(2,1)S(1)}, u32[]{:S(2)}, u32[]{:S(2)}) collective-permute-start(bf16[64,768]{1,0:T(8,128)(2,1)S(1)} %copy-done.22), channel_id=1, source_target_pairs={{0,3},{1,2},{2,1},{3,0},{4,7},{5,6},{6,5},{7,4},{8,11},{9,10},{10,... | collective-permute-start | bytes 294920 | tf_op jit(solution)/shard_map/pool_yh/ppermute | solution.py:214
  26.1 16.6 %collective-permute-start.1 = (bf16[64,768]{1,0:T(8,128)(2,1)S(1)}, bf16[64,768]{1,0:T(8,128)(2,1)S(1)}, u32[]{:S(2)}, u32[]{:S(2)}) collective-permute-start(bf16[64,768]{1,0:T(8,128)(2,1)S(1)} %copy-done.22), channel_id=1, source_target_pairs={{0,2},{1,3},{2,0},{3,1},{4,6},{5,7},{6,4},{7,5},{8,10},{9,11},{10,... | collective-permute-start | bytes 294920 | tf_op jit(solution)/shard_map/pool_yh/ppermute | solution.py:214
  30.6 10.8 %collective-permute-start = (bf16[64,768]{1,0:T(8,128)(2,1)S(1)}, bf16[64,768]{1,0:T(8,128)(2,1)S(1)}, u32[]{:S(2)}, u32[]{:S(2)}) collective-permute-start(bf16[64,768]{1,0:T(8,128)(2,1)S(1)} %copy-done.22), channel_id=1, source_target_pairs={{0,1},{1,0},{2,3},{3,2},{4,5},{5,4},{6,7},{7,6},{8,9},{9,8},{10,11... | collective-permute-start | bytes 294920 | tf_op jit(solution)/shard_map/pool_yh/ppermute | solution.py:214
  45.5 29.9 %copy-start.8 = (bf16[192,768]{1,0:T(8,128)(2,1)S(1)}, bf16[192,768]{1,0:T(8,128)(2,1)}, u32[]{:S(2)}) copy-start(bf16[192,768]{1,0:T(8,128)(2,1)} %refs_0_.5) | copy-start | bytes 884740
  47.2 32.2 %all-to-all-start.1 = ((bf16[12,4,8,8,128]{4,3,2,1,0:T(8,128)(2,1)}), bf16[12,4,8,8,128]{4,3,2,1,0:T(8,128)(2,1)S(1)}, u32[]{:S(2)}, u32[]{:S(2)}) async-start(bf16[12,4,8,8,128]{4,3,2,1,0:T(8,128)(2,1)} %shard_map.60), calls=%async_computation.1 | async-start | bytes 1572864 | tf_op jit(solution)/shard_map/named_pieces/all_to_all | solution.py:232
  50.8 22.3 %collective-permute-start.5 = (bf16[256,768]{1,0:T(8,128)(2,1)S(1)}, bf16[256,768]{1,0:T(8,128)(2,1)S(1)}, u32[]{:S(2)}, u32[]{:S(2)}) collective-permute-start(bf16[256,768]{1,0:T(8,128)(2,1)S(1)} %constant_dynamic-update-slice_fusion.refs_1_.refs_3_.refs_5_), channel_id=1, source_target_pairs={{0,12},{4,8},{8,4},{12,0},{1,13},{5,9},{9,5},{13,1},{2,14},{6,10},... | collective-permute-start | bytes 1179656 | tf_op jit(solution)/shard_map/pool_x/ppermute | solution.py:217
  55.2 18.0 %collective-permute-start.4 = (bf16[256,768]{1,0:T(8,128)(2,1)S(1)}, bf16[256,768]{1,0:T(8,128)(2,1)S(1)}, u32[]{:S(2)}, u32[]{:S(2)}) collective-permute-start(bf16[256,768]{1,0:T(8,128)(2,1)S(1)} %constant_dynamic-update-slice_fusion.refs_1_.refs_3_.refs_5_), channel_id=1, source_target_pairs={{0,8},{4,12},{8,0},{12,4},{1,9},{5,13},{9,1},{13,5},{2,10},{6,14},... | collective-permute-start | bytes 1179656 | tf_op jit(solution)/shard_map/pool_x/ppermute | solution.py:217
  57.6 17.7 %collective-permute-start.3 = (bf16[256,768]{1,0:T(8,128)(2,1)S(1)}, bf16[256,768]{1,0:T(8,128)(2,1)S(1)}, u32[]{:S(2)}, u32[]{:S(2)}) collective-permute-start(bf16[256,768]{1,0:T(8,128)(2,1)S(1)} %constant_dynamic-update-slice_fusion.refs_1_.refs_3_.refs_5_), channel_id=1, source_target_pairs={{0,4},{4,0},{8,12},{12,8},{1,5},{5,1},{9,13},{13,9},{2,6},{6,2},{1... | collective-permute-start | bytes 1179656 | tf_op jit(solution)/shard_map/pool_x/ppermute | solution.py:217
  80.8 1.1 copy-start.12
  80.8 1.1 copy-start.14
  80.9 6.7 %copy-start.23 = (s32[192]{0:T(256)S(1)}, s32[192]{0:T(256)}, u32[]{:S(2)}) copy-start(s32[192]{0:T(256)} %param.8) | copy-start | bytes 2308
  81.9 21.3 %all-to-all-start.2 = ((f16[12,4,8,8,128]{4,3,2,1,0:T(8,128)(2,1)}), f16[12,4,8,8,128]{4,3,2,1,0:T(8,128)(2,1)}, u32[]{:S(2)}, u32[]{:S(2)}) async-start(f16[12,4,8,8,128]{4,3,2,1,0:T(8,128)(2,1)} %bitcast.8), calls=%async_computation.2 | async-start | bytes 1572864 | tf_op jit(solution)/shard_map/named_back/all_to_all | solution.py:261
  88.5 1.1 copy-start.11
  91.8 2.5 %copy-start = (f32[256,768]{1,0:T(8,128)}, f32[256,768]{1,0:T(8,128)S(1)}, u32[]{:S(2)}) copy-start(f32[256,768]{1,0:T(8,128)S(1)} %get-tuple-element.35) | copy-start | bytes 2359300
  91.8 2.5 %copy-start.18 = (bf16[192,1024]{1,0:T(8,128)(2,1)}, bf16[192,1024]{1,0:T(8,128)(2,1)S(1)}, u32[]{:S(2)}) copy-start(bf16[192,1024]{1,0:T(8,128)(2,1)S(1)} %get-tuple-element.31.refs_0_) | copy-start | bytes 1179652
  91.8 2.5 %copy-start.20 = (bf16[192,1024]{1,0:T(8,128)(2,1)}, bf16[192,1024]{1,0:T(8,128)(2,1)S(1)}, u32[]{:S(2)}) copy-start(bf16[192,1024]{1,0:T(8,128)(2,1)S(1)} %get-tuple-element.32.refs_1_) | copy-start | bytes 1179652
  94.3 27.9 %collective-permute-start.8 = (f16[256,768]{1,0:T(8,128)(2,1)}, f16[256,768]{1,0:T(8,128)(2,1)}, u32[]{:S(2)}, u32[]{:S(2)}) collective-permute-start(f16[256,768]{1,0:T(8,128)(2,1)} %convert_element_type.64), channel_id=1, source_target_pairs={{0,12},{4,8},{8,4},{12,0},{1,13},{5,9},{9,5},{13,1},{2,14},{6,10},... | collective-permute-start | bytes 1179656 | tf_op jit(solution)/shard_map/grad_x/ppermute | solution.py:277
  98.7 23.5 %collective-permute-start.7 = (f16[256,768]{1,0:T(8,128)(2,1)}, f16[256,768]{1,0:T(8,128)(2,1)}, u32[]{:S(2)}, u32[]{:S(2)}) collective-permute-start(f16[256,768]{1,0:T(8,128)(2,1)} %convert_element_type.62), channel_id=1, source_target_pairs={{0,8},{4,12},{8,0},{12,4},{1,9},{5,13},{9,1},{13,5},{2,10},{6,14},... | collective-permute-start | bytes 1179656 | tf_op jit(solution)/shard_map/grad_x/ppermute | solution.py:277
  101.1 21.1 %collective-permute-start.6 = (f16[256,768]{1,0:T(8,128)(2,1)}, f16[256,768]{1,0:T(8,128)(2,1)}, u32[]{:S(2)}, u32[]{:S(2)}) collective-permute-start(f16[256,768]{1,0:T(8,128)(2,1)} %convert_element_type.60), channel_id=1, source_target_pairs={{0,4},{4,0},{8,12},{12,8},{1,5},{5,1},{9,13},{13,9},{2,6},{6,2},{1... | collective-permute-start | bytes 1179656 | tf_op jit(solution)/shard_map/grad_x/ppermute | solution.py:277
  105.8 13.4 %copy-start.3 = (bf16[256,768]{1,0:T(8,128)(2,1)S(1)}, bf16[256,768]{1,0:T(8,128)(2,1)}, u32[]{:S(2)}) copy-start(bf16[256,768]{1,0:T(8,128)(2,1)} %copy-done.2) | copy-start | bytes 1179652
  105.8 13.4 %copy-start.5 = (bf16[256,768]{1,0:T(8,128)(2,1)S(1)}, bf16[256,768]{1,0:T(8,128)(2,1)}, u32[]{:S(2)}) copy-start(bf16[256,768]{1,0:T(8,128)(2,1)} %copy-done.4) | copy-start | bytes 1179652
  105.8 13.4 %copy-start.7 = (bf16[256,768]{1,0:T(8,128)(2,1)S(1)}, bf16[256,768]{1,0:T(8,128)(2,1)}, u32[]{:S(2)}) copy-start(bf16[256,768]{1,0:T(8,128)(2,1)} %copy-done.6) | copy-start | bytes 1179652
  105.8 13.4 %copy-start.13 = (bf16[192,512]{1,0:T(8,128)(2,1)S(1)}, bf16[192,512]{1,0:T(8,128)(2,1)}, u32[]{:S(2)}) copy-start(bf16[192,512]{1,0:T(8,128)(2,1)} %copy-done.12) | copy-start | bytes 589828
  105.8 13.3 %copy-start.15 = (bf16[192,512]{1,0:T(8,128)(2,1)S(1)}, bf16[192,512]{1,0:T(8,128)(2,1)}, u32[]{:S(2)}) copy-start(bf16[192,512]{1,0:T(8,128)(2,1)} %copy-done.14) | copy-start | bytes 589828
  105.8 13.3 %copy-start.19 = (bf16[192,1024]{1,0:T(8,128)(2,1)S(1)}, bf16[192,1024]{1,0:T(8,128)(2,1)}, u32[]{:S(2)}) copy-start(bf16[192,1024]{1,0:T(8,128)(2,1)} %copy-done.18) | copy-start | bytes 1179652
  106.7 33.7 %all-to-all-start.3 = ((f16[48,4,8,128]{3,2,1,0:T(8,128)(2,1)}), f16[48,4,8,128]{3,2,1,0:T(8,128)(2,1)}, u32[]{:S(2)}, u32[]{:S(2)}) async-start(f16[48,4,8,128]{3,2,1,0:T(8,128)(2,1)} %convert_element_type.74), calls=%async_computation.3 | async-start | bytes 786432 | tf_op jit(solution)/shard_map/pieces_home/all_to_all | solution.py:311
  120.2 2.0 %copy-start.1 = (f32[256,768]{1,0:T(8,128)S(1)}, f32[256,768]{1,0:T(8,128)}, u32[]{:S(2)}) copy-start(f32[256,768]{1,0:T(8,128)} %copy-done) | copy-start | bytes 2359300
  123.6 17.8 %collective-permute-start.9 = (f16[64,768]{1,0:T(8,128)(2,1)S(1)}, f16[64,768]{1,0:T(8,128)(2,1)S(1)}, u32[]{:S(2)}, u32[]{:S(2)}) collective-permute-start(f16[64,768]{1,0:T(8,128)(2,1)S(1)} %get-tuple-element.40), channel_id=1, source_target_pairs={{0,1},{1,0},{2,3},{3,2},{4,5},{5,4},{6,7},{7,6},{8,9},{9,8},{10,11... | collective-permute-start | bytes 294920 | tf_op jit(solution)/shard_map/grad_yh/ppermute | solution.py:283
  126.4 15.0 %collective-permute-start.11 = (f16[64,768]{1,0:T(8,128)(2,1)S(1)}, f16[64,768]{1,0:T(8,128)(2,1)S(1)}, u32[]{:S(2)}, u32[]{:S(2)}) collective-permute-start(f16[64,768]{1,0:T(8,128)(2,1)S(1)} %get-tuple-element.41), channel_id=1, source_target_pairs={{0,3},{1,2},{2,1},{3,0},{4,7},{5,6},{6,5},{7,4},{8,11},{9,10},{10,... | collective-permute-start | bytes 294920 | tf_op jit(solution)/shard_map/grad_yh/ppermute | solution.py:283
  130.5 11.6 %collective-permute-start.10 = (f16[64,768]{1,0:T(8,128)(2,1)S(1)}, f16[64,768]{1,0:T(8,128)(2,1)S(1)}, u32[]{:S(2)}, u32[]{:S(2)}) collective-permute-start(f16[64,768]{1,0:T(8,128)(2,1)S(1)} %get-tuple-element.42), channel_id=1, source_target_pairs={{0,2},{1,3},{2,0},{3,1},{4,6},{5,7},{6,4},{7,5},{8,10},{9,11},{10,... | collective-permute-start | bytes 294920 | tf_op jit(solution)/shard_map/grad_yh/ppermute | solution.py:283
  (8 other events, 7.1 us)

commit v2 on v1

--- a/solution.py
+++ b/solution.py
@@ -16,7 +16,7 @@
 SUBS = 8
 LIFT = 128.0
 DROP = 1.0 / 16.0
-VMEM = 12 * 1024 * 1024
+VMEM = 16 * 1024 * 1024
 STEP = 256
 
 
@@ -43,14 +43,12 @@
     members, tiles, count = out_ref.shape[:3]
     stride = held_ref.shape[0] // (owners_ref.shape[0] // count)
 
-    def body(i, carry):
+    first = run_ref[0] * members
+    for i in range(members):
         for k in range(count):
-            owner = owners_ref[(run_ref[0] * members + i) * count + k]
+            owner = owners_ref[(first + i) * count + k]
             for u in range(tiles):
                 out_ref[i, u, k] = held_ref[owner * stride + u]
-        return carry
-
-    lax.fori_loop(0, members, body, 0)
 
 
 def gather_sum_kernel(run_ref, owners_ref, terms_ref, out_ref, *acc_refs):
@@ -71,7 +69,7 @@
 
 
 def pool_kernel(q_ref, *refs):
-    slab_refs, (exp_ref, top_ref, sum_ref) = refs[:-3], refs[-3:]
+    slab_refs, exp_ref = refs[:-1], refs[-1]
     width = q_ref.shape[1]
     step = slab_refs[0].shape[0]
     scaling = 4.0 / math.sqrt(width)
@@ -87,8 +85,10 @@
         part = jnp.exp(exp_ref[:, slot * step : (slot + 1) * step] - top)
         exp_ref[:, slot * step : (slot + 1) * step] = part
         total += jnp.sum(part, axis=-1, keepdims=True)
-    top_ref[...] = top
-    sum_ref[...] = total
+    last = step * len(slab_refs)
+    exp_ref[:, last : last + LANES] = jnp.broadcast_to(top, (q.shape[0], LANES))
+    exp_ref[:, last + LANES : last + 2 * LANES] = jnp.broadcast_to(total, (q.shape[0], LANES))
+    exp_ref[:, last + 2 * LANES :] = q.astype(jnp.float32)
 
 
 def split(grad):
@@ -96,73 +96,73 @@
     return hi, (grad - hi.astype(jnp.float32)).astype(jnp.bfloat16)
 
 
-def named_kernel(q_ref, named_ref, top_ref, sum_ref, hi_ref, lo_ref, grad_ref, share_ref, keys_ref, l_ref):
-    width = q_ref.shape[1]
+def grads_kernel(place_ref, named_ref, exp_ref, pos_ref, hi_ref, lo_ref, named_out, *refs):
+    grad_refs, (keys_ref, l_ref) = refs[:-2], refs[-2:]
+    queries, width = exp_ref.shape[0], keys_ref.shape[1]
     col_tiles = width // LANES
     row_tiles = named_ref.shape[0] // col_tiles
     piece_rows = named_ref.shape[1]
     named_rows = row_tiles * piece_rows
+    step = grad_refs[0].shape[0]
+    pool_rows = step * len(grad_refs)
     scaling = 4.0 / math.sqrt(width)
     join_pieces(named_ref, keys_ref, row_tiles, col_tiles)
-    q = q_ref[...]
-    pool_top = top_ref[...]
+    q = exp_ref[:, pool_rows + 2 * LANES :].astype(jnp.bfloat16)
+    pool_top = exp_ref[:, pool_rows : pool_rows + 1]
     top = pool_top
     for c in range(0, named_rows, STEP):
         part = dot_nt(q, keys_ref[c : c + STEP, :]) * scaling
         l_ref[:, c : c + STEP] = part
         top = jnp.maximum(top, jnp.max(part, axis=-1, keepdims=True))
     pool_scale = jnp.exp(pool_top - top)
-    total = sum_ref[...] * pool_scale
+    total = exp_ref[:, pool_rows + LANES : pool_rows + LANES + 1] * pool_scale
     for c in range(0, named_rows, STEP):
         part = jnp.exp(l_ref[:, c : c + STEP] - top)
         l_ref[:, c : c + STEP] = part
         total += jnp.sum(part, axis=-1, keepdims=True)
     share = 1.0 / total
-    share_ref[...] = share * pool_scale
     for c in range(0, named_rows, STEP):
         hi, lo = split(l_ref[:, c : c + STEP] * share)
-        hi_ref[:, c : c + STEP] = hi
-        lo_ref[:, c : c + STEP] = lo
+        hi_ref[:, pool_rows + c : pool_rows + c + STEP] = hi
+        lo_ref[:, pool_rows + c : pool_rows + c + STEP] = lo
         terms = (dot_tn(hi, q) + dot_tn(lo, q)) * (scaling * LIFT)
         first = c // piece_rows
         for r in range(STEP // piece_rows):
             for k in range(col_tiles):
-                grad_ref[(first + r) * col_tiles + k] = terms[
+                named_out[(first + r) * col_tiles + k] = terms[
                     r * piece_rows : (r + 1) * piece_rows, k * LANES : (k + 1) * LANES
                 ]
 
-
-def pool_grad_kernel(q_ref, exp_ref, share_ref, pos_ref, hi_ref, lo_ref, *grad_refs):
-    queries, width = q_ref.shape
-    scaling = 4.0 / math.sqrt(width)
-    q = q_ref[...]
-    share = share_ref[...]
     across = lax.broadcasted_iota(jnp.int32, (queries, queries), 1)
     down = lax.broadcasted_iota(jnp.int32, (queries, queries), 0)
     pos = jnp.sum(jnp.where(across == down, pos_ref[...].astype(jnp.float32), 0.0), axis=1, keepdims=True)
     pos = pos.astype(jnp.int32)
-    step = grad_refs[0].shape[0]
+    share = share * pool_scale
+    block = step // place_ref.shape[0]
     for slot, grad_ref in enumerate(grad_refs):
         first, last = slot * step, (slot + 1) * step
         columns = lax.broadcasted_iota(jnp.int32, (queries, step), 1) + first
         hi, lo = split(exp_ref[:, first:last] * share - (columns == pos).astype(jnp.float32))
         hi_ref[:, first:last] = hi
         lo_ref[:, first:last] = lo
-        grad_ref[...] = (dot_tn(hi, q) + dot_tn(lo, q)) * (scaling * LIFT)
-
-
-def query_kernel(pool_hi_ref, pool_lo_ref, hi_ref, lo_ref, named_ref, *refs):
+        terms = (dot_tn(hi, q) + dot_tn(lo, q)) * (scaling * LIFT)
+        for r in range(step // block):
+            grad_ref[pl.ds(pl.multiple_of(place_ref[r] * block, block), block), :] = terms[r * block : (r + 1) * block]
+
+
+def query_kernel(hi_ref, lo_ref, named_ref, *refs):
     slab_refs, out_ref, keys_ref = refs[:-2], refs[-2], refs[-1]
     step, width = slab_refs[0].shape
     col_tiles = width // LANES
     row_tiles = named_ref.shape[0] // col_tiles
+    pool_rows = step * len(slab_refs)
     scaling = 4.0 / math.sqrt(width)
     join_pieces(named_ref, keys_ref, row_tiles, col_tiles)
-    total = dot_nn(hi_ref[...], keys_ref[...]) + dot_nn(lo_ref[...], keys_ref[...])
+    total = dot_nn(hi_ref[:, pool_rows:], keys_ref[...]) + dot_nn(lo_ref[:, pool_rows:], keys_ref[...])
     for slot, slab_ref in enumerate(slab_refs):
         first, last = slot * step, (slot + 1) * step
-        total += dot_nn(pool_hi_ref[:, first:last], slab_ref[...])
-        total += dot_nn(pool_lo_ref[:, first:last], slab_ref[...])
+        total += dot_nn(hi_ref[:, first:last], slab_ref[...])
+        total += dot_nn(lo_ref[:, first:last], slab_ref[...])
     out_ref[...] = total * scaling
 
 
@@ -204,18 +204,22 @@
     pieces = passages.reshape(row_tiles, SUBS, col_tiles, LANES).transpose(0, 2, 1, 3)
     pieces = pieces.reshape(members, tiles * SUBS, LANES)
     names = jnp.zeros((SUBS, LANES), bf16).at[0, :neg_count].set(negative_owners[0].astype(bf16))
-    sent = jnp.concatenate([pieces, jnp.broadcast_to(names[None], (members, SUBS, LANES))], axis=1)
-    sent = jnp.broadcast_to(sent[None], (runs,) + sent.shape).reshape((wide,) + sent.shape[1:])
+    sent = jnp.concatenate(
+        [
+            jnp.broadcast_to(pieces[None], (runs,) + pieces.shape),
+            jnp.broadcast_to(names[None, None], (runs, members) + names.shape),
+        ],
+        axis=2,
+    ).reshape(wide, (tiles + 1) * SUBS, LANES)
     with jax.named_scope("spread_pieces"):
         spread = lax.all_to_all(sent, WIDE, 0, 0, tiled=True)
     owners = spread[:, tiles * SUBS, :neg_count].astype(jnp.int32).reshape(wide * neg_count)
 
     with jax.named_scope("pool_yh"):
-        mine = [passages] + [lax.ppermute(passages, "yh", swaps[k]) for k in range(1, near)]
+        mine = lax.all_gather(passages, "yh", axis=0, tiled=True)
     with jax.named_scope("pool_x"):
-        mine = jnp.concatenate(mine, axis=0)
         slabs = [mine] + [lax.ppermute(mine, "x", swaps[k]) for k in range(1, far)]
-    slots = positive ^ ((here_x * near + here_y) * block_rows)
+    slots = positive ^ (here_x * (near * block_rows))
 
     (picked,) = call(
         pick_kernel,
@@ -233,43 +237,35 @@
     named = named.reshape(members * tiles, neg_count * SUBS, LANES)
 
     product = 2 * query_count * width
-    exps, top, total = call(
+    (exps,) = call(
         pool_kernel,
-        [((query_count, pool_rows), f32), ((query_count, 1), f32), ((query_count, 1), f32)],
+        [((query_count, pool_rows + 2 * LANES + width), f32)],
         [],
-        product * pool_rows,
+        100 * product * pool_rows,
         queries,
         *slabs,
     )
-    named_hi, named_lo, named_grad, share = call(
-        named_kernel,
+    total_rows = pool_rows + named_rows
+    hi, lo, named_grad, *pool_grads = call(
+        grads_kernel,
         [
-            ((query_count, named_rows), bf16),
-            ((query_count, named_rows), bf16),
+            ((query_count, total_rows), bf16),
+            ((query_count, total_rows), bf16),
             ((members * tiles, neg_count * SUBS, LANES), f32),
-            ((query_count, 1), f32),
-        ],
+        ]
+        + [((near * block_rows, width), f32)] * far,
         [pltpu.VMEM((named_rows, width), bf16), pltpu.VMEM((query_count, named_rows), f32)],
-        3 * product * named_rows,
-        queries,
+        2 * product * total_rows,
+        jnp.arange(near, dtype=jnp.int32) ^ here_y.astype(jnp.int32),
         named,
-        top,
-        total,
+        exps,
+        slots[None, :],
+        smem=1,
     )
     with jax.named_scope("named_back"):
         back = named_grad.astype(half).reshape(members, tiles, neg_count, SUBS, LANES)
         back = lax.all_to_all(back, RUN, 0, 0, tiled=True)
 
-    pool_hi, pool_lo, *pool_grads = call(
-        pool_grad_kernel,
-        [((query_count, pool_rows), bf16)] * 2 + [((near * block_rows, width), f32)] * far,
-        [],
-        2 * product * pool_rows,
-        queries,
-        exps,
-        share,
-        slots[None, :],
-    )
     rows_x = pool_grads[0]
     leaving = [grad.astype(half) for grad in pool_grads[1:]]
     with jax.named_scope("grad_x"):
@@ -287,13 +283,12 @@
         query_kernel,
         [((query_count, width), f32)],
         [pltpu.VMEM((named_rows, width), bf16)],
-        30 * product * (pool_rows + named_rows),
-        pool_hi,
-        pool_lo,
-        named_hi,
-        named_lo,
+        8 * product * (pool_rows + named_rows),
+        hi,
+        lo,
         named,
         *slabs,
+        after=(rows_x,),
     )
 
     (summed,) = call(
@@ -305,7 +300,6 @@
         owners,
         back.astype(f32),
         smem=2,
-        after=tuple(pool_grads[1:]),
     )
     with jax.named_scope("pieces_home"):
         home = lax.all_to_all(summed.astype(half), WIDE, 0, 0, tiled=True)

time: 144 us -> 136 us (0.944)
  blocking collectives: 0 us -> 15.6 us
  waiting for transfers between devices: 34.3 us -> 22.8 us
  starting transfers between devices: 80.3 us -> 74.6 us
  local copies, waits for them, and re-layouts: 8.21 us -> 3.93 us
  other arithmetic: 10.6 us -> 9.07 us
    all_gather x0 -> x1, blocking collectives: none -> 15.6 us  [local(): mine = lax.all_gather(passages, 'yh', axis=0, tiled=True)]
    ppermute x3, waiting for transfers between devices: 15.6 us -> 3.23 us  [local(): slabs = [mine] + [lax.ppermute(mine, 'x', swaps[k]) for k in range(1, far)]]
    ppermute x3 -> x0, starting transfers between devices: 11.4 us -> none  [local(): lax.ppermute(passages, 'yh', swaps[k])]
    ppermute x3 -> x0, waiting for transfers between devices: 10.2 us -> none  [local(): lax.ppermute(passages, 'yh', swaps[k])]
    all_to_all x1, waiting for transfers between devices: 0.01 us -> 8.67 us  [local(): named = lax.all_to_all(picked, RUN, 0, 0, tiled=True)]
    all_to_all x1, starting transfers between devices: 3.57 us -> 8.73 us  [local(): named = lax.all_to_all(picked, RUN, 0, 0, tiled=True)]
    unnamed x51 -> x34, local copies, waits for them, and re-layouts: 7.26 us -> 2.87 us
    all_to_all x1, waiting for transfers between devices: 0.01 us -> 3.51 us  [local(): back = lax.all_to_all(back, RUN, 0, 0, tiled=True)]
  transfers between devices with their start and end apart: 16 -> 13, of which waited for: 7 -> 6; matrix products, arithmetic and copies ran while one was open for 5% -> 4% of each run, Pallas kernels for 4% -> 4%
where the time goes in v2:
time: 136 us
  starting transfers between devices  74.6 us (55%)
  waiting for transfers between devices  22.8 us (17%)
  blocking collectives  15.6 us (11%)
  other arithmetic  9.07 us (7%)
  Pallas kernels  8.57 us (6%)
  local copies, waits for them, and re-layouts  3.93 us (3%)
    all_to_all x1, starting transfers between devices, local(): spread = lax.all_to_all(sent, WIDE, 0, 0, tiled=True)  18 us
    all_gather x1, blocking collectives, local(): mine = lax.all_gather(passages, 'yh', axis=0, tiled=True)  15.6 us
    all_to_all x1, starting transfers between devices, local(): home = lax.all_to_all(summed.astype(half), WIDE, 0, 0, tiled=True)  13.1 us
    ppermute x3, starting transfers between devices, local(): part = lax.ppermute(part, 'yh', swaps[k])  11.4 us
    ppermute x3, starting transfers between devices, local(): part = lax.ppermute(leaving[k - 1], 'x', swaps[k])  8.97 us
    ppermute x3, starting transfers between devices, local(): slabs = [mine] + [lax.ppermute(mine, 'x', swaps[k]) for k in range(1, far)]  8.97 us
    all_to_all x1, starting transfers between devices, local(): named = lax.all_to_all(picked, RUN, 0, 0, tiled=True)  8.73 us
    all_to_all x1, waiting for transfers between devices, local(): named = lax.all_to_all(picked, RUN, 0, 0, tiled=True)  8.67 us
  transfers between devices with their start and end apart: 13, of which 6 were waited for; matrix products, arithmetic and copies ran while one was open for 4% of the time, Pallas kernels for 4%

profile of v2, /device:TPU:1, one launch (start us, length us, event | category | flops | bytes accessed | tf_op | source)
XLA Modules:
  0.0 135.5 jit_solution(4372058402561010251)
XLA Ops:
  1.4 0.9 broadcast_in_dim.22
  3.2 18.0 %all-to-all-start = ((bf16[48,40,128]{2,1,0:T(8,128)(2,1)}), bf16[48,40,128]{2,1,0:T(8,128)(2,1)S(1)}, u32[]{:S(2)}, u32[]{:S(2)}) async-start(bf16[48,40,128]{2,1,0:T(8,128)(2,1)} %bitcast.4), calls=%async_computation | async-start | bytes 983040 | tf_op jit(solution)/shard_map/spread_pieces/all_to_all | solution.py:215
  21.2 15.6 %all_gather.3.refs_3_.refs_1_ = bf16[256,768]{1,0:T(8,128)(2,1)S(1)} all-gather(bf16[64,768]{1,0:T(8,128)(2,1)S(1)} %copy-done.15), channel_id=1, replica_groups=mesh['zs'=4,'zl'=3,'yl'=2,'c'=2,'x'=4,'yh'=4] {'yh'}, dimensions={0}, use_global_device_ids=true | all-gather | bytes 491520 | tf_op jit(solution)/shard_map/pool_yh/all_gather | solution.py:219
  36.7 4.4 %collective-permute-start.2 = (bf16[256,768]{1,0:T(8,128)(2,1)S(1)}, bf16[256,768]{1,0:T(8,128)(2,1)S(1)}, u32[]{:S(2)}, u32[]{:S(2)}) collective-permute-start(bf16[256,768]{1,0:T(8,128)(2,1)S(1)} %all_gather.3.refs_3_.refs_1_), channel_id=1, source_target_pairs={{0,12},{4,8},{8,4},{12,0},{1,13},{5,9},{9,5},{13,1},{2,14},{6,10},... | collective-permute-start | bytes 1179656 | tf_op jit(solution)/shard_map/pool_x/ppermute | solution.py:221
  41.1 2.4 %collective-permute-start.1 = (bf16[256,768]{1,0:T(8,128)(2,1)S(1)}, bf16[256,768]{1,0:T(8,128)(2,1)S(1)}, u32[]{:S(2)}, u32[]{:S(2)}) collective-permute-start(bf16[256,768]{1,0:T(8,128)(2,1)S(1)} %all_gather.3.refs_3_.refs_1_), channel_id=1, source_target_pairs={{0,8},{4,12},{8,0},{12,4},{1,9},{5,13},{9,1},{13,5},{2,10},{6,14},... | collective-permute-start | bytes 1179656 | tf_op jit(solution)/shard_map/pool_x/ppermute | solution.py:221
  43.6 2.2 %collective-permute-start = (bf16[256,768]{1,0:T(8,128)(2,1)S(1)}, bf16[256,768]{1,0:T(8,128)(2,1)S(1)}, u32[]{:S(2)}, u32[]{:S(2)}) collective-permute-start(bf16[256,768]{1,0:T(8,128)(2,1)S(1)} %all_gather.3.refs_3_.refs_1_), channel_id=1, source_target_pairs={{0,4},{4,0},{8,12},{12,8},{1,5},{5,1},{9,13},{13,9},{2,6},{6,2},{1... | collective-permute-start | bytes 1179656 | tf_op jit(solution)/shard_map/pool_x/ppermute | solution.py:221
  46.0 1.6 %shard_map.59 = bf16[12,4,8,8,128]{4,3,2,1,0:T(8,128)(2,1)} custom-call(s32[1]{0:T(128)} %bitcast.refs_0_, s32[384]{0:T(512)S(1)} %reshape.74.refs_1_, bf16[240,8,128]{2,1,0:T(8,128)(2,1)S(1)} %bitcast.17, bf16[256,768]{1,0:T(8,128)(2,1)S(1)} %all_gather.3.refs_3_.refs_1_), custom_call_target="tpu_custom_call" | custom-call | bytes 4194304 | tf_op jit(solution)/shard_map/pallas_call | solution.py:178
  47.6 8.7 %all-to-all-start.1 = ((bf16[12,4,8,8,128]{4,3,2,1,0:T(8,128)(2,1)}), bf16[12,4,8,8,128]{4,3,2,1,0:T(8,128)(2,1)S(1)}, u32[]{:S(2)}, u32[]{:S(2)}) async-start(bf16[12,4,8,8,128]{4,3,2,1,0:T(8,128)(2,1)} %shard_map.59), calls=%async_computation.1 | async-start | bytes 1572864 | tf_op jit(solution)/shard_map/named_pieces/all_to_all | solution.py:236
  56.6 3.0 %collective-permute-done.refs_2_.refs_4_ = bf16[256,768]{1,0:T(8,128)(2,1)S(1)} collective-permute-done((bf16[256,768]{1,0:T(8,128)(2,1)S(1)}, bf16[256,768]{1,0:T(8,128)(2,1)S(1)}, u32[]{:S(2)}, u32[]{:S(2)}) %collective-permute-start) | collective-permute-done | bytes 393248 | tf_op jit(solution)/shard_map/pool_x/ppermute | solution.py:221
  59.6 0.9 shard_map.60.refs_2_
  60.5 1.2 copy-done.9
  61.7 8.7 %all-to-all-done.1 = bf16[12,4,8,8,128]{4,3,2,1,0:T(8,128)(2,1)S(1)} async-done(((bf16[12,4,8,8,128]{4,3,2,1,0:T(8,128)(2,1)}), bf16[12,4,8,8,128]{4,3,2,1,0:T(8,128)(2,1)S(1)}, u32[]{:S(2)}, u32[]{:S(2)}) %all-to-all-start.1) | async-done | bytes 786464 | tf_op jit(solution)/shard_map/named_pieces/all_to_all | solution.py:236
  70.4 1.4 %copy-done.10 = f32[192,2048]{1,0:T(8,128)S(1)} copy-done((f32[192,2048]{1,0:T(8,128)S(1)}, f32[192,2048]{1,0:T(8,128)}, u32[]{:S(2)}) %copy-start.10) | copy-done | bytes 1572888
  71.8 2.8 %shard_map.61 = (bf16[192,1536]{1,0:T(8,128)(2,1)S(1)}, bf16[192,1536]{1,0:T(8,128)(2,1)S(1)}, f32[48,64,128]{2,1,0:T(8,128)S(1)}, f32[256,768]{1,0:T(8,128)S(1)...) custom-call(s32[4]{0:T(128)S(1)} %iota_xor_fusion.refs_0_, ...), custom_call_target="tpu_custom_call" | custom-call | flops 905969664 | bytes 4194304 | tf_op jit(solution)/shard_map/pallas_call | solution.py:178
  74.7 1.3 convert_element_type.72
  76.2 5.4 %all-to-all-start.2 = ((f16[12,4,8,8,128]{4,3,2,1,0:T(8,128)(2,1)}), f16[12,4,8,8,128]{4,3,2,1,0:T(8,128)(2,1)}, u32[]{:S(2)}, u32[]{:S(2)}) async-start(f16[12,4,8,8,128]{4,3,2,1,0:T(8,128)(2,1)} %bitcast.21), calls=%async_computation.2 | async-start | bytes 1572864 | tf_op jit(solution)/shard_map/named_back/all_to_all | solution.py:267
  81.6 0.8 convert_element_type.60
  83.3 4.4 %collective-permute-start.5 = (f16[256,768]{1,0:T(8,128)(2,1)}, f16[256,768]{1,0:T(8,128)(2,1)}, u32[]{:S(2)}, u32[]{:S(2)}) collective-permute-start(f16[256,768]{1,0:T(8,128)(2,1)} %convert_element_type.64), channel_id=1, source_target_pairs={{0,12},{4,8},{8,4},{12,0},{1,13},{5,9},{9,5},{13,1},{2,14},{6,10},... | collective-permute-start | bytes 1179656 | tf_op jit(solution)/shard_map/grad_x/ppermute | solution.py:273
  87.7 2.4 %collective-permute-start.4 = (f16[256,768]{1,0:T(8,128)(2,1)S(1)}, f16[256,768]{1,0:T(8,128)(2,1)}, u32[]{:S(2)}, u32[]{:S(2)}) collective-permute-start(f16[256,768]{1,0:T(8,128)(2,1)S(1)} %convert_element_type.62), channel_id=1, source_target_pairs={{0,8},{4,12},{8,0},{12,4},{1,9},{5,13},{9,1},{13,5},{2,10},{6,14},... | collective-permute-start | bytes 1179656 | tf_op jit(solution)/shard_map/grad_x/ppermute | solution.py:273
  90.1 2.2 %collective-permute-start.3 = (f16[256,768]{1,0:T(8,128)(2,1)}, f16[256,768]{1,0:T(8,128)(2,1)}, u32[]{:S(2)}, u32[]{:S(2)}) collective-permute-start(f16[256,768]{1,0:T(8,128)(2,1)} %convert_element_type.60), channel_id=1, source_target_pairs={{0,4},{4,0},{8,12},{12,8},{1,5},{5,1},{9,13},{13,9},{2,6},{6,2},{1... | collective-permute-start | bytes 1179656 | tf_op jit(solution)/shard_map/grad_x/ppermute | solution.py:273
  92.3 3.5 %all-to-all-done.2 = f16[12,4,8,8,128]{4,3,2,1,0:T(8,128)(2,1)} async-done(((f16[12,4,8,8,128]{4,3,2,1,0:T(8,128)(2,1)}), f16[12,4,8,8,128]{4,3,2,1,0:T(8,128)(2,1)}, u32[]{:S(2)}, u32[]{:S(2)}) %all-to-all-start.2) | async-done | bytes 786464 | tf_op jit(solution)/shard_map/named_back/all_to_all | solution.py:267
  95.8 1.3 convert_element_type.73.refs_2_
  97.1 1.2 shard_map.63
  98.3 0.8 convert_element_type.74
  99.1 13.1 %all-to-all-start.3 = ((f16[48,4,8,128]{3,2,1,0:T(8,128)(2,1)}), f16[48,4,8,128]{3,2,1,0:T(8,128)(2,1)S(1)}, u32[]{:S(2)}, u32[]{:S(2)}) async-start(f16[48,4,8,128]{3,2,1,0:T(8,128)(2,1)} %convert_element_type.74), calls=%async_computation.3 | async-start | bytes 786432 | tf_op jit(solution)/shard_map/pieces_home/all_to_all | solution.py:305
  112.3 1.5 %convert_add_fusion.refs_7_ = f32[256,768]{1,0:T(8,128)S(1)} fusion(f16[256,768]{1,0:T(8,128)(2,1)} %collective-permute-done.5, f16[256,768]{1,0:T(8,128)(2,1)} %collective-permute-done.4, f32[256,768]{1,0:T(8,128)S(1)} %copy-done.1, f16[256,768]{1,0:T(8,128)(2,1)} %collective-permute-done.3), kind=kLoop, calls=%fused_computation.1 | loop fusion | flops 1179648 | bytes 2752512 | tf_op jit(solution)/shard_map/grad_x/add | solution.py:274
  113.9 2.0 %collective-permute-start.6 = (f16[64,768]{1,0:T(8,128)(2,1)S(1)}, f16[64,768]{1,0:T(8,128)(2,1)S(1)}, u32[]{:S(2)}, u32[]{:S(2)}) collective-permute-start(f16[64,768]{1,0:T(8,128)(2,1)S(1)} %get-tuple-element.28), channel_id=1, source_target_pairs={{0,1},{1,0},{2,3},{3,2},{4,5},{5,4},{6,7},{7,6},{8,9},{9,8},{10,11... | collective-permute-start | bytes 294920 | tf_op jit(solution)/shard_map/grad_yh/ppermute | solution.py:279
  115.9 5.2 %collective-permute-start.8 = (f16[64,768]{1,0:T(8,128)(2,1)S(1)}, f16[64,768]{1,0:T(8,128)(2,1)S(1)}, u32[]{:S(2)}, u32[]{:S(2)}) collective-permute-start(f16[64,768]{1,0:T(8,128)(2,1)S(1)} %get-tuple-element.29), channel_id=1, source_target_pairs={{0,3},{1,2},{2,1},{3,0},{4,7},{5,6},{6,5},{7,4},{8,11},{9,10},{10,... | collective-permute-start | bytes 294920 | tf_op jit(solution)/shard_map/grad_yh/ppermute | solution.py:279
  121.1 4.2 %collective-permute-start.7 = (f16[64,768]{1,0:T(8,128)(2,1)S(1)}, f16[64,768]{1,0:T(8,128)(2,1)S(1)}, u32[]{:S(2)}, u32[]{:S(2)}) collective-permute-start(f16[64,768]{1,0:T(8,128)(2,1)S(1)} %get-tuple-element.30), channel_id=1, source_target_pairs={{0,2},{1,3},{2,0},{3,1},{4,6},{5,7},{6,4},{7,5},{8,10},{9,11},{10,... | collective-permute-start | bytes 294920 | tf_op jit(solution)/shard_map/grad_yh/ppermute | solution.py:279
  125.4 2.0 %shard_map.62 = f32[192,768]{1,0:T(8,128)} custom-call(bf16[192,1536]{1,0:T(8,128)(2,1)S(1)} %copy-done.12, bf16[192,1536]{1,0:T(8,128)(2,1)S(1)} %copy-done.14, bf16[48,64,128]{2,1,0:T(8,128)(2,1)S(1)} %bitcast.19, bf16[256,768]{1,0:T(8,128)(2,1)S(1)} %all_gather.3.refs_3_.refs_1_, bf16[256,768]{1,0:T(8,128)(2,1)S(1)} %copy-done.7, ...), custom_call_target="tpu_custom_call" | custom-call | flops 3623878656 | bytes 4194304 | tf_op jit(solution)/shard_map/pallas_call | solution.py:178
  127.4 6.1 %all-to-all-done.3 = f16[48,4,8,128]{3,2,1,0:T(8,128)(2,1)S(1)} async-done(((f16[48,4,8,128]{3,2,1,0:T(8,128)(2,1)}), f16[48,4,8,128]{3,2,1,0:T(8,128)(2,1)S(1)}, u32[]{:S(2)}, u32[]{:S(2)}) %all-to-all-start.3) | async-done | bytes 393248 | tf_op jit(solution)/shard_map/pieces_home/all_to_all | solution.py:305
  133.5 1.3 collective-permute-done.7
  (53 shorter events, 3.9 us)
Async XLA Ops:
  0.6 20.5 %copy-start.15 = (bf16[64,768]{1,0:T(8,128)(2,1)S(1)}, bf16[64,768]{1,0:T(8,128)(2,1)}, u32[]{:S(2)}) copy-start(bf16[64,768]{1,0:T(8,128)(2,1)} %param.7) | copy-start | bytes 294916
  0.6 45.1 %copy-start.16 = (s32[192]{0:T(256)S(1)}, s32[192]{0:T(256)}, u32[]{:S(2)}) copy-start(s32[192]{0:T(256)} %param.8) | copy-start | bytes 2308
  3.2 42.6 %all-to-all-start = ((bf16[48,40,128]{2,1,0:T(8,128)(2,1)}), bf16[48,40,128]{2,1,0:T(8,128)(2,1)S(1)}, u32[]{:S(2)}, u32[]{:S(2)}) async-start(bf16[48,40,128]{2,1,0:T(8,128)(2,1)} %bitcast.4), calls=%async_computation | async-start | bytes 983040 | tf_op jit(solution)/shard_map/spread_pieces/all_to_all | solution.py:215
  36.7 19.8 %collective-permute-start.2 = (bf16[256,768]{1,0:T(8,128)(2,1)S(1)}, bf16[256,768]{1,0:T(8,128)(2,1)S(1)}, u32[]{:S(2)}, u32[]{:S(2)}) collective-permute-start(bf16[256,768]{1,0:T(8,128)(2,1)S(1)} %all_gather.3.refs_3_.refs_1_), channel_id=1, source_target_pairs={{0,12},{4,8},{8,4},{12,0},{1,13},{5,9},{9,5},{13,1},{2,14},{6,10},... | collective-permute-start | bytes 1179656 | tf_op jit(solution)/shard_map/pool_x/ppermute | solution.py:221
  41.1 15.4 %collective-permute-start.1 = (bf16[256,768]{1,0:T(8,128)(2,1)S(1)}, bf16[256,768]{1,0:T(8,128)(2,1)S(1)}, u32[]{:S(2)}, u32[]{:S(2)}) collective-permute-start(bf16[256,768]{1,0:T(8,128)(2,1)S(1)} %all_gather.3.refs_3_.refs_1_), channel_id=1, source_target_pairs={{0,8},{4,12},{8,0},{12,4},{1,9},{5,13},{9,1},{13,5},{2,10},{6,14},... | collective-permute-start | bytes 1179656 | tf_op jit(solution)/shard_map/pool_x/ppermute | solution.py:221
  43.6 16.0 %collective-permute-start = (bf16[256,768]{1,0:T(8,128)(2,1)S(1)}, bf16[256,768]{1,0:T(8,128)(2,1)S(1)}, u32[]{:S(2)}, u32[]{:S(2)}) collective-permute-start(bf16[256,768]{1,0:T(8,128)(2,1)S(1)} %all_gather.3.refs_3_.refs_1_), channel_id=1, source_target_pairs={{0,4},{4,0},{8,12},{12,8},{1,5},{5,1},{9,13},{13,9},{2,6},{6,2},{1... | collective-permute-start | bytes 1179656 | tf_op jit(solution)/shard_map/pool_x/ppermute | solution.py:221
  46.0 13.6 %copy-start.8 = (bf16[192,768]{1,0:T(8,128)(2,1)S(1)}, bf16[192,768]{1,0:T(8,128)(2,1)}, u32[]{:S(2)}) copy-start(bf16[192,768]{1,0:T(8,128)(2,1)} %refs_0_.1) | copy-start | bytes 884740
  47.6 22.8 %all-to-all-start.1 = ((bf16[12,4,8,8,128]{4,3,2,1,0:T(8,128)(2,1)}), bf16[12,4,8,8,128]{4,3,2,1,0:T(8,128)(2,1)S(1)}, u32[]{:S(2)}, u32[]{:S(2)}) async-start(bf16[12,4,8,8,128]{4,3,2,1,0:T(8,128)(2,1)} %shard_map.59), calls=%async_computation.1 | async-start | bytes 1572864 | tf_op jit(solution)/shard_map/named_pieces/all_to_all | solution.py:236
  56.5 4.0 %copy-start.2 = (bf16[256,768]{1,0:T(8,128)(2,1)}, bf16[256,768]{1,0:T(8,128)(2,1)S(1)}, u32[]{:S(2)}) copy-start(bf16[256,768]{1,0:T(8,128)(2,1)S(1)} %collective-permute-done.2.refs_4_.refs_6_) | copy-start | bytes 1179652
  56.6 4.0 %copy-start.4 = (bf16[256,768]{1,0:T(8,128)(2,1)}, bf16[256,768]{1,0:T(8,128)(2,1)S(1)}, u32[]{:S(2)}) copy-start(bf16[256,768]{1,0:T(8,128)(2,1)S(1)} %collective-permute-done.1.refs_3_.refs_5_) | copy-start | bytes 1179652
  59.6 0.9 copy-start.6
  60.5 1.2 copy-start.9
  70.4 1.4 %copy-start.10 = (f32[192,2048]{1,0:T(8,128)S(1)}, f32[192,2048]{1,0:T(8,128)}, u32[]{:S(2)}) copy-start(f32[192,2048]{1,0:T(8,128)} %copy-done.9) | copy-start | bytes 4718596
  74.6 1.3 copy-start
  74.7 1.3 copy-start.11
  74.7 1.5 %copy-start.13 = (bf16[192,1536]{1,0:T(8,128)(2,1)}, bf16[192,1536]{1,0:T(8,128)(2,1)S(1)}, u32[]{:S(2)}) copy-start(bf16[192,1536]{1,0:T(8,128)(2,1)S(1)} %get-tuple-element.22.refs_1_) | copy-start | bytes 1769476
  76.2 19.6 %all-to-all-start.2 = ((f16[12,4,8,8,128]{4,3,2,1,0:T(8,128)(2,1)}), f16[12,4,8,8,128]{4,3,2,1,0:T(8,128)(2,1)}, u32[]{:S(2)}, u32[]{:S(2)}) async-start(f16[12,4,8,8,128]{4,3,2,1,0:T(8,128)(2,1)} %bitcast.21), calls=%async_computation.2 | async-start | bytes 1572864 | tf_op jit(solution)/shard_map/named_back/all_to_all | solution.py:267
  83.3 28.9 %collective-permute-start.5 = (f16[256,768]{1,0:T(8,128)(2,1)}, f16[256,768]{1,0:T(8,128)(2,1)}, u32[]{:S(2)}, u32[]{:S(2)}) collective-permute-start(f16[256,768]{1,0:T(8,128)(2,1)} %convert_element_type.64), channel_id=1, source_target_pairs={{0,12},{4,8},{8,4},{12,0},{1,13},{5,9},{9,5},{13,1},{2,14},{6,10},... | collective-permute-start | bytes 1179656 | tf_op jit(solution)/shard_map/grad_x/ppermute | solution.py:273
  87.7 24.6 %collective-permute-start.4 = (f16[256,768]{1,0:T(8,128)(2,1)S(1)}, f16[256,768]{1,0:T(8,128)(2,1)}, u32[]{:S(2)}, u32[]{:S(2)}) collective-permute-start(f16[256,768]{1,0:T(8,128)(2,1)S(1)} %convert_element_type.62), channel_id=1, source_target_pairs={{0,8},{4,12},{8,0},{12,4},{1,9},{5,13},{9,1},{13,5},{2,10},{6,14},... | collective-permute-start | bytes 1179656 | tf_op jit(solution)/shard_map/grad_x/ppermute | solution.py:273
  90.1 22.2 %collective-permute-start.3 = (f16[256,768]{1,0:T(8,128)(2,1)}, f16[256,768]{1,0:T(8,128)(2,1)}, u32[]{:S(2)}, u32[]{:S(2)}) collective-permute-start(f16[256,768]{1,0:T(8,128)(2,1)} %convert_element_type.60), channel_id=1, source_target_pairs={{0,4},{4,0},{8,12},{12,8},{1,5},{5,1},{9,13},{13,9},{2,6},{6,2},{1... | collective-permute-start | bytes 1179656 | tf_op jit(solution)/shard_map/grad_x/ppermute | solution.py:273
  98.3 14.0 %copy-start.1 = (f32[256,768]{1,0:T(8,128)S(1)}, f32[256,768]{1,0:T(8,128)}, u32[]{:S(2)}) copy-start(f32[256,768]{1,0:T(8,128)} %copy-done) | copy-start | bytes 2359300
  99.1 34.3 %all-to-all-start.3 = ((f16[48,4,8,128]{3,2,1,0:T(8,128)(2,1)}), f16[48,4,8,128]{3,2,1,0:T(8,128)(2,1)S(1)}, u32[]{:S(2)}, u32[]{:S(2)}) async-start(f16[48,4,8,128]{3,2,1,0:T(8,128)(2,1)} %convert_element_type.74), calls=%async_computation.3 | async-start | bytes 786432 | tf_op jit(solution)/shard_map/pieces_home/all_to_all | solution.py:305
  112.3 13.1 %copy-start.3 = (bf16[256,768]{1,0:T(8,128)(2,1)S(1)}, bf16[256,768]{1,0:T(8,128)(2,1)}, u32[]{:S(2)}) copy-start(bf16[256,768]{1,0:T(8,128)(2,1)} %copy-done.2) | copy-start | bytes 1179652
  112.3 13.1 %copy-start.5 = (bf16[256,768]{1,0:T(8,128)(2,1)S(1)}, bf16[256,768]{1,0:T(8,128)(2,1)}, u32[]{:S(2)}) copy-start(bf16[256,768]{1,0:T(8,128)(2,1)} %copy-done.4) | copy-start | bytes 1179652
  112.3 13.1 %copy-start.7 = (bf16[256,768]{1,0:T(8,128)(2,1)S(1)}, bf16[256,768]{1,0:T(8,128)(2,1)}, u32[]{:S(2)}) copy-start(bf16[256,768]{1,0:T(8,128)(2,1)} %copy-done.6) | copy-start | bytes 1179652
  112.3 13.1 %copy-start.12 = (bf16[192,1536]{1,0:T(8,128)(2,1)S(1)}, bf16[192,1536]{1,0:T(8,128)(2,1)}, u32[]{:S(2)}) copy-start(bf16[192,1536]{1,0:T(8,128)(2,1)} %copy-done.11) | copy-start | bytes 1769476
  112.3 13.1 %copy-start.14 = (bf16[192,1536]{1,0:T(8,128)(2,1)S(1)}, bf16[192,1536]{1,0:T(8,128)(2,1)}, u32[]{:S(2)}) copy-start(bf16[192,1536]{1,0:T(8,128)(2,1)} %copy-done.13) | copy-start | bytes 1769476
  113.9 19.6 %collective-permute-start.6 = (f16[64,768]{1,0:T(8,128)(2,1)S(1)}, f16[64,768]{1,0:T(8,128)(2,1)S(1)}, u32[]{:S(2)}, u32[]{:S(2)}) collective-permute-start(f16[64,768]{1,0:T(8,128)(2,1)S(1)} %get-tuple-element.28), channel_id=1, source_target_pairs={{0,1},{1,0},{2,3},{3,2},{4,5},{5,4},{6,7},{7,6},{8,9},{9,8},{10,11... | collective-permute-start | bytes 294920 | tf_op jit(solution)/shard_map/grad_yh/ppermute | solution.py:279
  115.9 17.6 %collective-permute-start.8 = (f16[64,768]{1,0:T(8,128)(2,1)S(1)}, f16[64,768]{1,0:T(8,128)(2,1)S(1)}, u32[]{:S(2)}, u32[]{:S(2)}) collective-permute-start(f16[64,768]{1,0:T(8,128)(2,1)S(1)} %get-tuple-element.29), channel_id=1, source_target_pairs={{0,3},{1,2},{2,1},{3,0},{4,7},{5,6},{6,5},{7,4},{8,11},{9,10},{10,... | collective-permute-start | bytes 294920 | tf_op jit(solution)/shard_map/grad_yh/ppermute | solution.py:279
  121.1 13.7 %collective-permute-start.7 = (f16[64,768]{1,0:T(8,128)(2,1)S(1)}, f16[64,768]{1,0:T(8,128)(2,1)S(1)}, u32[]{:S(2)}, u32[]{:S(2)}) collective-permute-start(f16[64,768]{1,0:T(8,128)(2,1)S(1)} %get-tuple-element.30), channel_id=1, source_target_pairs={{0,2},{1,3},{2,0},{3,1},{4,6},{5,7},{6,4},{7,5},{8,10},{9,11},{10,... | collective-permute-start | bytes 294920 | tf_op jit(solution)/shard_map/grad_yh/ppermute | solution.py:279

commit v3 on v1

--- a/solution.py
+++ b/solution.py
@@ -16,7 +16,7 @@
 SUBS = 8
 LIFT = 128.0
 DROP = 1.0 / 16.0
-VMEM = 12 * 1024 * 1024
+VMEM = 16 * 1024 * 1024
 STEP = 256
 
 
@@ -43,14 +43,12 @@
     members, tiles, count = out_ref.shape[:3]
     stride = held_ref.shape[0] // (owners_ref.shape[0] // count)
 
-    def body(i, carry):
+    first = run_ref[0] * members
+    for i in range(members):
         for k in range(count):
-            owner = owners_ref[(run_ref[0] * members + i) * count + k]
+            owner = owners_ref[(first + i) * count + k]
             for u in range(tiles):
                 out_ref[i, u, k] = held_ref[owner * stride + u]
-        return carry
-
-    lax.fori_loop(0, members, body, 0)
 
 
 def gather_sum_kernel(run_ref, owners_ref, terms_ref, out_ref, *acc_refs):
@@ -71,7 +69,7 @@
 
 
 def pool_kernel(q_ref, *refs):
-    slab_refs, (exp_ref, top_ref, sum_ref) = refs[:-3], refs[-3:]
+    slab_refs, (exp_ref, stat_ref) = refs[:-2], refs[-2:]
     width = q_ref.shape[1]
     step = slab_refs[0].shape[0]
     scaling = 4.0 / math.sqrt(width)
@@ -87,8 +85,9 @@
         part = jnp.exp(exp_ref[:, slot * step : (slot + 1) * step] - top)
         exp_ref[:, slot * step : (slot + 1) * step] = part
         total += jnp.sum(part, axis=-1, keepdims=True)
-    top_ref[...] = top
-    sum_ref[...] = total
+    stat_ref[:, :LANES] = jnp.broadcast_to(top, (q.shape[0], LANES))
+    stat_ref[:, LANES : 2 * LANES] = jnp.broadcast_to(total, (q.shape[0], LANES))
+    stat_ref[:, 2 * LANES :] = q.astype(jnp.float32)
 
 
 def split(grad):
@@ -96,29 +95,29 @@
     return hi, (grad - hi.astype(jnp.float32)).astype(jnp.bfloat16)
 
 
-def named_kernel(q_ref, named_ref, top_ref, sum_ref, hi_ref, lo_ref, grad_ref, share_ref, keys_ref, l_ref):
-    width = q_ref.shape[1]
+def named_kernel(named_ref, stat_ref, hi_ref, lo_ref, named_out, share_ref, keys_ref, l_ref):
+    width = keys_ref.shape[1]
     col_tiles = width // LANES
     row_tiles = named_ref.shape[0] // col_tiles
     piece_rows = named_ref.shape[1]
     named_rows = row_tiles * piece_rows
     scaling = 4.0 / math.sqrt(width)
     join_pieces(named_ref, keys_ref, row_tiles, col_tiles)
-    q = q_ref[...]
-    pool_top = top_ref[...]
+    q = stat_ref[:, 2 * LANES :].astype(jnp.bfloat16)
+    pool_top = stat_ref[:, :1]
     top = pool_top
     for c in range(0, named_rows, STEP):
         part = dot_nt(q, keys_ref[c : c + STEP, :]) * scaling
         l_ref[:, c : c + STEP] = part
         top = jnp.maximum(top, jnp.max(part, axis=-1, keepdims=True))
     pool_scale = jnp.exp(pool_top - top)
-    total = sum_ref[...] * pool_scale
+    total = stat_ref[:, LANES : LANES + 1] * pool_scale
     for c in range(0, named_rows, STEP):
         part = jnp.exp(l_ref[:, c : c + STEP] - top)
         l_ref[:, c : c + STEP] = part
         total += jnp.sum(part, axis=-1, keepdims=True)
     share = 1.0 / total
-    share_ref[...] = share * pool_scale
+    share_ref[...] = jnp.broadcast_to(share * pool_scale, share_ref.shape)
     for c in range(0, named_rows, STEP):
         hi, lo = split(l_ref[:, c : c + STEP] * share)
         hi_ref[:, c : c + STEP] = hi
@@ -127,28 +126,31 @@
         first = c // piece_rows
         for r in range(STEP // piece_rows):
             for k in range(col_tiles):
-                grad_ref[(first + r) * col_tiles + k] = terms[
+                named_out[(first + r) * col_tiles + k] = terms[
                     r * piece_rows : (r + 1) * piece_rows, k * LANES : (k + 1) * LANES
                 ]
 
 
-def pool_grad_kernel(q_ref, exp_ref, share_ref, pos_ref, hi_ref, lo_ref, *grad_refs):
+def pool_grad_kernel(place_ref, q_ref, exp_ref, share_ref, pos_ref, hi_ref, lo_ref, *grad_refs):
     queries, width = q_ref.shape
+    step = grad_refs[0].shape[0]
     scaling = 4.0 / math.sqrt(width)
     q = q_ref[...]
-    share = share_ref[...]
+    share = share_ref[:, :1]
     across = lax.broadcasted_iota(jnp.int32, (queries, queries), 1)
     down = lax.broadcasted_iota(jnp.int32, (queries, queries), 0)
     pos = jnp.sum(jnp.where(across == down, pos_ref[...].astype(jnp.float32), 0.0), axis=1, keepdims=True)
     pos = pos.astype(jnp.int32)
-    step = grad_refs[0].shape[0]
+    block = step // place_ref.shape[0]
     for slot, grad_ref in enumerate(grad_refs):
         first, last = slot * step, (slot + 1) * step
         columns = lax.broadcasted_iota(jnp.int32, (queries, step), 1) + first
         hi, lo = split(exp_ref[:, first:last] * share - (columns == pos).astype(jnp.float32))
         hi_ref[:, first:last] = hi
         lo_ref[:, first:last] = lo
-        grad_ref[...] = (dot_tn(hi, q) + dot_tn(lo, q)) * (scaling * LIFT)
+        terms = (dot_tn(hi, q) + dot_tn(lo, q)) * (scaling * LIFT)
+        for r in range(step // block):
+            grad_ref[pl.ds(pl.multiple_of(place_ref[r] * block, block), block), :] = terms[r * block : (r + 1) * block]
 
 
 def query_kernel(pool_hi_ref, pool_lo_ref, hi_ref, lo_ref, named_ref, *refs):
@@ -203,19 +205,22 @@
 
     pieces = passages.reshape(row_tiles, SUBS, col_tiles, LANES).transpose(0, 2, 1, 3)
     pieces = pieces.reshape(members, tiles * SUBS, LANES)
-    names = jnp.zeros((SUBS, LANES), bf16).at[0, :neg_count].set(negative_owners[0].astype(bf16))
-    sent = jnp.concatenate([pieces, jnp.broadcast_to(names[None], (members, SUBS, LANES))], axis=1)
-    sent = jnp.broadcast_to(sent[None], (runs,) + sent.shape).reshape((wide,) + sent.shape[1:])
+    names = jnp.pad(negative_owners[0].astype(bf16), (0, LANES - neg_count))
+    rows = tiles * SUBS
+    shape = (runs, members, rows + SUBS, LANES)
+    row = lax.broadcasted_iota(jnp.int32, shape, 2)
+    sent = jnp.pad(pieces, ((0, 0), (0, SUBS), (0, 0)))
+    sent = jnp.where(row < rows, jnp.broadcast_to(sent[None], shape), jnp.broadcast_to(names, shape))
+    sent = sent.reshape(wide, rows + SUBS, LANES)
     with jax.named_scope("spread_pieces"):
         spread = lax.all_to_all(sent, WIDE, 0, 0, tiled=True)
     owners = spread[:, tiles * SUBS, :neg_count].astype(jnp.int32).reshape(wide * neg_count)
 
     with jax.named_scope("pool_yh"):
-        mine = [passages] + [lax.ppermute(passages, "yh", swaps[k]) for k in range(1, near)]
+        mine = lax.all_gather(passages, "yh", axis=0, tiled=True)
     with jax.named_scope("pool_x"):
-        mine = jnp.concatenate(mine, axis=0)
         slabs = [mine] + [lax.ppermute(mine, "x", swaps[k]) for k in range(1, far)]
-    slots = positive ^ ((here_x * near + here_y) * block_rows)
+    slots = positive ^ (here_x * (near * block_rows))
 
     (picked,) = call(
         pick_kernel,
@@ -233,11 +238,11 @@
     named = named.reshape(members * tiles, neg_count * SUBS, LANES)
 
     product = 2 * query_count * width
-    exps, top, total = call(
+    exps, stats = call(
         pool_kernel,
-        [((query_count, pool_rows), f32), ((query_count, 1), f32), ((query_count, 1), f32)],
+        [((query_count, pool_rows), f32), ((query_count, 2 * LANES + width), f32)],
         [],
-        product * pool_rows,
+        100 * product * pool_rows,
         queries,
         *slabs,
     )
@@ -247,14 +252,12 @@
             ((query_count, named_rows), bf16),
             ((query_count, named_rows), bf16),
             ((members * tiles, neg_count * SUBS, LANES), f32),
-            ((query_count, 1), f32),
+            ((query_count, LANES), f32),
         ],
         [pltpu.VMEM((named_rows, width), bf16), pltpu.VMEM((query_count, named_rows), f32)],
         3 * product * named_rows,
-        queries,
         named,
-        top,
-        total,
+        stats,
     )
     with jax.named_scope("named_back"):
         back = named_grad.astype(half).reshape(members, tiles, neg_count, SUBS, LANES)
@@ -265,10 +268,12 @@
         [((query_count, pool_rows), bf16)] * 2 + [((near * block_rows, width), f32)] * far,
         [],
         2 * product * pool_rows,
+        jnp.arange(near, dtype=jnp.int32) ^ here_y.astype(jnp.int32),
         queries,
         exps,
         share,
         slots[None, :],
+        smem=1,
     )
     rows_x = pool_grads[0]
     leaving = [grad.astype(half) for grad in pool_grads[1:]]
@@ -278,7 +283,7 @@
             rows_x = rows_x + part.astype(f32)
     owned = rows_x[:block_rows]
     with jax.named_scope("grad_yh"):
-        for k in range(1, near):
+        for k in (2, 1, 3):
             part = (rows_x[k * block_rows : (k + 1) * block_rows] * (1.0 / far)).astype(half)
             part = lax.ppermute(part, "yh", swaps[k])
             owned = owned + part.astype(f32) * float(far)
@@ -287,13 +292,14 @@
         query_kernel,
         [((query_count, width), f32)],
         [pltpu.VMEM((named_rows, width), bf16)],
-        30 * product * (pool_rows + named_rows),
+        8 * product * (pool_rows + named_rows),
         pool_hi,
         pool_lo,
         named_hi,
         named_lo,
         named,
         *slabs,
+        after=(rows_x,),
     )
 
     (summed,) = call(
@@ -305,7 +311,6 @@
         owners,
         back.astype(f32),
         smem=2,
-        after=tuple(pool_grads[1:]),
     )
     with jax.named_scope("pieces_home"):
         home = lax.all_to_all(summed.astype(half), WIDE, 0, 0, tiled=True)

time: 144 us -> 134 us (0.931)
  waiting for transfers between devices: 34.3 us -> 17.9 us
  blocking collectives: 0 us -> 15.6 us
  starting transfers between devices: 80.3 us -> 74.7 us
  local copies, waits for them, and re-layouts: 8.21 us -> 5.16 us
    all_gather x0 -> x1, blocking collectives: none -> 15.6 us  [local(): mine = lax.all_gather(passages, 'yh', axis=0, tiled=True)]
    ppermute x3, waiting for transfers between devices: 15.6 us -> 3.27 us  [local(): slabs = [mine] + [lax.ppermute(mine, 'x', swaps[k]) for k in range(1, far)]]
    ppermute x3 -> x0, starting transfers between devices: 11.4 us -> none  [local(): lax.ppermute(passages, 'yh', swaps[k])]
    ppermute x3 -> x0, waiting for transfers between devices: 10.2 us -> none  [local(): lax.ppermute(passages, 'yh', swaps[k])]
    all_to_all x1, waiting for transfers between devices: 0.01 us -> 8.02 us  [local(): named = lax.all_to_all(picked, RUN, 0, 0, tiled=True)]
    all_to_all x1, starting transfers between devices: 3.57 us -> 8.73 us  [local(): named = lax.all_to_all(picked, RUN, 0, 0, tiled=True)]
    unnamed x51 -> x36, local copies, waits for them, and re-layouts: 7.26 us -> 4.16 us
    all_to_all x1, waiting for transfers between devices: 2.52 us -> 0.01 us  [local(): spread = lax.all_to_all(sent, WIDE, 0, 0, tiled=True)]
  transfers between devices with their start and end apart: 16 -> 13, of which waited for: 7 -> 5; matrix products, arithmetic and copies ran while one was open for 5% -> 5% of each run, Pallas kernels for 4% -> 6%
where the time goes in v3:
time: 134 us; the launch traced here: 133 us
  starting transfers between devices  74.7 us (56%)
  waiting for transfers between devices  17.9 us (13%)
  blocking collectives  15.6 us (12%)
  other arithmetic  10 us (7%)
  Pallas kernels  8.93 us (7%)
  local copies, waits for them, and re-layouts  5.16 us (4%)
    all_to_all x1, starting transfers between devices, local(): spread = lax.all_to_all(sent, WIDE, 0, 0, tiled=True)  18 us
    all_gather x1, blocking collectives, local(): mine = lax.all_gather(passages, 'yh', axis=0, tiled=True)  15.6 us
    all_to_all x1, starting transfers between devices, local(): home = lax.all_to_all(summed.astype(half), WIDE, 0, 0, tiled=True)  13.2 us
    ppermute x3, starting transfers between devices, local(): part = lax.ppermute(part, 'yh', swaps[k])  11.4 us
    ppermute x3, starting transfers between devices, local(): part = lax.ppermute(leaving[k - 1], 'x', swaps[k])  8.97 us
    ppermute x3, starting transfers between devices, local(): slabs = [mine] + [lax.ppermute(mine, 'x', swaps[k]) for k in range(1, far)]  8.97 us
    pallas_call x6, Pallas kernels, call(): pl.pallas_call(body, out_shape=tuple((jax.ShapeDtypeStruct(shape, dtype)...  8.93 us
    all_to_all x1, starting transfers between devices, local(): named = lax.all_to_all(picked, RUN, 0, 0, tiled=True)  8.73 us
  transfers between devices with their start and end apart: 13, of which 5 were waited for; matrix products, arithmetic and copies ran while one was open for 5% of the time, Pallas kernels for 6%

profile of v3, /device:TPU:1, one launch (start us, length us, event | category | flops | bytes accessed | tf_op | source)
XLA Modules:
  0.0 133.3 jit_solution(2949208654249915063)
XLA Ops:
  1.4 0.9 pad.8
  3.1 18.0 %all-to-all-start = ((bf16[48,40,128]{2,1,0:T(8,128)(2,1)}), bf16[48,40,128]{2,1,0:T(8,128)(2,1)S(1)}, u32[]{:S(2)}, u32[]{:S(2)}) async-start(bf16[48,40,128]{2,1,0:T(8,128)(2,1)} %bitcast_select_fusion), calls=%async_computation | async-start | bytes 983040 | tf_op jit(solution)/shard_map/spread_pieces/all_to_all | solution.py:216
  21.2 15.6 %all_gather.3.refs_1_.refs_3_.refs_5_ = bf16[256,768]{1,0:T(8,128)(2,1)S(1)} all-gather(bf16[64,768]{1,0:T(8,128)(2,1)S(1)} %copy-done.16), channel_id=1, replica_groups=mesh['zs'=4,'zl'=3,'yl'=2,'c'=2,'x'=4,'yh'=4] {'yh'}, dimensions={0}, use_global_device_ids=true | all-gather | bytes 491520 | tf_op jit(solution)/shard_map/pool_yh/all_gather | solution.py:220
  36.7 4.4 %collective-permute-start.2 = (bf16[256,768]{1,0:T(8,128)(2,1)S(1)}, bf16[256,768]{1,0:T(8,128)(2,1)S(1)}, u32[]{:S(2)}, u32[]{:S(2)}) collective-permute-start(bf16[256,768]{1,0:T(8,128)(2,1)S(1)} %all_gather.3.refs_1_.refs_3_.refs_5_), channel_id=1, source_target_pairs={{0,12},{4,8},{8,4},{12,0},{1,13},{5,9},{9,5},{13,1},{2,14},{6,10},... | collective-permute-start | bytes 1179656 | tf_op jit(solution)/shard_map/pool_x/ppermute | solution.py:222
  41.1 2.4 %collective-permute-start.1 = (bf16[256,768]{1,0:T(8,128)(2,1)S(1)}, bf16[256,768]{1,0:T(8,128)(2,1)S(1)}, u32[]{:S(2)}, u32[]{:S(2)}) collective-permute-start(bf16[256,768]{1,0:T(8,128)(2,1)S(1)} %all_gather.3.refs_1_.refs_3_.refs_5_), channel_id=1, source_target_pairs={{0,8},{4,12},{8,0},{12,4},{1,9},{5,13},{9,1},{13,5},{2,10},{6,14},... | collective-permute-start | bytes 1179656 | tf_op jit(solution)/shard_map/pool_x/ppermute | solution.py:222
  43.5 2.2 %collective-permute-start = (bf16[256,768]{1,0:T(8,128)(2,1)S(1)}, bf16[256,768]{1,0:T(8,128)(2,1)S(1)}, u32[]{:S(2)}, u32[]{:S(2)}) collective-permute-start(bf16[256,768]{1,0:T(8,128)(2,1)S(1)} %all_gather.3.refs_1_.refs_3_.refs_5_), channel_id=1, source_target_pairs={{0,4},{4,0},{8,12},{12,8},{1,5},{5,1},{9,13},{13,9},{2,6},{6,2},{1... | collective-permute-start | bytes 1179656 | tf_op jit(solution)/shard_map/pool_x/ppermute | solution.py:222
  45.9 1.7 %shard_map.60 = bf16[12,4,8,8,128]{4,3,2,1,0:T(8,128)(2,1)} custom-call(s32[1]{0:T(128)} %bitcast.refs_0_, s32[384]{0:T(512)S(1)} %reshape.43.refs_1_, bf16[240,8,128]{2,1,0:T(8,128)(2,1)S(1)} %bitcast.20, bf16[256,768]{1,0:T(8,128)(2,1)S(1)} %all_gather.3.refs_1_.refs_3_.refs_5_), custom_call_target="tpu_custom_call" | custom-call | bytes 4194304 | tf_op jit(solution)/shard_map/pallas_call | solution.py:180
  47.6 8.7 %all-to-all-start.1 = ((bf16[12,4,8,8,128]{4,3,2,1,0:T(8,128)(2,1)}), bf16[12,4,8,8,128]{4,3,2,1,0:T(8,128)(2,1)S(1)}, u32[]{:S(2)}, u32[]{:S(2)}) async-start(bf16[12,4,8,8,128]{4,3,2,1,0:T(8,128)(2,1)} %shard_map.60), calls=%async_computation.1 | async-start | bytes 1572864 | tf_op jit(solution)/shard_map/named_pieces/all_to_all | solution.py:237
  56.5 3.0 %collective-permute-done.refs_2_.refs_6_ = bf16[256,768]{1,0:T(8,128)(2,1)S(1)} collective-permute-done((bf16[256,768]{1,0:T(8,128)(2,1)S(1)}, bf16[256,768]{1,0:T(8,128)(2,1)S(1)}, u32[]{:S(2)}, u32[]{:S(2)}) %collective-permute-start) | collective-permute-done | bytes 393248 | tf_op jit(solution)/shard_map/pool_x/ppermute | solution.py:222
  60.5 0.9 copy-done.4
  61.4 0.9 copy-done.10
  62.3 8.0 %all-to-all-done.1 = bf16[12,4,8,8,128]{4,3,2,1,0:T(8,128)(2,1)S(1)} async-done(((bf16[12,4,8,8,128]{4,3,2,1,0:T(8,128)(2,1)}), bf16[12,4,8,8,128]{4,3,2,1,0:T(8,128)(2,1)S(1)}, u32[]{:S(2)}, u32[]{:S(2)}) %all-to-all-start.1) | async-done | bytes 786464 | tf_op jit(solution)/shard_map/named_pieces/all_to_all | solution.py:237
  70.4 1.1 copy-done.5
  71.5 1.4 %shard_map.61 = (bf16[192,512]{1,0:T(8,128)(2,1)S(1)}, bf16[192,512]{1,0:T(8,128)(2,1)S(1)}, f32[48,64,128]{2,1,0:T(8,128)S(1)}, f32[192,128]{1,0:T(8,128)S(1)}) custom-call(bf16[48,64,128]{2,1,0:T(8,128)(2,1)S(1)} %bitcast.21, f32[192,1024]{1,0:T(8,128)S(1)} %copy-done.5), custom_call_target="tpu_custom_call" | custom-call | flops 452984832 | bytes 4194304 | tf_op jit(solution)/shard_map/pallas_call | solution.py:180
  72.9 1.1 convert_element_type.79
  74.0 5.4 %all-to-all-start.2 = ((f16[12,4,8,8,128]{4,3,2,1,0:T(8,128)(2,1)}), f16[12,4,8,8,128]{4,3,2,1,0:T(8,128)(2,1)}, u32[]{:S(2)}, u32[]{:S(2)}) async-start(f16[12,4,8,8,128]{4,3,2,1,0:T(8,128)(2,1)} %bitcast.9), calls=%async_computation.2 | async-start | bytes 1572864 | tf_op jit(solution)/shard_map/named_back/all_to_all | solution.py:264
  79.5 1.1 copy-done.11
  80.6 1.8 %shard_map.62 = (bf16[192,1024]{1,0:T(8,128)(2,1)S(1)}, bf16[192,1024]{1,0:T(8,128)(2,1)S(1)}, f32[256,768]{1,0:T(8,128)S(1)}, f32[256,768]{1,0:T(8,128)S(1)}, f...) custom-call(s32[4]{0:T(128)S(1)} %iota_xor_fusion.refs_0_, bf16[192,768]{1,0:T(8,128)(2,1)S(1)} %copy-done.3, ...), custom_call_target="tpu_custom_call" | custom-call | flops 603979776 | bytes 4194304 | tf_op jit(solution)/shard_map/pallas_call | solution.py:180
  82.5 0.9 convert_element_type.69
  84.2 4.4 %collective-permute-start.5 = (f16[256,768]{1,0:T(8,128)(2,1)}, f16[256,768]{1,0:T(8,128)(2,1)}, u32[]{:S(2)}, u32[]{:S(2)}) collective-permute-start(f16[256,768]{1,0:T(8,128)(2,1)} %convert_element_type.71), channel_id=1, source_target_pairs={{0,12},{4,8},{8,4},{12,0},{1,13},{5,9},{9,5},{13,1},{2,14},{6,10},... | collective-permute-start | bytes 1179656 | tf_op jit(solution)/shard_map/grad_x/ppermute | solution.py:282
  88.6 2.4 %collective-permute-start.4 = (f16[256,768]{1,0:T(8,128)(2,1)}, f16[256,768]{1,0:T(8,128)(2,1)}, u32[]{:S(2)}, u32[]{:S(2)}) collective-permute-start(f16[256,768]{1,0:T(8,128)(2,1)} %convert_element_type.69), channel_id=1, source_target_pairs={{0,8},{4,12},{8,0},{12,4},{1,9},{5,13},{9,1},{13,5},{2,10},{6,14},... | collective-permute-start | bytes 1179656 | tf_op jit(solution)/shard_map/grad_x/ppermute | solution.py:282
  91.0 2.2 %collective-permute-start.3 = (f16[256,768]{1,0:T(8,128)(2,1)S(1)}, f16[256,768]{1,0:T(8,128)(2,1)}, u32[]{:S(2)}, u32[]{:S(2)}) collective-permute-start(f16[256,768]{1,0:T(8,128)(2,1)S(1)} %convert_element_type.67), channel_id=1, source_target_pairs={{0,4},{4,0},{8,12},{12,8},{1,5},{5,1},{9,13},{13,9},{2,6},{6,2},{1... | collective-permute-start | bytes 1179656 | tf_op jit(solution)/shard_map/grad_x/ppermute | solution.py:282
  93.7 1.3 convert_element_type.80.refs_2_
  94.9 1.2 shard_map.64
  97.0 13.2 %all-to-all-start.3 = ((f16[48,4,8,128]{3,2,1,0:T(8,128)(2,1)}), f16[48,4,8,128]{3,2,1,0:T(8,128)(2,1)}, u32[]{:S(2)}, u32[]{:S(2)}) async-start(f16[48,4,8,128]{3,2,1,0:T(8,128)(2,1)} %convert_element_type.81), calls=%async_computation.3 | async-start | bytes 786432 | tf_op jit(solution)/shard_map/pieces_home/all_to_all | solution.py:316
  110.3 1.5 %convert_add_fusion.refs_9_ = f32[256,768]{1,0:T(8,128)S(1)} fusion(f16[256,768]{1,0:T(8,128)(2,1)} %collective-permute-done.5, f16[256,768]{1,0:T(8,128)(2,1)} %collective-permute-done.4, f32[256,768]{1,0:T(8,128)S(1)} %get-tuple-element.21, f16[256,768]{1,0:T(8,128)(2,1)} %collective-permute-done.3), kind=kLoop, calls=%fused_computation.1 | loop fusion | flops 1179648 | bytes 2752512 | tf_op jit(solution)/shard_map/grad_x/add | solution.py:283
  111.9 4.9 %collective-permute-start.6 = (f16[64,768]{1,0:T(8,128)(2,1)S(1)}, f16[64,768]{1,0:T(8,128)(2,1)S(1)}, u32[]{:S(2)}, u32[]{:S(2)}) collective-permute-start(f16[64,768]{1,0:T(8,128)(2,1)S(1)} %get-tuple-element.26), channel_id=1, source_target_pairs={{0,2},{1,3},{2,0},{3,1},{4,6},{5,7},{6,4},{7,5},{8,10},{9,11},{10,... | collective-permute-start | bytes 294920 | tf_op jit(solution)/shard_map/grad_yh/ppermute | solution.py:288
  116.8 3.7 %collective-permute-start.8 = (f16[64,768]{1,0:T(8,128)(2,1)S(1)}, f16[64,768]{1,0:T(8,128)(2,1)S(1)}, u32[]{:S(2)}, u32[]{:S(2)}) collective-permute-start(f16[64,768]{1,0:T(8,128)(2,1)S(1)} %get-tuple-element.27), channel_id=1, source_target_pairs={{0,3},{1,2},{2,1},{3,0},{4,7},{5,6},{6,5},{7,4},{8,11},{9,10},{10,... | collective-permute-start | bytes 294920 | tf_op jit(solution)/shard_map/grad_yh/ppermute | solution.py:288
  120.5 2.8 %collective-permute-start.7 = (f16[64,768]{1,0:T(8,128)(2,1)S(1)}, f16[64,768]{1,0:T(8,128)(2,1)S(1)}, u32[]{:S(2)}, u32[]{:S(2)}) collective-permute-start(f16[64,768]{1,0:T(8,128)(2,1)S(1)} %get-tuple-element.28), channel_id=1, source_target_pairs={{0,1},{1,0},{2,3},{3,2},{4,5},{5,4},{6,7},{7,6},{8,9},{9,8},{10,11... | collective-permute-start | bytes 294920 | tf_op jit(solution)/shard_map/grad_yh/ppermute | solution.py:288
  123.3 2.0 %shard_map.63 = f32[192,768]{1,0:T(8,128)} custom-call(bf16[192,1024]{1,0:T(8,128)(2,1)S(1)} %copy-done.13, bf16[192,1024]{1,0:T(8,128)(2,1)S(1)} %copy-done.15, bf16[192,512]{1,0:T(8,128)(2,1)S(1)} %copy-done.7, bf16[192,512]{1,0:T(8,128)(2,1)S(1)} %copy-done.9, bf16[48,64,128]{2,1,0:T(8,128)(2,1)S(1)} %bitcast.22, ...), custom_call_target="tpu_custom_call" | custom-call | flops 3623878656 | bytes 4194304 | tf_op jit(solution)/shard_map/pallas_call | solution.py:180
  125.3 6.1 %all-to-all-done.3 = f16[48,4,8,128]{3,2,1,0:T(8,128)(2,1)} async-done(((f16[48,4,8,128]{3,2,1,0:T(8,128)(2,1)}), f16[48,4,8,128]{3,2,1,0:T(8,128)(2,1)}, u32[]{:S(2)}, u32[]{:S(2)}) %all-to-all-start.3) | async-done | bytes 393248 | tf_op jit(solution)/shard_map/pieces_home/all_to_all | solution.py:316
  131.4 1.1 convert_reduce_fusion
  (56 shorter events, 5.9 us)
Async XLA Ops:
  0.6 20.5 %copy-start.16 = (bf16[64,768]{1,0:T(8,128)(2,1)S(1)}, bf16[64,768]{1,0:T(8,128)(2,1)}, u32[]{:S(2)}) copy-start(bf16[64,768]{1,0:T(8,128)(2,1)} %param.5) | copy-start | bytes 294916
  3.1 42.6 %all-to-all-start = ((bf16[48,40,128]{2,1,0:T(8,128)(2,1)}), bf16[48,40,128]{2,1,0:T(8,128)(2,1)S(1)}, u32[]{:S(2)}, u32[]{:S(2)}) async-start(bf16[48,40,128]{2,1,0:T(8,128)(2,1)} %bitcast_select_fusion), calls=%async_computation | async-start | bytes 983040 | tf_op jit(solution)/shard_map/spread_pieces/all_to_all | solution.py:216
  36.7 19.8 %collective-permute-start.2 = (bf16[256,768]{1,0:T(8,128)(2,1)S(1)}, bf16[256,768]{1,0:T(8,128)(2,1)S(1)}, u32[]{:S(2)}, u32[]{:S(2)}) collective-permute-start(bf16[256,768]{1,0:T(8,128)(2,1)S(1)} %all_gather.3.refs_1_.refs_3_.refs_5_), channel_id=1, source_target_pairs={{0,12},{4,8},{8,4},{12,0},{1,13},{5,9},{9,5},{13,1},{2,14},{6,10},... | collective-permute-start | bytes 1179656 | tf_op jit(solution)/shard_map/pool_x/ppermute | solution.py:222
  41.1 15.4 %collective-permute-start.1 = (bf16[256,768]{1,0:T(8,128)(2,1)S(1)}, bf16[256,768]{1,0:T(8,128)(2,1)S(1)}, u32[]{:S(2)}, u32[]{:S(2)}) collective-permute-start(bf16[256,768]{1,0:T(8,128)(2,1)S(1)} %all_gather.3.refs_1_.refs_3_.refs_5_), channel_id=1, source_target_pairs={{0,8},{4,12},{8,0},{12,4},{1,9},{5,13},{9,1},{13,5},{2,10},{6,14},... | collective-permute-start | bytes 1179656 | tf_op jit(solution)/shard_map/pool_x/ppermute | solution.py:222
  43.5 16.0 %collective-permute-start = (bf16[256,768]{1,0:T(8,128)(2,1)S(1)}, bf16[256,768]{1,0:T(8,128)(2,1)S(1)}, u32[]{:S(2)}, u32[]{:S(2)}) collective-permute-start(bf16[256,768]{1,0:T(8,128)(2,1)S(1)} %all_gather.3.refs_1_.refs_3_.refs_5_), channel_id=1, source_target_pairs={{0,4},{4,0},{8,12},{12,8},{1,5},{5,1},{9,13},{13,9},{2,6},{6,2},{1... | collective-permute-start | bytes 1179656 | tf_op jit(solution)/shard_map/pool_x/ppermute | solution.py:222
  45.9 13.7 %copy-start.2 = (bf16[192,768]{1,0:T(8,128)(2,1)S(1)}, bf16[192,768]{1,0:T(8,128)(2,1)}, u32[]{:S(2)}) copy-start(bf16[192,768]{1,0:T(8,128)(2,1)} %refs_1_.1) | copy-start | bytes 884740
  47.6 22.8 %all-to-all-start.1 = ((bf16[12,4,8,8,128]{4,3,2,1,0:T(8,128)(2,1)}), bf16[12,4,8,8,128]{4,3,2,1,0:T(8,128)(2,1)S(1)}, u32[]{:S(2)}, u32[]{:S(2)}) async-start(bf16[12,4,8,8,128]{4,3,2,1,0:T(8,128)(2,1)} %shard_map.60), calls=%async_computation.1 | async-start | bytes 1572864 | tf_op jit(solution)/shard_map/named_pieces/all_to_all | solution.py:237
  59.6 0.9 copy-start
  60.5 0.9 copy-start.4
  61.4 0.9 copy-start.10
  70.4 1.1 copy-start.5
  72.9 1.2 copy-start.8
  72.9 1.1 copy-start.6
  72.9 6.6 %copy-start.17 = (s32[192]{0:T(256)S(1)}, s32[192]{0:T(256)}, u32[]{:S(2)}) copy-start(s32[192]{0:T(256)} %param.6) | copy-start | bytes 2308
  72.9 6.6 %copy-start.3 = (bf16[192,768]{1,0:T(8,128)(2,1)S(1)}, bf16[192,768]{1,0:T(8,128)(2,1)}, u32[]{:S(2)}) copy-start(bf16[192,768]{1,0:T(8,128)(2,1)} %refs_1_.1) | copy-start | bytes 884740
  74.0 19.6 %all-to-all-start.2 = ((f16[12,4,8,8,128]{4,3,2,1,0:T(8,128)(2,1)}), f16[12,4,8,8,128]{4,3,2,1,0:T(8,128)(2,1)}, u32[]{:S(2)}, u32[]{:S(2)}) async-start(f16[12,4,8,8,128]{4,3,2,1,0:T(8,128)(2,1)} %bitcast.9), calls=%async_computation.2 | async-start | bytes 1572864 | tf_op jit(solution)/shard_map/named_back/all_to_all | solution.py:264
  79.5 1.1 copy-start.11
  82.4 1.8 %copy-start.12 = (bf16[192,1024]{1,0:T(8,128)(2,1)}, bf16[192,1024]{1,0:T(8,128)(2,1)S(1)}, u32[]{:S(2)}) copy-start(bf16[192,1024]{1,0:T(8,128)(2,1)S(1)} %get-tuple-element.17.refs_0_) | copy-start | bytes 1179652
  82.4 1.8 %copy-start.14 = (bf16[192,1024]{1,0:T(8,128)(2,1)}, bf16[192,1024]{1,0:T(8,128)(2,1)S(1)}, u32[]{:S(2)}) copy-start(bf16[192,1024]{1,0:T(8,128)(2,1)S(1)} %get-tuple-element.18.refs_1_) | copy-start | bytes 1179652
  84.2 26.0 %collective-permute-start.5 = (f16[256,768]{1,0:T(8,128)(2,1)}, f16[256,768]{1,0:T(8,128)(2,1)}, u32[]{:S(2)}, u32[]{:S(2)}) collective-permute-start(f16[256,768]{1,0:T(8,128)(2,1)} %convert_element_type.71), channel_id=1, source_target_pairs={{0,12},{4,8},{8,4},{12,0},{1,13},{5,9},{9,5},{13,1},{2,14},{6,10},... | collective-permute-start | bytes 1179656 | tf_op jit(solution)/shard_map/grad_x/ppermute | solution.py:282
  88.6 21.6 %collective-permute-start.4 = (f16[256,768]{1,0:T(8,128)(2,1)}, f16[256,768]{1,0:T(8,128)(2,1)}, u32[]{:S(2)}, u32[]{:S(2)}) collective-permute-start(f16[256,768]{1,0:T(8,128)(2,1)} %convert_element_type.69), channel_id=1, source_target_pairs={{0,8},{4,12},{8,0},{12,4},{1,9},{5,13},{9,1},{13,5},{2,10},{6,14},... | collective-permute-start | bytes 1179656 | tf_op jit(solution)/shard_map/grad_x/ppermute | solution.py:282
  91.0 19.2 %collective-permute-start.3 = (f16[256,768]{1,0:T(8,128)(2,1)S(1)}, f16[256,768]{1,0:T(8,128)(2,1)}, u32[]{:S(2)}, u32[]{:S(2)}) collective-permute-start(f16[256,768]{1,0:T(8,128)(2,1)S(1)} %convert_element_type.67), channel_id=1, source_target_pairs={{0,4},{4,0},{8,12},{12,8},{1,5},{5,1},{9,13},{13,9},{2,6},{6,2},{1... | collective-permute-start | bytes 1179656 | tf_op jit(solution)/shard_map/grad_x/ppermute | solution.py:282
  97.0 34.4 %all-to-all-start.3 = ((f16[48,4,8,128]{3,2,1,0:T(8,128)(2,1)}), f16[48,4,8,128]{3,2,1,0:T(8,128)(2,1)}, u32[]{:S(2)}, u32[]{:S(2)}) async-start(f16[48,4,8,128]{3,2,1,0:T(8,128)(2,1)} %convert_element_type.81), calls=%async_computation.3 | async-start | bytes 786432 | tf_op jit(solution)/shard_map/pieces_home/all_to_all | solution.py:316
  110.2 13.0 %copy-start.1 = (bf16[256,768]{1,0:T(8,128)(2,1)S(1)}, bf16[256,768]{1,0:T(8,128)(2,1)}, u32[]{:S(2)}) copy-start(bf16[256,768]{1,0:T(8,128)(2,1)} %copy-done) | copy-start | bytes 1179652
  110.3 13.0 %copy-start.7 = (bf16[192,512]{1,0:T(8,128)(2,1)S(1)}, bf16[192,512]{1,0:T(8,128)(2,1)}, u32[]{:S(2)}) copy-start(bf16[192,512]{1,0:T(8,128)(2,1)} %copy-done.6) | copy-start | bytes 589828
  110.3 13.0 %copy-start.9 = (bf16[192,512]{1,0:T(8,128)(2,1)S(1)}, bf16[192,512]{1,0:T(8,128)(2,1)}, u32[]{:S(2)}) copy-start(bf16[192,512]{1,0:T(8,128)(2,1)} %copy-done.8) | copy-start | bytes 589828
  110.3 13.0 %copy-start.13 = (bf16[192,1024]{1,0:T(8,128)(2,1)S(1)}, bf16[192,1024]{1,0:T(8,128)(2,1)}, u32[]{:S(2)}) copy-start(bf16[192,1024]{1,0:T(8,128)(2,1)} %copy-done.12) | copy-start | bytes 1179652
  110.3 13.0 %copy-start.15 = (bf16[192,1024]{1,0:T(8,128)(2,1)S(1)}, bf16[192,1024]{1,0:T(8,128)(2,1)}, u32[]{:S(2)}) copy-start(bf16[192,1024]{1,0:T(8,128)(2,1)} %copy-done.14) | copy-start | bytes 1179652
  111.9 20.6 %collective-permute-start.6 = (f16[64,768]{1,0:T(8,128)(2,1)S(1)}, f16[64,768]{1,0:T(8,128)(2,1)S(1)}, u32[]{:S(2)}, u32[]{:S(2)}) collective-permute-start(f16[64,768]{1,0:T(8,128)(2,1)S(1)} %get-tuple-element.26), channel_id=1, source_target_pairs={{0,2},{1,3},{2,0},{3,1},{4,6},{5,7},{6,4},{7,5},{8,10},{9,11},{10,... | collective-permute-start | bytes 294920 | tf_op jit(solution)/shard_map/grad_yh/ppermute | solution.py:288
  116.8 15.7 %collective-permute-start.8 = (f16[64,768]{1,0:T(8,128)(2,1)S(1)}, f16[64,768]{1,0:T(8,128)(2,1)S(1)}, u32[]{:S(2)}, u32[]{:S(2)}) collective-permute-start(f16[64,768]{1,0:T(8,128)(2,1)S(1)} %get-tuple-element.27), channel_id=1, source_target_pairs={{0,3},{1,2},{2,1},{3,0},{4,7},{5,6},{6,5},{7,4},{8,11},{9,10},{10,... | collective-permute-start | bytes 294920 | tf_op jit(solution)/shard_map/grad_yh/ppermute | solution.py:288
  120.5 12.0 %collective-permute-start.7 = (f16[64,768]{1,0:T(8,128)(2,1)S(1)}, f16[64,768]{1,0:T(8,128)(2,1)S(1)}, u32[]{:S(2)}, u32[]{:S(2)}) collective-permute-start(f16[64,768]{1,0:T(8,128)(2,1)S(1)} %get-tuple-element.28), channel_id=1, source_target_pairs={{0,1},{1,0},{2,3},{3,2},{4,5},{5,4},{6,7},{7,6},{8,9},{9,8},{10,11... | collective-permute-start | bytes 294920 | tf_op jit(solution)/shard_map/grad_yh/ppermute | solution.py:288

commit v4 on v3

--- a/solution.py
+++ b/solution.py
@@ -314,8 +314,11 @@
     )
     with jax.named_scope("pieces_home"):
         home = lax.all_to_all(summed.astype(half), WIDE, 0, 0, tiled=True)
-    home = home.astype(f32).reshape(runs, row_tiles, col_tiles, SUBS, LANES)
-    returned = home.sum(0).transpose(0, 2, 1, 3).reshape(block_rows, width)
+    home = home.reshape(runs, row_tiles, col_tiles, SUBS, LANES).transpose(0, 1, 3, 2, 4)
+    home = home.reshape(runs * block_rows, width)
+    returned = home[:block_rows].astype(f32)
+    for r in range(1, runs):
+        returned = returned + home[r * block_rows : (r + 1) * block_rows].astype(f32)
     return (query_grad, owned * (1.0 / LIFT) + returned * (1.0 / (LIFT * DROP)))
 
 

time: 134 us -> 134 us (level)
    all_to_all x1, waiting for transfers between devices: 6.1 us -> 1.94 us  [local(): home = lax.all_to_all(summed.astype(half), WIDE, 0, 0, tiled=True)]
    ppermute x3, waiting for transfers between devices: 0.01 us -> 4.17 us  [local(): part = lax.ppermute(part, 'yh', swaps[k])]
  transfers between devices with their start and end apart: 13 -> 13, of which waited for: 5 -> 7; matrix products, arithmetic and copies ran while one was open for 5% -> 4% of each run, Pallas kernels for 6% -> 6%
where the time goes in v4:
time: 134 us; the launch traced here: 133 us
  starting transfers between devices  74.7 us (56%)
  waiting for transfers between devices  17.9 us (13%)
  blocking collectives  15.6 us (12%)
  other arithmetic  9.97 us (7%)
  Pallas kernels  8.9 us (7%)
  local copies, waits for them, and re-layouts  5.11 us (4%)
    all_to_all x1, starting transfers between devices, local(): spread = lax.all_to_all(sent, WIDE, 0, 0, tiled=True)  18 us
    all_gather x1, blocking collectives, local(): mine = lax.all_gather(passages, 'yh', axis=0, tiled=True)  15.6 us
    all_to_all x1, starting transfers between devices, local(): home = lax.all_to_all(summed.astype(half), WIDE, 0, 0, tiled=True)  13.2 us
    ppermute x3, starting transfers between devices, local(): part = lax.ppermute(part, 'yh', swaps[k])  11.4 us
    ppermute x3, starting transfers between devices, local(): part = lax.ppermute(leaving[k - 1], 'x', swaps[k])  8.97 us
    ppermute x3, starting transfers between devices, local(): slabs = [mine] + [lax.ppermute(mine, 'x', swaps[k]) for k in range(1, far)]  8.97 us
    pallas_call x6, Pallas kernels, call(): pl.pallas_call(body, out_shape=tuple((jax.ShapeDtypeStruct(shape, dtype)...  8.9 us
    all_to_all x1, starting transfers between devices, local(): named = lax.all_to_all(picked, RUN, 0, 0, tiled=True)  8.73 us
  transfers between devices with their start and end apart: 13, of which 7 were waited for; matrix products, arithmetic and copies ran while one was open for 4% of the time, Pallas kernels for 6%

profile of v4, /device:TPU:1, one launch (start us, length us, event | category | flops | bytes accessed | tf_op | source)
XLA Modules:
  0.0 133.2 jit_solution(12545149195237728141)
XLA Ops:
  1.4 0.9 pad.8
  3.1 18.0 %all-to-all-start = ((bf16[48,40,128]{2,1,0:T(8,128)(2,1)}), bf16[48,40,128]{2,1,0:T(8,128)(2,1)S(1)}, u32[]{:S(2)}, u32[]{:S(2)}) async-start(bf16[48,40,128]{2,1,0:T(8,128)(2,1)} %bitcast_select_fusion), calls=%async_computation | async-start | bytes 983040 | tf_op jit(solution)/shard_map/spread_pieces/all_to_all | solution.py:216
  21.2 15.6 %all_gather.3.refs_1_.refs_3_.refs_5_ = bf16[256,768]{1,0:T(8,128)(2,1)S(1)} all-gather(bf16[64,768]{1,0:T(8,128)(2,1)S(1)} %copy-done.16), channel_id=1, replica_groups=mesh['zs'=4,'zl'=3,'yl'=2,'c'=2,'x'=4,'yh'=4] {'yh'}, dimensions={0}, use_global_device_ids=true | all-gather | bytes 491520 | tf_op jit(solution)/shard_map/pool_yh/all_gather | solution.py:220
  36.7 4.4 %collective-permute-start.2 = (bf16[256,768]{1,0:T(8,128)(2,1)S(1)}, bf16[256,768]{1,0:T(8,128)(2,1)S(1)}, u32[]{:S(2)}, u32[]{:S(2)}) collective-permute-start(bf16[256,768]{1,0:T(8,128)(2,1)S(1)} %all_gather.3.refs_1_.refs_3_.refs_5_), channel_id=1, source_target_pairs={{0,12},{4,8},{8,4},{12,0},{1,13},{5,9},{9,5},{13,1},{2,14},{6,10},... | collective-permute-start | bytes 1179656 | tf_op jit(solution)/shard_map/pool_x/ppermute | solution.py:222
  41.1 2.4 %collective-permute-start.1 = (bf16[256,768]{1,0:T(8,128)(2,1)S(1)}, bf16[256,768]{1,0:T(8,128)(2,1)S(1)}, u32[]{:S(2)}, u32[]{:S(2)}) collective-permute-start(bf16[256,768]{1,0:T(8,128)(2,1)S(1)} %all_gather.3.refs_1_.refs_3_.refs_5_), channel_id=1, source_target_pairs={{0,8},{4,12},{8,0},{12,4},{1,9},{5,13},{9,1},{13,5},{2,10},{6,14},... | collective-permute-start | bytes 1179656 | tf_op jit(solution)/shard_map/pool_x/ppermute | solution.py:222
  43.5 2.2 %collective-permute-start = (bf16[256,768]{1,0:T(8,128)(2,1)S(1)}, bf16[256,768]{1,0:T(8,128)(2,1)S(1)}, u32[]{:S(2)}, u32[]{:S(2)}) collective-permute-start(bf16[256,768]{1,0:T(8,128)(2,1)S(1)} %all_gather.3.refs_1_.refs_3_.refs_5_), channel_id=1, source_target_pairs={{0,4},{4,0},{8,12},{12,8},{1,5},{5,1},{9,13},{13,9},{2,6},{6,2},{1... | collective-permute-start | bytes 1179656 | tf_op jit(solution)/shard_map/pool_x/ppermute | solution.py:222
  45.9 1.6 %shard_map.60 = bf16[12,4,8,8,128]{4,3,2,1,0:T(8,128)(2,1)} custom-call(s32[1]{0:T(128)} %bitcast.refs_0_, s32[384]{0:T(512)S(1)} %reshape.48.refs_1_, bf16[240,8,128]{2,1,0:T(8,128)(2,1)S(1)} %bitcast.19, bf16[256,768]{1,0:T(8,128)(2,1)S(1)} %all_gather.3.refs_1_.refs_3_.refs_5_), custom_call_target="tpu_custom_call" | custom-call | bytes 4194304 | tf_op jit(solution)/shard_map/pallas_call | solution.py:180
  47.6 8.7 %all-to-all-start.1 = ((bf16[12,4,8,8,128]{4,3,2,1,0:T(8,128)(2,1)}), bf16[12,4,8,8,128]{4,3,2,1,0:T(8,128)(2,1)S(1)}, u32[]{:S(2)}, u32[]{:S(2)}) async-start(bf16[12,4,8,8,128]{4,3,2,1,0:T(8,128)(2,1)} %shard_map.60), calls=%async_computation.1 | async-start | bytes 1572864 | tf_op jit(solution)/shard_map/named_pieces/all_to_all | solution.py:237
  56.5 3.0 %collective-permute-done.refs_2_.refs_6_ = bf16[256,768]{1,0:T(8,128)(2,1)S(1)} collective-permute-done((bf16[256,768]{1,0:T(8,128)(2,1)S(1)}, bf16[256,768]{1,0:T(8,128)(2,1)S(1)}, u32[]{:S(2)}, u32[]{:S(2)}) %collective-permute-start) | collective-permute-done | bytes 393248 | tf_op jit(solution)/shard_map/pool_x/ppermute | solution.py:222
  62.3 8.1 %all-to-all-done.1 = bf16[12,4,8,8,128]{4,3,2,1,0:T(8,128)(2,1)S(1)} async-done(((bf16[12,4,8,8,128]{4,3,2,1,0:T(8,128)(2,1)}), bf16[12,4,8,8,128]{4,3,2,1,0:T(8,128)(2,1)S(1)}, u32[]{:S(2)}, u32[]{:S(2)}) %all-to-all-start.1) | async-done | bytes 786464 | tf_op jit(solution)/shard_map/named_pieces/all_to_all | solution.py:237
  70.3 1.1 copy-done.5
  71.5 1.4 %shard_map.61 = (bf16[192,512]{1,0:T(8,128)(2,1)S(1)}, bf16[192,512]{1,0:T(8,128)(2,1)S(1)}, f32[48,64,128]{2,1,0:T(8,128)S(1)}, f32[192,128]{1,0:T(8,128)S(1)}) custom-call(bf16[48,64,128]{2,1,0:T(8,128)(2,1)S(1)} %bitcast.20, f32[192,1024]{1,0:T(8,128)S(1)} %copy-done.5), custom_call_target="tpu_custom_call" | custom-call | flops 452984832 | bytes 4194304 | tf_op jit(solution)/shard_map/pallas_call | solution.py:180
  72.9 1.1 convert_element_type.94
  74.0 5.4 %all-to-all-start.2 = ((f16[12,4,8,8,128]{4,3,2,1,0:T(8,128)(2,1)}), f16[12,4,8,8,128]{4,3,2,1,0:T(8,128)(2,1)}, u32[]{:S(2)}, u32[]{:S(2)}) async-start(f16[12,4,8,8,128]{4,3,2,1,0:T(8,128)(2,1)} %bitcast.9), calls=%async_computation.2 | async-start | bytes 1572864 | tf_op jit(solution)/shard_map/named_back/all_to_all | solution.py:264
  79.5 1.1 copy-done.11
  80.6 1.8 %shard_map.62 = (bf16[192,1024]{1,0:T(8,128)(2,1)S(1)}, bf16[192,1024]{1,0:T(8,128)(2,1)S(1)}, f32[256,768]{1,0:T(8,128)S(1)}, f32[256,768]{1,0:T(8,128)S(1)}, f...) custom-call(s32[4]{0:T(128)S(1)} %iota_xor_fusion.refs_0_, bf16[192,768]{1,0:T(8,128)(2,1)S(1)} %copy-done.3, ...), custom_call_target="tpu_custom_call" | custom-call | flops 603979776 | bytes 4194304 | tf_op jit(solution)/shard_map/pallas_call | solution.py:180
  82.5 0.9 convert_element_type.84
  84.2 4.4 %collective-permute-start.5 = (f16[256,768]{1,0:T(8,128)(2,1)}, f16[256,768]{1,0:T(8,128)(2,1)}, u32[]{:S(2)}, u32[]{:S(2)}) collective-permute-start(f16[256,768]{1,0:T(8,128)(2,1)} %convert_element_type.86), channel_id=1, source_target_pairs={{0,12},{4,8},{8,4},{12,0},{1,13},{5,9},{9,5},{13,1},{2,14},{6,10},... | collective-permute-start | bytes 1179656 | tf_op jit(solution)/shard_map/grad_x/ppermute | solution.py:282
  88.6 2.4 %collective-permute-start.4 = (f16[256,768]{1,0:T(8,128)(2,1)}, f16[256,768]{1,0:T(8,128)(2,1)}, u32[]{:S(2)}, u32[]{:S(2)}) collective-permute-start(f16[256,768]{1,0:T(8,128)(2,1)} %convert_element_type.84), channel_id=1, source_target_pairs={{0,8},{4,12},{8,0},{12,4},{1,9},{5,13},{9,1},{13,5},{2,10},{6,14},... | collective-permute-start | bytes 1179656 | tf_op jit(solution)/shard_map/grad_x/ppermute | solution.py:282
  91.0 2.2 %collective-permute-start.3 = (f16[256,768]{1,0:T(8,128)(2,1)S(1)}, f16[256,768]{1,0:T(8,128)(2,1)}, u32[]{:S(2)}, u32[]{:S(2)}) collective-permute-start(f16[256,768]{1,0:T(8,128)(2,1)S(1)} %convert_element_type.82), channel_id=1, source_target_pairs={{0,4},{4,0},{8,12},{12,8},{1,5},{5,1},{9,13},{13,9},{2,6},{6,2},{1... | collective-permute-start | bytes 1179656 | tf_op jit(solution)/shard_map/grad_x/ppermute | solution.py:282
  93.6 1.3 convert_element_type.95.refs_2_
  94.9 1.2 shard_map.64
  96.9 13.2 %all-to-all-start.3 = ((f16[48,4,8,128]{3,2,1,0:T(8,128)(2,1)}), f16[48,4,8,128]{3,2,1,0:T(8,128)(2,1)}, u32[]{:S(2)}, u32[]{:S(2)}) async-start(f16[48,4,8,128]{3,2,1,0:T(8,128)(2,1)} %convert_element_type.96), calls=%async_computation.3 | async-start | bytes 786432 | tf_op jit(solution)/shard_map/pieces_home/all_to_all | solution.py:316
  110.2 1.5 %convert_add_fusion.refs_9_ = f32[256,768]{1,0:T(8,128)S(1)} fusion(f16[256,768]{1,0:T(8,128)(2,1)} %collective-permute-done.5, f16[256,768]{1,0:T(8,128)(2,1)} %collective-permute-done.4, f32[256,768]{1,0:T(8,128)S(1)} %get-tuple-element.21, f16[256,768]{1,0:T(8,128)(2,1)} %collective-permute-done.3), kind=kLoop, calls=%fused_computation | loop fusion | flops 1179648 | bytes 2752512 | tf_op jit(solution)/shard_map/grad_x/add | solution.py:283
  111.8 4.9 %collective-permute-start.6 = (f16[64,768]{1,0:T(8,128)(2,1)S(1)}, f16[64,768]{1,0:T(8,128)(2,1)S(1)}, u32[]{:S(2)}, u32[]{:S(2)}) collective-permute-start(f16[64,768]{1,0:T(8,128)(2,1)S(1)} %get-tuple-element.26), channel_id=1, source_target_pairs={{0,2},{1,3},{2,0},{3,1},{4,6},{5,7},{6,4},{7,5},{8,10},{9,11},{10,... | collective-permute-start | bytes 294920 | tf_op jit(solution)/shard_map/grad_yh/ppermute | solution.py:288
  116.7 3.7 %collective-permute-start.8 = (f16[64,768]{1,0:T(8,128)(2,1)S(1)}, f16[64,768]{1,0:T(8,128)(2,1)S(1)}, u32[]{:S(2)}, u32[]{:S(2)}) collective-permute-start(f16[64,768]{1,0:T(8,128)(2,1)S(1)} %get-tuple-element.27), channel_id=1, source_target_pairs={{0,3},{1,2},{2,1},{3,0},{4,7},{5,6},{6,5},{7,4},{8,11},{9,10},{10,... | collective-permute-start | bytes 294920 | tf_op jit(solution)/shard_map/grad_yh/ppermute | solution.py:288
  120.5 2.7 %collective-permute-start.7 = (f16[64,768]{1,0:T(8,128)(2,1)S(1)}, f16[64,768]{1,0:T(8,128)(2,1)S(1)}, u32[]{:S(2)}, u32[]{:S(2)}) collective-permute-start(f16[64,768]{1,0:T(8,128)(2,1)S(1)} %get-tuple-element.28), channel_id=1, source_target_pairs={{0,1},{1,0},{2,3},{3,2},{4,5},{5,4},{6,7},{7,6},{8,9},{9,8},{10,11... | collective-permute-start | bytes 294920 | tf_op jit(solution)/shard_map/grad_yh/ppermute | solution.py:288
  123.3 2.0 %shard_map.63 = f32[192,768]{1,0:T(8,128)} custom-call(bf16[192,1024]{1,0:T(8,128)(2,1)S(1)} %copy-done.13, bf16[192,1024]{1,0:T(8,128)(2,1)S(1)} %copy-done.15, bf16[192,512]{1,0:T(8,128)(2,1)S(1)} %copy-done.7, bf16[192,512]{1,0:T(8,128)(2,1)S(1)} %copy-done.9, bf16[48,64,128]{2,1,0:T(8,128)(2,1)S(1)} %bitcast.21, ...), custom_call_target="tpu_custom_call" | custom-call | flops 3623878656 | bytes 4194304 | tf_op jit(solution)/shard_map/pallas_call | solution.py:180
  125.2 3.0 %collective-permute-done.8 = f16[64,768]{1,0:T(8,128)(2,1)S(1)} collective-permute-done((f16[64,768]{1,0:T(8,128)(2,1)S(1)}, f16[64,768]{1,0:T(8,128)(2,1)S(1)}, u32[]{:S(2)}, u32[]{:S(2)}) %collective-permute-start.8) | collective-permute-done | bytes 98336 | tf_op jit(solution)/shard_map/grad_yh/ppermute | solution.py:288
  128.3 1.1 collective-permute-done.7
  129.4 1.9 %all-to-all-done.3 = f16[48,4,8,128]{3,2,1,0:T(8,128)(2,1)} async-done(((f16[48,4,8,128]{3,2,1,0:T(8,128)(2,1)}), f16[48,4,8,128]{3,2,1,0:T(8,128)(2,1)}, u32[]{:S(2)}, u32[]{:S(2)}) %all-to-all-start.3) | async-done | bytes 393248 | tf_op jit(solution)/shard_map/pieces_home/all_to_all | solution.py:316
  131.4 1.8 %fusion.6 = f32[64,768]{1,0:T(8,128)} fusion(f32[256,768]{1,0:T(8,128)S(1)} %convert_add_fusion.refs_9_, f16[64,768]{1,0:T(8,128)(2,1)S(1)} %collective-permute-done.8, f16[64,768]{1,0:T(8,128)(2,1)S(1)} %collective-permute-done.7, f16[64,768]{1,0:T(8,128)(2,1)S(1)} %collective-permute-done.6, f16[4,8,8,6,128]{4,2,3,1,0:T(8,128)(2,1)} %bitcast.11), kind=kLoop, calls=%fused_computation.12 | loop fusion | flops 933888 | bytes 1081344 | tf_op jit(solution)/shard_map/add | solution.py:322
  (55 shorter events, 6.9 us)
Async XLA Ops:
  0.6 20.5 %copy-start.16 = (bf16[64,768]{1,0:T(8,128)(2,1)S(1)}, bf16[64,768]{1,0:T(8,128)(2,1)}, u32[]{:S(2)}) copy-start(bf16[64,768]{1,0:T(8,128)(2,1)} %param.5) | copy-start | bytes 294916
  3.1 42.6 %all-to-all-start = ((bf16[48,40,128]{2,1,0:T(8,128)(2,1)}), bf16[48,40,128]{2,1,0:T(8,128)(2,1)S(1)}, u32[]{:S(2)}, u32[]{:S(2)}) async-start(bf16[48,40,128]{2,1,0:T(8,128)(2,1)} %bitcast_select_fusion), calls=%async_computation | async-start | bytes 983040 | tf_op jit(solution)/shard_map/spread_pieces/all_to_all | solution.py:216
  36.7 19.8 %collective-permute-start.2 = (bf16[256,768]{1,0:T(8,128)(2,1)S(1)}, bf16[256,768]{1,0:T(8,128)(2,1)S(1)}, u32[]{:S(2)}, u32[]{:S(2)}) collective-permute-start(bf16[256,768]{1,0:T(8,128)(2,1)S(1)} %all_gather.3.refs_1_.refs_3_.refs_5_), channel_id=1, source_target_pairs={{0,12},{4,8},{8,4},{12,0},{1,13},{5,9},{9,5},{13,1},{2,14},{6,10},... | collective-permute-start | bytes 1179656 | tf_op jit(solution)/shard_map/pool_x/ppermute | solution.py:222
  41.1 15.4 %collective-permute-start.1 = (bf16[256,768]{1,0:T(8,128)(2,1)S(1)}, bf16[256,768]{1,0:T(8,128)(2,1)S(1)}, u32[]{:S(2)}, u32[]{:S(2)}) collective-permute-start(bf16[256,768]{1,0:T(8,128)(2,1)S(1)} %all_gather.3.refs_1_.refs_3_.refs_5_), channel_id=1, source_target_pairs={{0,8},{4,12},{8,0},{12,4},{1,9},{5,13},{9,1},{13,5},{2,10},{6,14},... | collective-permute-start | bytes 1179656 | tf_op jit(solution)/shard_map/pool_x/ppermute | solution.py:222
  43.5 16.0 %collective-permute-start = (bf16[256,768]{1,0:T(8,128)(2,1)S(1)}, bf16[256,768]{1,0:T(8,128)(2,1)S(1)}, u32[]{:S(2)}, u32[]{:S(2)}) collective-permute-start(bf16[256,768]{1,0:T(8,128)(2,1)S(1)} %all_gather.3.refs_1_.refs_3_.refs_5_), channel_id=1, source_target_pairs={{0,4},{4,0},{8,12},{12,8},{1,5},{5,1},{9,13},{13,9},{2,6},{6,2},{1... | collective-permute-start | bytes 1179656 | tf_op jit(solution)/shard_map/pool_x/ppermute | solution.py:222
  45.9 13.7 %copy-start.2 = (bf16[192,768]{1,0:T(8,128)(2,1)S(1)}, bf16[192,768]{1,0:T(8,128)(2,1)}, u32[]{:S(2)}) copy-start(bf16[192,768]{1,0:T(8,128)(2,1)} %refs_1_.1) | copy-start | bytes 884740
  47.6 22.8 %all-to-all-start.1 = ((bf16[12,4,8,8,128]{4,3,2,1,0:T(8,128)(2,1)}), bf16[12,4,8,8,128]{4,3,2,1,0:T(8,128)(2,1)S(1)}, u32[]{:S(2)}, u32[]{:S(2)}) async-start(bf16[12,4,8,8,128]{4,3,2,1,0:T(8,128)(2,1)} %shard_map.60), calls=%async_computation.1 | async-start | bytes 1572864 | tf_op jit(solution)/shard_map/named_pieces/all_to_all | solution.py:237
  59.6 0.9 copy-start
  60.5 0.9 copy-start.4
  61.4 0.9 copy-start.10
  70.3 1.1 copy-start.5
  72.9 1.1 copy-start.8
  72.9 1.1 copy-start.6
  72.9 6.5 %copy-start.17 = (s32[192]{0:T(256)S(1)}, s32[192]{0:T(256)}, u32[]{:S(2)}) copy-start(s32[192]{0:T(256)} %param.6) | copy-start | bytes 2308
  72.9 6.6 %copy-start.3 = (bf16[192,768]{1,0:T(8,128)(2,1)S(1)}, bf16[192,768]{1,0:T(8,128)(2,1)}, u32[]{:S(2)}) copy-start(bf16[192,768]{1,0:T(8,128)(2,1)} %refs_1_.1) | copy-start | bytes 884740
  74.0 19.6 %all-to-all-start.2 = ((f16[12,4,8,8,128]{4,3,2,1,0:T(8,128)(2,1)}), f16[12,4,8,8,128]{4,3,2,1,0:T(8,128)(2,1)}, u32[]{:S(2)}, u32[]{:S(2)}) async-start(f16[12,4,8,8,128]{4,3,2,1,0:T(8,128)(2,1)} %bitcast.9), calls=%async_computation.2 | async-start | bytes 1572864 | tf_op jit(solution)/shard_map/named_back/all_to_all | solution.py:264
  79.5 1.1 copy-start.11
  82.4 1.8 %copy-start.12 = (bf16[192,1024]{1,0:T(8,128)(2,1)}, bf16[192,1024]{1,0:T(8,128)(2,1)S(1)}, u32[]{:S(2)}) copy-start(bf16[192,1024]{1,0:T(8,128)(2,1)S(1)} %get-tuple-element.17.refs_0_) | copy-start | bytes 1179652
  82.4 1.8 %copy-start.14 = (bf16[192,1024]{1,0:T(8,128)(2,1)}, bf16[192,1024]{1,0:T(8,128)(2,1)S(1)}, u32[]{:S(2)}) copy-start(bf16[192,1024]{1,0:T(8,128)(2,1)S(1)} %get-tuple-element.18.refs_1_) | copy-start | bytes 1179652
  84.2 26.0 %collective-permute-start.5 = (f16[256,768]{1,0:T(8,128)(2,1)}, f16[256,768]{1,0:T(8,128)(2,1)}, u32[]{:S(2)}, u32[]{:S(2)}) collective-permute-start(f16[256,768]{1,0:T(8,128)(2,1)} %convert_element_type.86), channel_id=1, source_target_pairs={{0,12},{4,8},{8,4},{12,0},{1,13},{5,9},{9,5},{13,1},{2,14},{6,10},... | collective-permute-start | bytes 1179656 | tf_op jit(solution)/shard_map/grad_x/ppermute | solution.py:282
  88.6 21.6 %collective-permute-start.4 = (f16[256,768]{1,0:T(8,128)(2,1)}, f16[256,768]{1,0:T(8,128)(2,1)}, u32[]{:S(2)}, u32[]{:S(2)}) collective-permute-start(f16[256,768]{1,0:T(8,128)(2,1)} %convert_element_type.84), channel_id=1, source_target_pairs={{0,8},{4,12},{8,0},{12,4},{1,9},{5,13},{9,1},{13,5},{2,10},{6,14},... | collective-permute-start | bytes 1179656 | tf_op jit(solution)/shard_map/grad_x/ppermute | solution.py:282
  91.0 19.2 %collective-permute-start.3 = (f16[256,768]{1,0:T(8,128)(2,1)S(1)}, f16[256,768]{1,0:T(8,128)(2,1)}, u32[]{:S(2)}, u32[]{:S(2)}) collective-permute-start(f16[256,768]{1,0:T(8,128)(2,1)S(1)} %convert_element_type.82), channel_id=1, source_target_pairs={{0,4},{4,0},{8,12},{12,8},{1,5},{5,1},{9,13},{13,9},{2,6},{6,2},{1... | collective-permute-start | bytes 1179656 | tf_op jit(solution)/shard_map/grad_x/ppermute | solution.py:282
  96.9 34.4 %all-to-all-start.3 = ((f16[48,4,8,128]{3,2,1,0:T(8,128)(2,1)}), f16[48,4,8,128]{3,2,1,0:T(8,128)(2,1)}, u32[]{:S(2)}, u32[]{:S(2)}) async-start(f16[48,4,8,128]{3,2,1,0:T(8,128)(2,1)} %convert_element_type.96), calls=%async_computation.3 | async-start | bytes 786432 | tf_op jit(solution)/shard_map/pieces_home/all_to_all | solution.py:316
  110.2 13.0 %copy-start.1 = (bf16[256,768]{1,0:T(8,128)(2,1)S(1)}, bf16[256,768]{1,0:T(8,128)(2,1)}, u32[]{:S(2)}) copy-start(bf16[256,768]{1,0:T(8,128)(2,1)} %copy-done) | copy-start | bytes 1179652
  110.2 13.0 %copy-start.7 = (bf16[192,512]{1,0:T(8,128)(2,1)S(1)}, bf16[192,512]{1,0:T(8,128)(2,1)}, u32[]{:S(2)}) copy-start(bf16[192,512]{1,0:T(8,128)(2,1)} %copy-done.6) | copy-start | bytes 589828
  110.2 13.0 %copy-start.9 = (bf16[192,512]{1,0:T(8,128)(2,1)S(1)}, bf16[192,512]{1,0:T(8,128)(2,1)}, u32[]{:S(2)}) copy-start(bf16[192,512]{1,0:T(8,128)(2,1)} %copy-done.8) | copy-start | bytes 589828
  110.2 13.0 %copy-start.13 = (bf16[192,1024]{1,0:T(8,128)(2,1)S(1)}, bf16[192,1024]{1,0:T(8,128)(2,1)}, u32[]{:S(2)}) copy-start(bf16[192,1024]{1,0:T(8,128)(2,1)} %copy-done.12) | copy-start | bytes 1179652
  110.2 13.0 %copy-start.15 = (bf16[192,1024]{1,0:T(8,128)(2,1)S(1)}, bf16[192,1024]{1,0:T(8,128)(2,1)}, u32[]{:S(2)}) copy-start(bf16[192,1024]{1,0:T(8,128)(2,1)} %copy-done.14) | copy-start | bytes 1179652
  111.8 13.4 %collective-permute-start.6 = (f16[64,768]{1,0:T(8,128)(2,1)S(1)}, f16[64,768]{1,0:T(8,128)(2,1)S(1)}, u32[]{:S(2)}, u32[]{:S(2)}) collective-permute-start(f16[64,768]{1,0:T(8,128)(2,1)S(1)} %get-tuple-element.26), channel_id=1, source_target_pairs={{0,2},{1,3},{2,0},{3,1},{4,6},{5,7},{6,4},{7,5},{8,10},{9,11},{10,... | collective-permute-start | bytes 294920 | tf_op jit(solution)/shard_map/grad_yh/ppermute | solution.py:288
  116.7 11.5 %collective-permute-start.8 = (f16[64,768]{1,0:T(8,128)(2,1)S(1)}, f16[64,768]{1,0:T(8,128)(2,1)S(1)}, u32[]{:S(2)}, u32[]{:S(2)}) collective-permute-start(f16[64,768]{1,0:T(8,128)(2,1)S(1)} %get-tuple-element.27), channel_id=1, source_target_pairs={{0,3},{1,2},{2,1},{3,0},{4,7},{5,6},{6,5},{7,4},{8,11},{9,10},{10,... | collective-permute-start | bytes 294920 | tf_op jit(solution)/shard_map/grad_yh/ppermute | solution.py:288
  120.5 9.0 %collective-permute-start.7 = (f16[64,768]{1,0:T(8,128)(2,1)S(1)}, f16[64,768]{1,0:T(8,128)(2,1)S(1)}, u32[]{:S(2)}, u32[]{:S(2)}) collective-permute-start(f16[64,768]{1,0:T(8,128)(2,1)S(1)} %get-tuple-element.28), channel_id=1, source_target_pairs={{0,1},{1,0},{2,3},{3,2},{4,5},{5,4},{6,7},{7,6},{8,9},{9,8},{10,11... | collective-permute-start | bytes 294920 | tf_op jit(solution)/shard_map/grad_yh/ppermute | solution.py:288

commit v5 on v4

--- a/solution.py
+++ b/solution.py
@@ -205,12 +205,13 @@
 
     pieces = passages.reshape(row_tiles, SUBS, col_tiles, LANES).transpose(0, 2, 1, 3)
     pieces = pieces.reshape(members, tiles * SUBS, LANES)
-    names = jnp.pad(negative_owners[0].astype(bf16), (0, LANES - neg_count))
     rows = tiles * SUBS
+    names = jnp.pad(negative_owners, ((0, SUBS - 1), (0, LANES - neg_count))).astype(bf16)
+    names = jnp.pad(names, ((rows, 0), (0, 0)))
     shape = (runs, members, rows + SUBS, LANES)
     row = lax.broadcasted_iota(jnp.int32, shape, 2)
     sent = jnp.pad(pieces, ((0, 0), (0, SUBS), (0, 0)))
-    sent = jnp.where(row < rows, jnp.broadcast_to(sent[None], shape), jnp.broadcast_to(names, shape))
+    sent = jnp.where(row < rows, jnp.broadcast_to(sent[None], shape), jnp.broadcast_to(names[None, None], shape))
     sent = sent.reshape(wide, rows + SUBS, LANES)
     with jax.named_scope("spread_pieces"):
         spread = lax.all_to_all(sent, WIDE, 0, 0, tiled=True)

time: 134 us -> 134 us (level)
  no operation moved by 1% of the time
where the time goes in v5:
time: 134 us; the launch traced here: 133 us
  starting transfers between devices  74.7 us (56%)
  waiting for transfers between devices  17.9 us (13%)
  blocking collectives  15.6 us (12%)
  other arithmetic  9.97 us (7%)
  Pallas kernels  8.91 us (7%)
  local copies, waits for them, and re-layouts  5.12 us (4%)
    all_to_all x1, starting transfers between devices, local(): spread = lax.all_to_all(sent, WIDE, 0, 0, tiled=True)  18 us
    all_gather x1, blocking collectives, local(): mine = lax.all_gather(passages, 'yh', axis=0, tiled=True)  15.6 us
    all_to_all x1, starting transfers between devices, local(): home = lax.all_to_all(summed.astype(half), WIDE, 0, 0, tiled=True)  13.2 us
    ppermute x3, starting transfers between devices, local(): part = lax.ppermute(part, 'yh', swaps[k])  11.4 us
    ppermute x3, starting transfers between devices, local(): part = lax.ppermute(leaving[k - 1], 'x', swaps[k])  8.97 us
    ppermute x3, starting transfers between devices, local(): slabs = [mine] + [lax.ppermute(mine, 'x', swaps[k]) for k in range(1, far)]  8.97 us
    pallas_call x6, Pallas kernels, call(): pl.pallas_call(body, out_shape=tuple((jax.ShapeDtypeStruct(shape, dtype)...  8.91 us
    all_to_all x1, starting transfers between devices, local(): named = lax.all_to_all(picked, RUN, 0, 0, tiled=True)  8.73 us
  transfers between devices with their start and end apart: 13, of which 7 were waited for; matrix products, arithmetic and copies ran while one was open for 4% of the time, Pallas kernels for 6%

profile of v5, /device:TPU:1, one launch (start us, length us, event | category | flops | bytes accessed | tf_op | source)
XLA Modules:
  0.0 133.2 jit_solution(5413695595919854459)
XLA Ops:
  1.4 0.9 pad.13
  3.2 18.0 %all-to-all-start = ((bf16[48,40,128]{2,1,0:T(8,128)(2,1)}), bf16[48,40,128]{2,1,0:T(8,128)(2,1)S(1)}, u32[]{:S(2)}, u32[]{:S(2)}) async-start(bf16[48,40,128]{2,1,0:T(8,128)(2,1)} %bitcast_select_fusion), calls=%async_computation | async-start | bytes 983040 | tf_op jit(solution)/shard_map/spread_pieces/all_to_all | solution.py:217
  21.2 15.6 %all_gather.3.refs_1_.refs_3_.refs_5_ = bf16[256,768]{1,0:T(8,128)(2,1)S(1)} all-gather(bf16[64,768]{1,0:T(8,128)(2,1)S(1)} %copy-done.16), channel_id=1, replica_groups=mesh['zs'=4,'zl'=3,'yl'=2,'c'=2,'x'=4,'yh'=4] {'yh'}, dimensions={0}, use_global_device_ids=true | all-gather | bytes 491520 | tf_op jit(solution)/shard_map/pool_yh/all_gather | solution.py:221
  36.7 4.4 %collective-permute-start.2 = (bf16[256,768]{1,0:T(8,128)(2,1)S(1)}, bf16[256,768]{1,0:T(8,128)(2,1)S(1)}, u32[]{:S(2)}, u32[]{:S(2)}) collective-permute-start(bf16[256,768]{1,0:T(8,128)(2,1)S(1)} %all_gather.3.refs_1_.refs_3_.refs_5_), channel_id=1, source_target_pairs={{0,12},{4,8},{8,4},{12,0},{1,13},{5,9},{9,5},{13,1},{2,14},{6,10},... | collective-permute-start | bytes 1179656 | tf_op jit(solution)/shard_map/pool_x/ppermute | solution.py:223
  41.1 2.4 %collective-permute-start.1 = (bf16[256,768]{1,0:T(8,128)(2,1)S(1)}, bf16[256,768]{1,0:T(8,128)(2,1)S(1)}, u32[]{:S(2)}, u32[]{:S(2)}) collective-permute-start(bf16[256,768]{1,0:T(8,128)(2,1)S(1)} %all_gather.3.refs_1_.refs_3_.refs_5_), channel_id=1, source_target_pairs={{0,8},{4,12},{8,0},{12,4},{1,9},{5,13},{9,1},{13,5},{2,10},{6,14},... | collective-permute-start | bytes 1179656 | tf_op jit(solution)/shard_map/pool_x/ppermute | solution.py:223
  43.6 2.2 %collective-permute-start = (bf16[256,768]{1,0:T(8,128)(2,1)S(1)}, bf16[256,768]{1,0:T(8,128)(2,1)S(1)}, u32[]{:S(2)}, u32[]{:S(2)}) collective-permute-start(bf16[256,768]{1,0:T(8,128)(2,1)S(1)} %all_gather.3.refs_1_.refs_3_.refs_5_), channel_id=1, source_target_pairs={{0,4},{4,0},{8,12},{12,8},{1,5},{5,1},{9,13},{13,9},{2,6},{6,2},{1... | collective-permute-start | bytes 1179656 | tf_op jit(solution)/shard_map/pool_x/ppermute | solution.py:223
  45.9 1.6 %shard_map.60 = bf16[12,4,8,8,128]{4,3,2,1,0:T(8,128)(2,1)} custom-call(s32[1]{0:T(128)} %bitcast.refs_0_, s32[384]{0:T(512)S(1)} %reshape.48.refs_1_, bf16[240,8,128]{2,1,0:T(8,128)(2,1)S(1)} %bitcast.17, bf16[256,768]{1,0:T(8,128)(2,1)S(1)} %all_gather.3.refs_1_.refs_3_.refs_5_), custom_call_target="tpu_custom_call" | custom-call | bytes 4194304 | tf_op jit(solution)/shard_map/pallas_call | solution.py:180
  47.6 8.7 %all-to-all-start.1 = ((bf16[12,4,8,8,128]{4,3,2,1,0:T(8,128)(2,1)}), bf16[12,4,8,8,128]{4,3,2,1,0:T(8,128)(2,1)S(1)}, u32[]{:S(2)}, u32[]{:S(2)}) async-start(bf16[12,4,8,8,128]{4,3,2,1,0:T(8,128)(2,1)} %shard_map.60), calls=%async_computation.1 | async-start | bytes 1572864 | tf_op jit(solution)/shard_map/named_pieces/all_to_all | solution.py:238
  56.5 3.0 %collective-permute-done.refs_2_.refs_6_ = bf16[256,768]{1,0:T(8,128)(2,1)S(1)} collective-permute-done((bf16[256,768]{1,0:T(8,128)(2,1)S(1)}, bf16[256,768]{1,0:T(8,128)(2,1)S(1)}, u32[]{:S(2)}, u32[]{:S(2)}) %collective-permute-start) | collective-permute-done | bytes 393248 | tf_op jit(solution)/shard_map/pool_x/ppermute | solution.py:223
  62.3 8.1 %all-to-all-done.1 = bf16[12,4,8,8,128]{4,3,2,1,0:T(8,128)(2,1)S(1)} async-done(((bf16[12,4,8,8,128]{4,3,2,1,0:T(8,128)(2,1)}), bf16[12,4,8,8,128]{4,3,2,1,0:T(8,128)(2,1)S(1)}, u32[]{:S(2)}, u32[]{:S(2)}) %all-to-all-start.1) | async-done | bytes 786464 | tf_op jit(solution)/shard_map/named_pieces/all_to_all | solution.py:238
  70.3 1.1 copy-done.5
  71.5 1.4 %shard_map.61 = (bf16[192,512]{1,0:T(8,128)(2,1)S(1)}, bf16[192,512]{1,0:T(8,128)(2,1)S(1)}, f32[48,64,128]{2,1,0:T(8,128)S(1)}, f32[192,128]{1,0:T(8,128)S(1)}) custom-call(bf16[48,64,128]{2,1,0:T(8,128)(2,1)S(1)} %bitcast.18, f32[192,1024]{1,0:T(8,128)S(1)} %copy-done.5), custom_call_target="tpu_custom_call" | custom-call | flops 452984832 | bytes 4194304 | tf_op jit(solution)/shard_map/pallas_call | solution.py:180
  72.9 1.1 convert_element_type.87
  74.0 5.4 %all-to-all-start.2 = ((f16[12,4,8,8,128]{4,3,2,1,0:T(8,128)(2,1)}), f16[12,4,8,8,128]{4,3,2,1,0:T(8,128)(2,1)}, u32[]{:S(2)}, u32[]{:S(2)}) async-start(f16[12,4,8,8,128]{4,3,2,1,0:T(8,128)(2,1)} %bitcast.8), calls=%async_computation.2 | async-start | bytes 1572864 | tf_op jit(solution)/shard_map/named_back/all_to_all | solution.py:265
  79.5 1.1 copy-done.11
  80.6 1.8 %shard_map.62 = (bf16[192,1024]{1,0:T(8,128)(2,1)S(1)}, bf16[192,1024]{1,0:T(8,128)(2,1)S(1)}, f32[256,768]{1,0:T(8,128)S(1)}, f32[256,768]{1,0:T(8,128)S(1)}, f...) custom-call(s32[4]{0:T(128)S(1)} %iota_xor_fusion.refs_0_, bf16[192,768]{1,0:T(8,128)(2,1)S(1)} %copy-done.3, ...), custom_call_target="tpu_custom_call" | custom-call | flops 603979776 | bytes 4194304 | tf_op jit(solution)/shard_map/pallas_call | solution.py:180
  82.5 0.9 convert_element_type.77
  84.2 4.4 %collective-permute-start.5 = (f16[256,768]{1,0:T(8,128)(2,1)}, f16[256,768]{1,0:T(8,128)(2,1)}, u32[]{:S(2)}, u32[]{:S(2)}) collective-permute-start(f16[256,768]{1,0:T(8,128)(2,1)} %convert_element_type.79), channel_id=1, source_target_pairs={{0,12},{4,8},{8,4},{12,0},{1,13},{5,9},{9,5},{13,1},{2,14},{6,10},... | collective-permute-start | bytes 1179656 | tf_op jit(solution)/shard_map/grad_x/ppermute | solution.py:283
  88.6 2.4 %collective-permute-start.4 = (f16[256,768]{1,0:T(8,128)(2,1)}, f16[256,768]{1,0:T(8,128)(2,1)}, u32[]{:S(2)}, u32[]{:S(2)}) collective-permute-start(f16[256,768]{1,0:T(8,128)(2,1)} %convert_element_type.77), channel_id=1, source_target_pairs={{0,8},{4,12},{8,0},{12,4},{1,9},{5,13},{9,1},{13,5},{2,10},{6,14},... | collective-permute-start | bytes 1179656 | tf_op jit(solution)/shard_map/grad_x/ppermute | solution.py:283
  91.0 2.2 %collective-permute-start.3 = (f16[256,768]{1,0:T(8,128)(2,1)S(1)}, f16[256,768]{1,0:T(8,128)(2,1)}, u32[]{:S(2)}, u32[]{:S(2)}) collective-permute-start(f16[256,768]{1,0:T(8,128)(2,1)S(1)} %convert_element_type.75), channel_id=1, source_target_pairs={{0,4},{4,0},{8,12},{12,8},{1,5},{5,1},{9,13},{13,9},{2,6},{6,2},{1... | collective-permute-start | bytes 1179656 | tf_op jit(solution)/shard_map/grad_x/ppermute | solution.py:283
  93.6 1.3 convert_element_type.88.refs_2_
  94.9 1.2 shard_map.64
  96.9 13.2 %all-to-all-start.3 = ((f16[48,4,8,128]{3,2,1,0:T(8,128)(2,1)}), f16[48,4,8,128]{3,2,1,0:T(8,128)(2,1)}, u32[]{:S(2)}, u32[]{:S(2)}) async-start(f16[48,4,8,128]{3,2,1,0:T(8,128)(2,1)} %convert_element_type.89), calls=%async_computation.3 | async-start | bytes 786432 | tf_op jit(solution)/shard_map/pieces_home/all_to_all | solution.py:317
  110.2 1.5 %convert_add_fusion.refs_9_ = f32[256,768]{1,0:T(8,128)S(1)} fusion(f16[256,768]{1,0:T(8,128)(2,1)} %collective-permute-done.5, f16[256,768]{1,0:T(8,128)(2,1)} %collective-permute-done.4, f32[256,768]{1,0:T(8,128)S(1)} %get-tuple-element.21, f16[256,768]{1,0:T(8,128)(2,1)} %collective-permute-done.3), kind=kLoop, calls=%fused_computation | loop fusion | flops 1179648 | bytes 2752512 | tf_op jit(solution)/shard_map/grad_x/add | solution.py:284
  111.8 4.9 %collective-permute-start.6 = (f16[64,768]{1,0:T(8,128)(2,1)S(1)}, f16[64,768]{1,0:T(8,128)(2,1)S(1)}, u32[]{:S(2)}, u32[]{:S(2)}) collective-permute-start(f16[64,768]{1,0:T(8,128)(2,1)S(1)} %get-tuple-element.26), channel_id=1, source_target_pairs={{0,2},{1,3},{2,0},{3,1},{4,6},{5,7},{6,4},{7,5},{8,10},{9,11},{10,... | collective-permute-start | bytes 294920 | tf_op jit(solution)/shard_map/grad_yh/ppermute | solution.py:289
  116.8 3.7 %collective-permute-start.8 = (f16[64,768]{1,0:T(8,128)(2,1)S(1)}, f16[64,768]{1,0:T(8,128)(2,1)S(1)}, u32[]{:S(2)}, u32[]{:S(2)}) collective-permute-start(f16[64,768]{1,0:T(8,128)(2,1)S(1)} %get-tuple-element.27), channel_id=1, source_target_pairs={{0,3},{1,2},{2,1},{3,0},{4,7},{5,6},{6,5},{7,4},{8,11},{9,10},{10,... | collective-permute-start | bytes 294920 | tf_op jit(solution)/shard_map/grad_yh/ppermute | solution.py:289
  120.5 2.7 %collective-permute-start.7 = (f16[64,768]{1,0:T(8,128)(2,1)S(1)}, f16[64,768]{1,0:T(8,128)(2,1)S(1)}, u32[]{:S(2)}, u32[]{:S(2)}) collective-permute-start(f16[64,768]{1,0:T(8,128)(2,1)S(1)} %get-tuple-element.28), channel_id=1, source_target_pairs={{0,1},{1,0},{2,3},{3,2},{4,5},{5,4},{6,7},{7,6},{8,9},{9,8},{10,11... | collective-permute-start | bytes 294920 | tf_op jit(solution)/shard_map/grad_yh/ppermute | solution.py:289
  123.3 2.0 %shard_map.63 = f32[192,768]{1,0:T(8,128)} custom-call(bf16[192,1024]{1,0:T(8,128)(2,1)S(1)} %copy-done.13, bf16[192,1024]{1,0:T(8,128)(2,1)S(1)} %copy-done.15, bf16[192,512]{1,0:T(8,128)(2,1)S(1)} %copy-done.7, bf16[192,512]{1,0:T(8,128)(2,1)S(1)} %copy-done.9, bf16[48,64,128]{2,1,0:T(8,128)(2,1)S(1)} %bitcast.19, ...), custom_call_target="tpu_custom_call" | custom-call | flops 3623878656 | bytes 4194304 | tf_op jit(solution)/shard_map/pallas_call | solution.py:180
  125.3 3.0 %collective-permute-done.8 = f16[64,768]{1,0:T(8,128)(2,1)S(1)} collective-permute-done((f16[64,768]{1,0:T(8,128)(2,1)S(1)}, f16[64,768]{1,0:T(8,128)(2,1)S(1)}, u32[]{:S(2)}, u32[]{:S(2)}) %collective-permute-start.8) | collective-permute-done | bytes 98336 | tf_op jit(solution)/shard_map/grad_yh/ppermute | solution.py:289
  128.3 1.1 collective-permute-done.7
  129.4 1.9 %all-to-all-done.3 = f16[48,4,8,128]{3,2,1,0:T(8,128)(2,1)} async-done(((f16[48,4,8,128]{3,2,1,0:T(8,128)(2,1)}), f16[48,4,8,128]{3,2,1,0:T(8,128)(2,1)}, u32[]{:S(2)}, u32[]{:S(2)}) %all-to-all-start.3) | async-done | bytes 393248 | tf_op jit(solution)/shard_map/pieces_home/all_to_all | solution.py:317
  131.4 1.8 %fusion.6 = f32[64,768]{1,0:T(8,128)} fusion(f32[256,768]{1,0:T(8,128)S(1)} %convert_add_fusion.refs_9_, f16[64,768]{1,0:T(8,128)(2,1)S(1)} %collective-permute-done.8, f16[64,768]{1,0:T(8,128)(2,1)S(1)} %collective-permute-done.7, f16[64,768]{1,0:T(8,128)(2,1)S(1)} %collective-permute-done.6, f16[4,8,8,6,128]{4,2,3,1,0:T(8,128)(2,1)} %bitcast.10), kind=kLoop, calls=%fused_computation.12 | loop fusion | flops 933888 | bytes 1081344 | tf_op jit(solution)/shard_map/add | solution.py:323
  (55 shorter events, 6.9 us)
Async XLA Ops:
  0.6 20.5 %copy-start.16 = (bf16[64,768]{1,0:T(8,128)(2,1)S(1)}, bf16[64,768]{1,0:T(8,128)(2,1)}, u32[]{:S(2)}) copy-start(bf16[64,768]{1,0:T(8,128)(2,1)} %param.5) | copy-start | bytes 294916
  3.2 42.6 %all-to-all-start = ((bf16[48,40,128]{2,1,0:T(8,128)(2,1)}), bf16[48,40,128]{2,1,0:T(8,128)(2,1)S(1)}, u32[]{:S(2)}, u32[]{:S(2)}) async-start(bf16[48,40,128]{2,1,0:T(8,128)(2,1)} %bitcast_select_fusion), calls=%async_computation | async-start | bytes 983040 | tf_op jit(solution)/shard_map/spread_pieces/all_to_all | solution.py:217
  36.7 19.8 %collective-permute-start.2 = (bf16[256,768]{1,0:T(8,128)(2,1)S(1)}, bf16[256,768]{1,0:T(8,128)(2,1)S(1)}, u32[]{:S(2)}, u32[]{:S(2)}) collective-permute-start(bf16[256,768]{1,0:T(8,128)(2,1)S(1)} %all_gather.3.refs_1_.refs_3_.refs_5_), channel_id=1, source_target_pairs={{0,12},{4,8},{8,4},{12,0},{1,13},{5,9},{9,5},{13,1},{2,14},{6,10},... | collective-permute-start | bytes 1179656 | tf_op jit(solution)/shard_map/pool_x/ppermute | solution.py:223
  41.1 15.4 %collective-permute-start.1 = (bf16[256,768]{1,0:T(8,128)(2,1)S(1)}, bf16[256,768]{1,0:T(8,128)(2,1)S(1)}, u32[]{:S(2)}, u32[]{:S(2)}) collective-permute-start(bf16[256,768]{1,0:T(8,128)(2,1)S(1)} %all_gather.3.refs_1_.refs_3_.refs_5_), channel_id=1, source_target_pairs={{0,8},{4,12},{8,0},{12,4},{1,9},{5,13},{9,1},{13,5},{2,10},{6,14},... | collective-permute-start | bytes 1179656 | tf_op jit(solution)/shard_map/pool_x/ppermute | solution.py:223
  43.6 16.0 %collective-permute-start = (bf16[256,768]{1,0:T(8,128)(2,1)S(1)}, bf16[256,768]{1,0:T(8,128)(2,1)S(1)}, u32[]{:S(2)}, u32[]{:S(2)}) collective-permute-start(bf16[256,768]{1,0:T(8,128)(2,1)S(1)} %all_gather.3.refs_1_.refs_3_.refs_5_), channel_id=1, source_target_pairs={{0,4},{4,0},{8,12},{12,8},{1,5},{5,1},{9,13},{13,9},{2,6},{6,2},{1... | collective-permute-start | bytes 1179656 | tf_op jit(solution)/shard_map/pool_x/ppermute | solution.py:223
  45.9 13.7 %copy-start.2 = (bf16[192,768]{1,0:T(8,128)(2,1)S(1)}, bf16[192,768]{1,0:T(8,128)(2,1)}, u32[]{:S(2)}) copy-start(bf16[192,768]{1,0:T(8,128)(2,1)} %refs_1_.1) | copy-start | bytes 884740
  47.6 22.8 %all-to-all-start.1 = ((bf16[12,4,8,8,128]{4,3,2,1,0:T(8,128)(2,1)}), bf16[12,4,8,8,128]{4,3,2,1,0:T(8,128)(2,1)S(1)}, u32[]{:S(2)}, u32[]{:S(2)}) async-start(bf16[12,4,8,8,128]{4,3,2,1,0:T(8,128)(2,1)} %shard_map.60), calls=%async_computation.1 | async-start | bytes 1572864 | tf_op jit(solution)/shard_map/named_pieces/all_to_all | solution.py:238
  59.6 0.9 copy-start
  60.5 0.9 copy-start.4
  61.4 0.9 copy-start.10
  70.3 1.1 copy-start.5
  72.9 1.1 copy-start.8
  72.9 1.1 copy-start.6
  72.9 6.5 %copy-start.17 = (s32[192]{0:T(256)S(1)}, s32[192]{0:T(256)}, u32[]{:S(2)}) copy-start(s32[192]{0:T(256)} %param.6) | copy-start | bytes 2308
  72.9 6.5 %copy-start.3 = (bf16[192,768]{1,0:T(8,128)(2,1)S(1)}, bf16[192,768]{1,0:T(8,128)(2,1)}, u32[]{:S(2)}) copy-start(bf16[192,768]{1,0:T(8,128)(2,1)} %refs_1_.1) | copy-start | bytes 884740
  74.0 19.6 %all-to-all-start.2 = ((f16[12,4,8,8,128]{4,3,2,1,0:T(8,128)(2,1)}), f16[12,4,8,8,128]{4,3,2,1,0:T(8,128)(2,1)}, u32[]{:S(2)}, u32[]{:S(2)}) async-start(f16[12,4,8,8,128]{4,3,2,1,0:T(8,128)(2,1)} %bitcast.8), calls=%async_computation.2 | async-start | bytes 1572864 | tf_op jit(solution)/shard_map/named_back/all_to_all | solution.py:265
  79.5 1.1 copy-start.11
  82.4 1.8 %copy-start.12 = (bf16[192,1024]{1,0:T(8,128)(2,1)}, bf16[192,1024]{1,0:T(8,128)(2,1)S(1)}, u32[]{:S(2)}) copy-start(bf16[192,1024]{1,0:T(8,128)(2,1)S(1)} %get-tuple-element.17.refs_0_) | copy-start | bytes 1179652
  82.4 1.8 %copy-start.14 = (bf16[192,1024]{1,0:T(8,128)(2,1)}, bf16[192,1024]{1,0:T(8,128)(2,1)S(1)}, u32[]{:S(2)}) copy-start(bf16[192,1024]{1,0:T(8,128)(2,1)S(1)} %get-tuple-element.18.refs_1_) | copy-start | bytes 1179652
  84.2 26.0 %collective-permute-start.5 = (f16[256,768]{1,0:T(8,128)(2,1)}, f16[256,768]{1,0:T(8,128)(2,1)}, u32[]{:S(2)}, u32[]{:S(2)}) collective-permute-start(f16[256,768]{1,0:T(8,128)(2,1)} %convert_element_type.79), channel_id=1, source_target_pairs={{0,12},{4,8},{8,4},{12,0},{1,13},{5,9},{9,5},{13,1},{2,14},{6,10},... | collective-permute-start | bytes 1179656 | tf_op jit(solution)/shard_map/grad_x/ppermute | solution.py:283
  88.6 21.6 %collective-permute-start.4 = (f16[256,768]{1,0:T(8,128)(2,1)}, f16[256,768]{1,0:T(8,128)(2,1)}, u32[]{:S(2)}, u32[]{:S(2)}) collective-permute-start(f16[256,768]{1,0:T(8,128)(2,1)} %convert_element_type.77), channel_id=1, source_target_pairs={{0,8},{4,12},{8,0},{12,4},{1,9},{5,13},{9,1},{13,5},{2,10},{6,14},... | collective-permute-start | bytes 1179656 | tf_op jit(solution)/shard_map/grad_x/ppermute | solution.py:283
  91.0 19.2 %collective-permute-start.3 = (f16[256,768]{1,0:T(8,128)(2,1)S(1)}, f16[256,768]{1,0:T(8,128)(2,1)}, u32[]{:S(2)}, u32[]{:S(2)}) collective-permute-start(f16[256,768]{1,0:T(8,128)(2,1)S(1)} %convert_element_type.75), channel_id=1, source_target_pairs={{0,4},{4,0},{8,12},{12,8},{1,5},{5,1},{9,13},{13,9},{2,6},{6,2},{1... | collective-permute-start | bytes 1179656 | tf_op jit(solution)/shard_map/grad_x/ppermute | solution.py:283
  96.9 34.4 %all-to-all-start.3 = ((f16[48,4,8,128]{3,2,1,0:T(8,128)(2,1)}), f16[48,4,8,128]{3,2,1,0:T(8,128)(2,1)}, u32[]{:S(2)}, u32[]{:S(2)}) async-start(f16[48,4,8,128]{3,2,1,0:T(8,128)(2,1)} %convert_element_type.89), calls=%async_computation.3 | async-start | bytes 786432 | tf_op jit(solution)/shard_map/pieces_home/all_to_all | solution.py:317
  110.2 13.0 %copy-start.1 = (bf16[256,768]{1,0:T(8,128)(2,1)S(1)}, bf16[256,768]{1,0:T(8,128)(2,1)}, u32[]{:S(2)}) copy-start(bf16[256,768]{1,0:T(8,128)(2,1)} %copy-done) | copy-start | bytes 1179652
  110.2 13.0 %copy-start.7 = (bf16[192,512]{1,0:T(8,128)(2,1)S(1)}, bf16[192,512]{1,0:T(8,128)(2,1)}, u32[]{:S(2)}) copy-start(bf16[192,512]{1,0:T(8,128)(2,1)} %copy-done.6) | copy-start | bytes 589828
  110.2 13.0 %copy-start.9 = (bf16[192,512]{1,0:T(8,128)(2,1)S(1)}, bf16[192,512]{1,0:T(8,128)(2,1)}, u32[]{:S(2)}) copy-start(bf16[192,512]{1,0:T(8,128)(2,1)} %copy-done.8) | copy-start | bytes 589828
  110.2 13.0 %copy-start.13 = (bf16[192,1024]{1,0:T(8,128)(2,1)S(1)}, bf16[192,1024]{1,0:T(8,128)(2,1)}, u32[]{:S(2)}) copy-start(bf16[192,1024]{1,0:T(8,128)(2,1)} %copy-done.12) | copy-start | bytes 1179652
  110.2 13.0 %copy-start.15 = (bf16[192,1024]{1,0:T(8,128)(2,1)S(1)}, bf16[192,1024]{1,0:T(8,128)(2,1)}, u32[]{:S(2)}) copy-start(bf16[192,1024]{1,0:T(8,128)(2,1)} %copy-done.14) | copy-start | bytes 1179652
  111.8 13.4 %collective-permute-start.6 = (f16[64,768]{1,0:T(8,128)(2,1)S(1)}, f16[64,768]{1,0:T(8,128)(2,1)S(1)}, u32[]{:S(2)}, u32[]{:S(2)}) collective-permute-start(f16[64,768]{1,0:T(8,128)(2,1)S(1)} %get-tuple-element.26), channel_id=1, source_target_pairs={{0,2},{1,3},{2,0},{3,1},{4,6},{5,7},{6,4},{7,5},{8,10},{9,11},{10,... | collective-permute-start | bytes 294920 | tf_op jit(solution)/shard_map/grad_yh/ppermute | solution.py:289
  116.8 11.5 %collective-permute-start.8 = (f16[64,768]{1,0:T(8,128)(2,1)S(1)}, f16[64,768]{1,0:T(8,128)(2,1)S(1)}, u32[]{:S(2)}, u32[]{:S(2)}) collective-permute-start(f16[64,768]{1,0:T(8,128)(2,1)S(1)} %get-tuple-element.27), channel_id=1, source_target_pairs={{0,3},{1,2},{2,1},{3,0},{4,7},{5,6},{6,5},{7,4},{8,11},{9,10},{10,... | collective-permute-start | bytes 294920 | tf_op jit(solution)/shard_map/grad_yh/ppermute | solution.py:289
  120.5 9.0 %collective-permute-start.7 = (f16[64,768]{1,0:T(8,128)(2,1)S(1)}, f16[64,768]{1,0:T(8,128)(2,1)S(1)}, u32[]{:S(2)}, u32[]{:S(2)}) collective-permute-start(f16[64,768]{1,0:T(8,128)(2,1)S(1)} %get-tuple-element.28), channel_id=1, source_target_pairs={{0,1},{1,0},{2,3},{3,2},{4,5},{5,4},{6,7},{7,6},{8,9},{9,8},{10,11... | collective-permute-start | bytes 294920 | tf_op jit(solution)/shard_map/grad_yh/ppermute | solution.py:289

commit v6 on v4

--- a/solution.py
+++ b/solution.py
@@ -56,14 +56,12 @@
     for u in range(tiles):
         acc_refs[u][...] = jnp.zeros_like(acc_refs[u])
 
-    def body(i, carry):
+    first = run_ref[0] * members
+    for i in range(members):
         for k in range(count):
-            owner = owners_ref[(run_ref[0] * members + i) * count + k]
+            owner = owners_ref[(first + i) * count + k]
             for u in range(tiles):
                 acc_refs[u][owner] += terms_ref[i, u, k]
-        return carry
-
-    lax.fori_loop(0, members, body, 0)
     for u in range(tiles):
         out_ref[:, u] = acc_refs[u][...] * DROP
 

time: 134 us -> 134 us (level)
  no operation moved by 1% of the time
where the time goes in v6:
time: 134 us; the launch traced here: 133 us
  starting transfers between devices  74.7 us (56%)
  waiting for transfers between devices  17.9 us (13%)
  blocking collectives  15.6 us (12%)
  other arithmetic  9.97 us (7%)
  Pallas kernels  8.81 us (7%)
  local copies, waits for them, and re-layouts  5.11 us (4%)
    all_to_all x1, starting transfers between devices, local(): spread = lax.all_to_all(sent, WIDE, 0, 0, tiled=True)  18 us
    all_gather x1, blocking collectives, local(): mine = lax.all_gather(passages, 'yh', axis=0, tiled=True)  15.6 us
    all_to_all x1, starting transfers between devices, local(): home = lax.all_to_all(summed.astype(half), WIDE, 0, 0, tiled=True)  13.2 us
    ppermute x3, starting transfers between devices, local(): part = lax.ppermute(part, 'yh', swaps[k])  11.4 us
    ppermute x3, starting transfers between devices, local(): part = lax.ppermute(leaving[k - 1], 'x', swaps[k])  8.97 us
    ppermute x3, starting transfers between devices, local(): slabs = [mine] + [lax.ppermute(mine, 'x', swaps[k]) for k in range(1, far)]  8.97 us
    pallas_call x6, Pallas kernels, call(): pl.pallas_call(body, out_shape=tuple((jax.ShapeDtypeStruct(shape, dtype)...  8.81 us
    all_to_all x1, starting transfers between devices, local(): named = lax.all_to_all(picked, RUN, 0, 0, tiled=True)  8.73 us
  transfers between devices with their start and end apart: 13, of which 7 were waited for; matrix products, arithmetic and copies ran while one was open for 4% of the time, Pallas kernels for 6%

profile of v6, /device:TPU:1, one launch (start us, length us, event | category | flops | bytes accessed | tf_op | source)
XLA Modules:
  0.0 133.1 jit_solution(15058072844649252503)
XLA Ops:
  1.4 0.9 pad.8
  3.1 18.0 %all-to-all-start = ((bf16[48,40,128]{2,1,0:T(8,128)(2,1)}), bf16[48,40,128]{2,1,0:T(8,128)(2,1)S(1)}, u32[]{:S(2)}, u32[]{:S(2)}) async-start(bf16[48,40,128]{2,1,0:T(8,128)(2,1)} %bitcast_select_fusion), calls=%async_computation | async-start | bytes 983040 | tf_op jit(solution)/shard_map/spread_pieces/all_to_all | solution.py:214
  21.2 15.6 %all_gather.3.refs_1_.refs_3_.refs_5_ = bf16[256,768]{1,0:T(8,128)(2,1)S(1)} all-gather(bf16[64,768]{1,0:T(8,128)(2,1)S(1)} %copy-done.16), channel_id=1, replica_groups=mesh['zs'=4,'zl'=3,'yl'=2,'c'=2,'x'=4,'yh'=4] {'yh'}, dimensions={0}, use_global_device_ids=true | all-gather | bytes 491520 | tf_op jit(solution)/shard_map/pool_yh/all_gather | solution.py:218
  36.7 4.4 %collective-permute-start.2 = (bf16[256,768]{1,0:T(8,128)(2,1)S(1)}, bf16[256,768]{1,0:T(8,128)(2,1)S(1)}, u32[]{:S(2)}, u32[]{:S(2)}) collective-permute-start(bf16[256,768]{1,0:T(8,128)(2,1)S(1)} %all_gather.3.refs_1_.refs_3_.refs_5_), channel_id=1, source_target_pairs={{0,12},{4,8},{8,4},{12,0},{1,13},{5,9},{9,5},{13,1},{2,14},{6,10},... | collective-permute-start | bytes 1179656 | tf_op jit(solution)/shard_map/pool_x/ppermute | solution.py:220
  41.1 2.4 %collective-permute-start.1 = (bf16[256,768]{1,0:T(8,128)(2,1)S(1)}, bf16[256,768]{1,0:T(8,128)(2,1)S(1)}, u32[]{:S(2)}, u32[]{:S(2)}) collective-permute-start(bf16[256,768]{1,0:T(8,128)(2,1)S(1)} %all_gather.3.refs_1_.refs_3_.refs_5_), channel_id=1, source_target_pairs={{0,8},{4,12},{8,0},{12,4},{1,9},{5,13},{9,1},{13,5},{2,10},{6,14},... | collective-permute-start | bytes 1179656 | tf_op jit(solution)/shard_map/pool_x/ppermute | solution.py:220
  43.5 2.2 %collective-permute-start = (bf16[256,768]{1,0:T(8,128)(2,1)S(1)}, bf16[256,768]{1,0:T(8,128)(2,1)S(1)}, u32[]{:S(2)}, u32[]{:S(2)}) collective-permute-start(bf16[256,768]{1,0:T(8,128)(2,1)S(1)} %all_gather.3.refs_1_.refs_3_.refs_5_), channel_id=1, source_target_pairs={{0,4},{4,0},{8,12},{12,8},{1,5},{5,1},{9,13},{13,9},{2,6},{6,2},{1... | collective-permute-start | bytes 1179656 | tf_op jit(solution)/shard_map/pool_x/ppermute | solution.py:220
  45.9 1.6 %shard_map.60 = bf16[12,4,8,8,128]{4,3,2,1,0:T(8,128)(2,1)} custom-call(s32[1]{0:T(128)} %bitcast.refs_0_, s32[384]{0:T(512)S(1)} %reshape.48.refs_1_, bf16[240,8,128]{2,1,0:T(8,128)(2,1)S(1)} %bitcast.19, bf16[256,768]{1,0:T(8,128)(2,1)S(1)} %all_gather.3.refs_1_.refs_3_.refs_5_), custom_call_target="tpu_custom_call" | custom-call | bytes 4194304 | tf_op jit(solution)/shard_map/pallas_call | solution.py:178
  47.6 8.7 %all-to-all-start.1 = ((bf16[12,4,8,8,128]{4,3,2,1,0:T(8,128)(2,1)}), bf16[12,4,8,8,128]{4,3,2,1,0:T(8,128)(2,1)S(1)}, u32[]{:S(2)}, u32[]{:S(2)}) async-start(bf16[12,4,8,8,128]{4,3,2,1,0:T(8,128)(2,1)} %shard_map.60), calls=%async_computation.1 | async-start | bytes 1572864 | tf_op jit(solution)/shard_map/named_pieces/all_to_all | solution.py:235
  56.5 3.0 %collective-permute-done.refs_2_.refs_6_ = bf16[256,768]{1,0:T(8,128)(2,1)S(1)} collective-permute-done((bf16[256,768]{1,0:T(8,128)(2,1)S(1)}, bf16[256,768]{1,0:T(8,128)(2,1)S(1)}, u32[]{:S(2)}, u32[]{:S(2)}) %collective-permute-start) | collective-permute-done | bytes 393248 | tf_op jit(solution)/shard_map/pool_x/ppermute | solution.py:220
  62.3 8.1 %all-to-all-done.1 = bf16[12,4,8,8,128]{4,3,2,1,0:T(8,128)(2,1)S(1)} async-done(((bf16[12,4,8,8,128]{4,3,2,1,0:T(8,128)(2,1)}), bf16[12,4,8,8,128]{4,3,2,1,0:T(8,128)(2,1)S(1)}, u32[]{:S(2)}, u32[]{:S(2)}) %all-to-all-start.1) | async-done | bytes 786464 | tf_op jit(solution)/shard_map/named_pieces/all_to_all | solution.py:235
  70.3 1.1 copy-done.5
  71.5 1.4 %shard_map.61 = (bf16[192,512]{1,0:T(8,128)(2,1)S(1)}, bf16[192,512]{1,0:T(8,128)(2,1)S(1)}, f32[48,64,128]{2,1,0:T(8,128)S(1)}, f32[192,128]{1,0:T(8,128)S(1)}) custom-call(bf16[48,64,128]{2,1,0:T(8,128)(2,1)S(1)} %bitcast.20, f32[192,1024]{1,0:T(8,128)S(1)} %copy-done.5), custom_call_target="tpu_custom_call" | custom-call | flops 452984832 | bytes 4194304 | tf_op jit(solution)/shard_map/pallas_call | solution.py:178
  72.9 1.1 convert_element_type.94
  74.0 5.4 %all-to-all-start.2 = ((f16[12,4,8,8,128]{4,3,2,1,0:T(8,128)(2,1)}), f16[12,4,8,8,128]{4,3,2,1,0:T(8,128)(2,1)}, u32[]{:S(2)}, u32[]{:S(2)}) async-start(f16[12,4,8,8,128]{4,3,2,1,0:T(8,128)(2,1)} %bitcast.9), calls=%async_computation.2 | async-start | bytes 1572864 | tf_op jit(solution)/shard_map/named_back/all_to_all | solution.py:262
  79.5 1.1 copy-done.11
  80.6 1.8 %shard_map.62 = (bf16[192,1024]{1,0:T(8,128)(2,1)S(1)}, bf16[192,1024]{1,0:T(8,128)(2,1)S(1)}, f32[256,768]{1,0:T(8,128)S(1)}, f32[256,768]{1,0:T(8,128)S(1)}, f...) custom-call(s32[4]{0:T(128)S(1)} %iota_xor_fusion.refs_0_, bf16[192,768]{1,0:T(8,128)(2,1)S(1)} %copy-done.3, ...), custom_call_target="tpu_custom_call" | custom-call | flops 603979776 | bytes 4194304 | tf_op jit(solution)/shard_map/pallas_call | solution.py:178
  82.5 0.9 convert_element_type.84
  84.2 4.4 %collective-permute-start.5 = (f16[256,768]{1,0:T(8,128)(2,1)}, f16[256,768]{1,0:T(8,128)(2,1)}, u32[]{:S(2)}, u32[]{:S(2)}) collective-permute-start(f16[256,768]{1,0:T(8,128)(2,1)} %convert_element_type.86), channel_id=1, source_target_pairs={{0,12},{4,8},{8,4},{12,0},{1,13},{5,9},{9,5},{13,1},{2,14},{6,10},... | collective-permute-start | bytes 1179656 | tf_op jit(solution)/shard_map/grad_x/ppermute | solution.py:280
  88.6 2.4 %collective-permute-start.4 = (f16[256,768]{1,0:T(8,128)(2,1)}, f16[256,768]{1,0:T(8,128)(2,1)}, u32[]{:S(2)}, u32[]{:S(2)}) collective-permute-start(f16[256,768]{1,0:T(8,128)(2,1)} %convert_element_type.84), channel_id=1, source_target_pairs={{0,8},{4,12},{8,0},{12,4},{1,9},{5,13},{9,1},{13,5},{2,10},{6,14},... | collective-permute-start | bytes 1179656 | tf_op jit(solution)/shard_map/grad_x/ppermute | solution.py:280
  91.0 2.2 %collective-permute-start.3 = (f16[256,768]{1,0:T(8,128)(2,1)S(1)}, f16[256,768]{1,0:T(8,128)(2,1)}, u32[]{:S(2)}, u32[]{:S(2)}) collective-permute-start(f16[256,768]{1,0:T(8,128)(2,1)S(1)} %convert_element_type.82), channel_id=1, source_target_pairs={{0,4},{4,0},{8,12},{12,8},{1,5},{5,1},{9,13},{13,9},{2,6},{6,2},{1... | collective-permute-start | bytes 1179656 | tf_op jit(solution)/shard_map/grad_x/ppermute | solution.py:280
  93.6 1.3 convert_element_type.95.refs_2_
  94.9 1.1 shard_map.64
  96.9 13.2 %all-to-all-start.3 = ((f16[48,4,8,128]{3,2,1,0:T(8,128)(2,1)}), f16[48,4,8,128]{3,2,1,0:T(8,128)(2,1)}, u32[]{:S(2)}, u32[]{:S(2)}) async-start(f16[48,4,8,128]{3,2,1,0:T(8,128)(2,1)} %convert_element_type.96), calls=%async_computation.3 | async-start | bytes 786432 | tf_op jit(solution)/shard_map/pieces_home/all_to_all | solution.py:314
  110.1 1.5 %convert_add_fusion.refs_9_ = f32[256,768]{1,0:T(8,128)S(1)} fusion(f16[256,768]{1,0:T(8,128)(2,1)} %collective-permute-done.5, f16[256,768]{1,0:T(8,128)(2,1)} %collective-permute-done.4, f32[256,768]{1,0:T(8,128)S(1)} %get-tuple-element.21, f16[256,768]{1,0:T(8,128)(2,1)} %collective-permute-done.3), kind=kLoop, calls=%fused_computation | loop fusion | flops 1179648 | bytes 2752512 | tf_op jit(solution)/shard_map/grad_x/add | solution.py:281
  111.7 4.9 %collective-permute-start.6 = (f16[64,768]{1,0:T(8,128)(2,1)S(1)}, f16[64,768]{1,0:T(8,128)(2,1)S(1)}, u32[]{:S(2)}, u32[]{:S(2)}) collective-permute-start(f16[64,768]{1,0:T(8,128)(2,1)S(1)} %get-tuple-element.26), channel_id=1, source_target_pairs={{0,2},{1,3},{2,0},{3,1},{4,6},{5,7},{6,4},{7,5},{8,10},{9,11},{10,... | collective-permute-start | bytes 294920 | tf_op jit(solution)/shard_map/grad_yh/ppermute | solution.py:286
  116.7 3.7 %collective-permute-start.8 = (f16[64,768]{1,0:T(8,128)(2,1)S(1)}, f16[64,768]{1,0:T(8,128)(2,1)S(1)}, u32[]{:S(2)}, u32[]{:S(2)}) collective-permute-start(f16[64,768]{1,0:T(8,128)(2,1)S(1)} %get-tuple-element.27), channel_id=1, source_target_pairs={{0,3},{1,2},{2,1},{3,0},{4,7},{5,6},{6,5},{7,4},{8,11},{9,10},{10,... | collective-permute-start | bytes 294920 | tf_op jit(solution)/shard_map/grad_yh/ppermute | solution.py:286
  120.4 2.7 %collective-permute-start.7 = (f16[64,768]{1,0:T(8,128)(2,1)S(1)}, f16[64,768]{1,0:T(8,128)(2,1)S(1)}, u32[]{:S(2)}, u32[]{:S(2)}) collective-permute-start(f16[64,768]{1,0:T(8,128)(2,1)S(1)} %get-tuple-element.28), channel_id=1, source_target_pairs={{0,1},{1,0},{2,3},{3,2},{4,5},{5,4},{6,7},{7,6},{8,9},{9,8},{10,11... | collective-permute-start | bytes 294920 | tf_op jit(solution)/shard_map/grad_yh/ppermute | solution.py:286
  123.2 2.0 %shard_map.63 = f32[192,768]{1,0:T(8,128)} custom-call(bf16[192,1024]{1,0:T(8,128)(2,1)S(1)} %copy-done.13, bf16[192,1024]{1,0:T(8,128)(2,1)S(1)} %copy-done.15, bf16[192,512]{1,0:T(8,128)(2,1)S(1)} %copy-done.7, bf16[192,512]{1,0:T(8,128)(2,1)S(1)} %copy-done.9, bf16[48,64,128]{2,1,0:T(8,128)(2,1)S(1)} %bitcast.21, ...), custom_call_target="tpu_custom_call" | custom-call | flops 3623878656 | bytes 4194304 | tf_op jit(solution)/shard_map/pallas_call | solution.py:178
  125.2 3.0 %collective-permute-done.8 = f16[64,768]{1,0:T(8,128)(2,1)S(1)} collective-permute-done((f16[64,768]{1,0:T(8,128)(2,1)S(1)}, f16[64,768]{1,0:T(8,128)(2,1)S(1)}, u32[]{:S(2)}, u32[]{:S(2)}) %collective-permute-start.8) | collective-permute-done | bytes 98336 | tf_op jit(solution)/shard_map/grad_yh/ppermute | solution.py:286
  128.2 1.1 collective-permute-done.7
  129.3 1.9 %all-to-all-done.3 = f16[48,4,8,128]{3,2,1,0:T(8,128)(2,1)} async-done(((f16[48,4,8,128]{3,2,1,0:T(8,128)(2,1)}), f16[48,4,8,128]{3,2,1,0:T(8,128)(2,1)}, u32[]{:S(2)}, u32[]{:S(2)}) %all-to-all-start.3) | async-done | bytes 393248 | tf_op jit(solution)/shard_map/pieces_home/all_to_all | solution.py:314
  131.3 1.8 %fusion.6 = f32[64,768]{1,0:T(8,128)} fusion(f32[256,768]{1,0:T(8,128)S(1)} %convert_add_fusion.refs_9_, f16[64,768]{1,0:T(8,128)(2,1)S(1)} %collective-permute-done.8, f16[64,768]{1,0:T(8,128)(2,1)S(1)} %collective-permute-done.7, f16[64,768]{1,0:T(8,128)(2,1)S(1)} %collective-permute-done.6, f16[4,8,8,6,128]{4,2,3,1,0:T(8,128)(2,1)} %bitcast.11), kind=kLoop, calls=%fused_computation.12 | loop fusion | flops 933888 | bytes 1081344 | tf_op jit(solution)/shard_map/add | solution.py:320
  (55 shorter events, 6.9 us)
Async XLA Ops:
  0.6 20.5 %copy-start.16 = (bf16[64,768]{1,0:T(8,128)(2,1)S(1)}, bf16[64,768]{1,0:T(8,128)(2,1)}, u32[]{:S(2)}) copy-start(bf16[64,768]{1,0:T(8,128)(2,1)} %param.5) | copy-start | bytes 294916
  3.1 42.6 %all-to-all-start = ((bf16[48,40,128]{2,1,0:T(8,128)(2,1)}), bf16[48,40,128]{2,1,0:T(8,128)(2,1)S(1)}, u32[]{:S(2)}, u32[]{:S(2)}) async-start(bf16[48,40,128]{2,1,0:T(8,128)(2,1)} %bitcast_select_fusion), calls=%async_computation | async-start | bytes 983040 | tf_op jit(solution)/shard_map/spread_pieces/all_to_all | solution.py:214
  36.7 19.8 %collective-permute-start.2 = (bf16[256,768]{1,0:T(8,128)(2,1)S(1)}, bf16[256,768]{1,0:T(8,128)(2,1)S(1)}, u32[]{:S(2)}, u32[]{:S(2)}) collective-permute-start(bf16[256,768]{1,0:T(8,128)(2,1)S(1)} %all_gather.3.refs_1_.refs_3_.refs_5_), channel_id=1, source_target_pairs={{0,12},{4,8},{8,4},{12,0},{1,13},{5,9},{9,5},{13,1},{2,14},{6,10},... | collective-permute-start | bytes 1179656 | tf_op jit(solution)/shard_map/pool_x/ppermute | solution.py:220
  41.1 15.4 %collective-permute-start.1 = (bf16[256,768]{1,0:T(8,128)(2,1)S(1)}, bf16[256,768]{1,0:T(8,128)(2,1)S(1)}, u32[]{:S(2)}, u32[]{:S(2)}) collective-permute-start(bf16[256,768]{1,0:T(8,128)(2,1)S(1)} %all_gather.3.refs_1_.refs_3_.refs_5_), channel_id=1, source_target_pairs={{0,8},{4,12},{8,0},{12,4},{1,9},{5,13},{9,1},{13,5},{2,10},{6,14},... | collective-permute-start | bytes 1179656 | tf_op jit(solution)/shard_map/pool_x/ppermute | solution.py:220
  43.5 16.0 %collective-permute-start = (bf16[256,768]{1,0:T(8,128)(2,1)S(1)}, bf16[256,768]{1,0:T(8,128)(2,1)S(1)}, u32[]{:S(2)}, u32[]{:S(2)}) collective-permute-start(bf16[256,768]{1,0:T(8,128)(2,1)S(1)} %all_gather.3.refs_1_.refs_3_.refs_5_), channel_id=1, source_target_pairs={{0,4},{4,0},{8,12},{12,8},{1,5},{5,1},{9,13},{13,9},{2,6},{6,2},{1... | collective-permute-start | bytes 1179656 | tf_op jit(solution)/shard_map/pool_x/ppermute | solution.py:220
  45.9 13.7 %copy-start.2 = (bf16[192,768]{1,0:T(8,128)(2,1)S(1)}, bf16[192,768]{1,0:T(8,128)(2,1)}, u32[]{:S(2)}) copy-start(bf16[192,768]{1,0:T(8,128)(2,1)} %refs_1_.1) | copy-start | bytes 884740
  47.6 22.8 %all-to-all-start.1 = ((bf16[12,4,8,8,128]{4,3,2,1,0:T(8,128)(2,1)}), bf16[12,4,8,8,128]{4,3,2,1,0:T(8,128)(2,1)S(1)}, u32[]{:S(2)}, u32[]{:S(2)}) async-start(bf16[12,4,8,8,128]{4,3,2,1,0:T(8,128)(2,1)} %shard_map.60), calls=%async_computation.1 | async-start | bytes 1572864 | tf_op jit(solution)/shard_map/named_pieces/all_to_all | solution.py:235
  59.6 0.9 copy-start
  60.5 0.9 copy-start.4
  61.4 0.9 copy-start.10
  70.3 1.1 copy-start.5
  72.9 1.1 copy-start.8
  72.9 1.1 copy-start.6
  72.9 6.5 %copy-start.17 = (s32[192]{0:T(256)S(1)}, s32[192]{0:T(256)}, u32[]{:S(2)}) copy-start(s32[192]{0:T(256)} %param.6) | copy-start | bytes 2308
  72.9 6.6 %copy-start.3 = (bf16[192,768]{1,0:T(8,128)(2,1)S(1)}, bf16[192,768]{1,0:T(8,128)(2,1)}, u32[]{:S(2)}) copy-start(bf16[192,768]{1,0:T(8,128)(2,1)} %refs_1_.1) | copy-start | bytes 884740
  74.0 19.6 %all-to-all-start.2 = ((f16[12,4,8,8,128]{4,3,2,1,0:T(8,128)(2,1)}), f16[12,4,8,8,128]{4,3,2,1,0:T(8,128)(2,1)}, u32[]{:S(2)}, u32[]{:S(2)}) async-start(f16[12,4,8,8,128]{4,3,2,1,0:T(8,128)(2,1)} %bitcast.9), calls=%async_computation.2 | async-start | bytes 1572864 | tf_op jit(solution)/shard_map/named_back/all_to_all | solution.py:262
  79.5 1.1 copy-start.11
  82.4 1.8 %copy-start.12 = (bf16[192,1024]{1,0:T(8,128)(2,1)}, bf16[192,1024]{1,0:T(8,128)(2,1)S(1)}, u32[]{:S(2)}) copy-start(bf16[192,1024]{1,0:T(8,128)(2,1)S(1)} %get-tuple-element.17.refs_0_) | copy-start | bytes 1179652
  82.4 1.8 %copy-start.14 = (bf16[192,1024]{1,0:T(8,128)(2,1)}, bf16[192,1024]{1,0:T(8,128)(2,1)S(1)}, u32[]{:S(2)}) copy-start(bf16[192,1024]{1,0:T(8,128)(2,1)S(1)} %get-tuple-element.18.refs_1_) | copy-start | bytes 1179652
  84.2 25.9 %collective-permute-start.5 = (f16[256,768]{1,0:T(8,128)(2,1)}, f16[256,768]{1,0:T(8,128)(2,1)}, u32[]{:S(2)}, u32[]{:S(2)}) collective-permute-start(f16[256,768]{1,0:T(8,128)(2,1)} %convert_element_type.86), channel_id=1, source_target_pairs={{0,12},{4,8},{8,4},{12,0},{1,13},{5,9},{9,5},{13,1},{2,14},{6,10},... | collective-permute-start | bytes 1179656 | tf_op jit(solution)/shard_map/grad_x/ppermute | solution.py:280
  88.6 21.5 %collective-permute-start.4 = (f16[256,768]{1,0:T(8,128)(2,1)}, f16[256,768]{1,0:T(8,128)(2,1)}, u32[]{:S(2)}, u32[]{:S(2)}) collective-permute-start(f16[256,768]{1,0:T(8,128)(2,1)} %convert_element_type.84), channel_id=1, source_target_pairs={{0,8},{4,12},{8,0},{12,4},{1,9},{5,13},{9,1},{13,5},{2,10},{6,14},... | collective-permute-start | bytes 1179656 | tf_op jit(solution)/shard_map/grad_x/ppermute | solution.py:280
  91.0 19.1 %collective-permute-start.3 = (f16[256,768]{1,0:T(8,128)(2,1)S(1)}, f16[256,768]{1,0:T(8,128)(2,1)}, u32[]{:S(2)}, u32[]{:S(2)}) collective-permute-start(f16[256,768]{1,0:T(8,128)(2,1)S(1)} %convert_element_type.82), channel_id=1, source_target_pairs={{0,4},{4,0},{8,12},{12,8},{1,5},{5,1},{9,13},{13,9},{2,6},{6,2},{1... | collective-permute-start | bytes 1179656 | tf_op jit(solution)/shard_map/grad_x/ppermute | solution.py:280
  96.9 34.4 %all-to-all-start.3 = ((f16[48,4,8,128]{3,2,1,0:T(8,128)(2,1)}), f16[48,4,8,128]{3,2,1,0:T(8,128)(2,1)}, u32[]{:S(2)}, u32[]{:S(2)}) async-start(f16[48,4,8,128]{3,2,1,0:T(8,128)(2,1)} %convert_element_type.96), calls=%async_computation.3 | async-start | bytes 786432 | tf_op jit(solution)/shard_map/pieces_home/all_to_all | solution.py:314
  110.1 13.0 %copy-start.1 = (bf16[256,768]{1,0:T(8,128)(2,1)S(1)}, bf16[256,768]{1,0:T(8,128)(2,1)}, u32[]{:S(2)}) copy-start(bf16[256,768]{1,0:T(8,128)(2,1)} %copy-done) | copy-start | bytes 1179652
  110.1 13.0 %copy-start.7 = (bf16[192,512]{1,0:T(8,128)(2,1)S(1)}, bf16[192,512]{1,0:T(8,128)(2,1)}, u32[]{:S(2)}) copy-start(bf16[192,512]{1,0:T(8,128)(2,1)} %copy-done.6) | copy-start | bytes 589828
  110.1 13.0 %copy-start.9 = (bf16[192,512]{1,0:T(8,128)(2,1)S(1)}, bf16[192,512]{1,0:T(8,128)(2,1)}, u32[]{:S(2)}) copy-start(bf16[192,512]{1,0:T(8,128)(2,1)} %copy-done.8) | copy-start | bytes 589828
  110.1 13.0 %copy-start.13 = (bf16[192,1024]{1,0:T(8,128)(2,1)S(1)}, bf16[192,1024]{1,0:T(8,128)(2,1)}, u32[]{:S(2)}) copy-start(bf16[192,1024]{1,0:T(8,128)(2,1)} %copy-done.12) | copy-start | bytes 1179652
  110.1 13.0 %copy-start.15 = (bf16[192,1024]{1,0:T(8,128)(2,1)S(1)}, bf16[192,1024]{1,0:T(8,128)(2,1)}, u32[]{:S(2)}) copy-start(bf16[192,1024]{1,0:T(8,128)(2,1)} %copy-done.14) | copy-start | bytes 1179652
  111.7 13.4 %collective-permute-start.6 = (f16[64,768]{1,0:T(8,128)(2,1)S(1)}, f16[64,768]{1,0:T(8,128)(2,1)S(1)}, u32[]{:S(2)}, u32[]{:S(2)}) collective-permute-start(f16[64,768]{1,0:T(8,128)(2,1)S(1)} %get-tuple-element.26), channel_id=1, source_target_pairs={{0,2},{1,3},{2,0},{3,1},{4,6},{5,7},{6,4},{7,5},{8,10},{9,11},{10,... | collective-permute-start | bytes 294920 | tf_op jit(solution)/shard_map/grad_yh/ppermute | solution.py:286
  116.7 11.5 %collective-permute-start.8 = (f16[64,768]{1,0:T(8,128)(2,1)S(1)}, f16[64,768]{1,0:T(8,128)(2,1)S(1)}, u32[]{:S(2)}, u32[]{:S(2)}) collective-permute-start(f16[64,768]{1,0:T(8,128)(2,1)S(1)} %get-tuple-element.27), channel_id=1, source_target_pairs={{0,3},{1,2},{2,1},{3,0},{4,7},{5,6},{6,5},{7,4},{8,11},{9,10},{10,... | collective-permute-start | bytes 294920 | tf_op jit(solution)/shard_map/grad_yh/ppermute | solution.py:286
  120.4 9.0 %collective-permute-start.7 = (f16[64,768]{1,0:T(8,128)(2,1)S(1)}, f16[64,768]{1,0:T(8,128)(2,1)S(1)}, u32[]{:S(2)}, u32[]{:S(2)}) collective-permute-start(f16[64,768]{1,0:T(8,128)(2,1)S(1)} %get-tuple-element.28), channel_id=1, source_target_pairs={{0,1},{1,0},{2,3},{3,2},{4,5},{5,4},{6,7},{7,6},{8,9},{9,8},{10,11... | collective-permute-start | bytes 294920 | tf_op jit(solution)/shard_map/grad_yh/ppermute | solution.py:286
